TPU v7x, 128 devices: a whole 4x4x4 slice. The times are simulated.
128 devices in a mesh: ctx: 32 (over x, y, core), tp: 4 (over z).
Axes of the slice: x: 4, y: 4, z: 4, core: 2. Of those that a mesh axis runs over, the one named last changes fastest.
Arguments:
- queries: bfloat16 [32768, 8192], P(('ctx', 'tp')), may hold values from -36 to 36
- key_rows: bfloat16 [32768, 1024], P(('ctx', 'tp')), may hold values from -6 to 6
- value_rows: bfloat16 [32768, 1024], P(('ctx', 'tp')), may hold values from -6 to 6
- vertical_keys: int32 [8, 1024], P('tp'), may hold values from 0 to 32767, as said below
- slash_offsets: int32 [8, 3], P('tp'), may hold values from 0 to 32704, as said below
Outputs:
- attended: bfloat16 [32768, 8192], P('ctx', 'tp')
Inputs may be any that keep to these rules, and one draw needn't show every extreme that they name: `vertical_keys`: each row holds 1024 distinct positions in ascending order; no more than 96 of a row lie in one aligned range of 1024 positions, and in every row some such range holds exactly 96. `slash_offsets`: each row holds 3 distinct multiples of 64, the first of them 0.
All inputs are finite; a program needn't handle non-finite values.
Results may differ from a plain program's by a relative error of at most 0.0035.
Values may be sent and summed in bfloat16 or wider, within the bound.
No kernel may reach another device: no remote copies, remote signals or barrier semaphores. Data moves between devices by JAX's collectives and lax.ppermute only.
A program may use at most 320 MiB of HBM per device.

v0:
```python
import jax
import jax.numpy as jnp
from jax import lax
from jax.sharding import PartitionSpec as P

HQ = 64
KVH = 8
DH = 128
NVERT = 1024


def shifted_2(block, axis, distance):
    devices = range(lax.axis_size(axis))
    route = [(i - distance, i) for i in devices if i - distance in devices]
    return lax.ppermute(block, axis, route)


def split_tiles(padded, tok_count, block_count):
    lower_half = padded[:, :, :tok_count]
    upper_half = padded[:, :, 128:]
    lower_half = lower_half.reshape(padded.shape[:2] + (block_count, 128) + padded.shape[3:])
    upper_half = upper_half.reshape(padded.shape[:2] + (block_count, 128) + padded.shape[3:])[
        :, :, :, :64
    ]
    return jnp.concatenate((lower_half, upper_half), axis=3)


def shards(queries, key_rows, value_rows, vertical_keys, slash_offsets):
    local_q, local_k, local_v = (
        lax.all_to_all(queries, "tp", split_axis=1, concat_axis=0, tiled=True),
        lax.all_to_all(key_rows, "tp", split_axis=1, concat_axis=0, tiled=True),
        lax.all_to_all(value_rows, "tp", split_axis=1, concat_axis=0, tiled=True),
    )
    tok_count = local_q.shape[0]
    head_count = vertical_keys.shape[0]
    band_count = slash_offsets.shape[1]
    vert_count = vertical_keys.shape[1]
    group_size = HQ // KVH
    block_count = tok_count // 128
    ctx_count = lax.axis_size("ctx")
    tokens_all = tok_count * ctx_count
    offset_base = lax.axis_index("ctx") * tok_count
    window_len = tok_count + 64
    scale_factor = DH ** (-0.5)
    kv_heads = jnp.concatenate(
        (local_k.reshape(tok_count, head_count, DH), local_v.reshape(tok_count, head_count, DH)),
        axis=2,
    ).transpose(1, 0, 2)
    earlier = shifted_2(kv_heads, "ctx", 1)
    joined = jnp.concatenate((earlier, kv_heads), axis=1)
    remains = slash_offsets % tok_count
    hop_counts = slash_offsets // tok_count
    window_first = tok_count - remains - 64
    head_windows = []
    for head in range(head_count):
        band_windows = []
        for band in range(band_count):
            band_windows.append(
                lax.dynamic_slice_in_dim(joined[head], window_first[head, band], window_len, 0)
            )
        head_windows.append(jnp.stack(band_windows, axis=0))
    windows = jnp.stack(head_windows, axis=0)
    nearest = windows[:, :1]
    distant = windows[:, 1:]
    for bit_index in range(max((ctx_count - 1).bit_length(), 1)):
        shifted = shifted_2(distant, "ctx", 1 << bit_index)
        selected = jnp.bitwise_and(jnp.right_shift(hop_counts[:, 1:], bit_index), 1) == 1
        distant = jnp.where(selected[:, :, None, None], shifted, distant)
    windows = jnp.concatenate((nearest, distant), axis=1)
    padded = jnp.concatenate(
        (windows, jnp.zeros((head_count, band_count, 64, 2 * DH), jnp.bfloat16)), axis=2
    )
    tiles = split_tiles(padded, tok_count, block_count)
    head_ids = jnp.arange(head_count, dtype=jnp.int32)[:, None]
    marked = jnp.zeros((head_count, tokens_all), jnp.int32).at[head_ids, vertical_keys].set(1)
    marked_pad = jnp.concatenate(
        (jnp.zeros_like(marked), marked, jnp.zeros((head_count, 128), jnp.int32)), axis=1
    )
    mark_starts = offset_base - slash_offsets - 64 + tokens_all
    member_heads = []
    for head in range(head_count):
        member_bands = []
        for band in range(band_count):
            member_bands.append(
                lax.dynamic_slice_in_dim(
                    marked_pad[head], mark_starts[head, band], tok_count + 128, 0
                )
            )
        member_heads.append(jnp.stack(member_bands, axis=0))
    member_w = jnp.stack(member_heads, axis=0)
    window_pos = (
        offset_base
        - slash_offsets[:, :, None]
        - 64
        + jnp.arange(tok_count + 128, dtype=jnp.int32)[None, None, :]
    )
    usable = ((window_pos >= 0) & (member_w == 0)).astype(jnp.int32)
    usable_tiles = split_tiles(usable, tok_count, block_count) == 1
    distance = jnp.arange(192, dtype=jnp.int32)[None, :] - jnp.arange(128, dtype=jnp.int32)[:, None]
    in_band = (distance >= 1) & (distance <= 64)
    cap_rows = 3 * NVERT // ctx_count
    first_own = jnp.sum(vertical_keys < offset_base, axis=1)
    own_count = jnp.sum(vertical_keys < offset_base + tok_count, axis=1) - first_own
    extended = jnp.concatenate(
        (vertical_keys, jnp.zeros((head_count, cap_rows), jnp.int32) + offset_base), axis=1
    )
    own_keys = jax.vmap(
        lambda line, first_row: lax.dynamic_slice_in_dim(line, first_row, cap_rows, 0)
    )(extended, first_own)
    live = jnp.arange(cap_rows, dtype=jnp.int32)[None, :] < own_count[:, None]
    own_rows = jax.vmap(
        lambda table, where_at: table[jnp.clip(where_at - offset_base, 0, tok_count - 1)]
    )(kv_heads, own_keys)
    own_rows = jnp.where(live[..., None], own_rows, jnp.zeros_like(own_rows))
    gathered = lax.all_gather(own_rows, "ctx", axis=1, tiled=True)
    owners = vertical_keys // tok_count
    owner_first = jnp.sum(
        vertical_keys[:, None, :]
        < (jnp.arange(ctx_count, dtype=jnp.int32) * tok_count)[None, :, None],
        axis=2,
    )
    slots = (
        owners * cap_rows
        + jnp.arange(vert_count, dtype=jnp.int32)[None, :]
        - jnp.take_along_axis(owner_first, owners, axis=1)
    )
    vert_rows = jax.vmap(lambda table, where_at: table[where_at])(gathered, slots)
    positions = offset_base + jnp.arange(tok_count, dtype=jnp.int32)
    query_heads = local_q.reshape(tok_count, head_count, group_size, DH)
    results = []
    for head in range(head_count):
        query_one = query_heads[:, head]
        vert_k = vert_rows[head, :, :DH]
        vert_v = vert_rows[head, :, DH:]
        vert_scores = (
            jnp.einsum("sgd,nd->gsn", query_one, vert_k, preferred_element_type=jnp.float32)
            * scale_factor
        )
        vert_mask = vertical_keys[head][None, None, :] <= positions[None, :, None]
        vert_scores = jnp.where(vert_mask, vert_scores, -jnp.inf)
        query_blocks = query_one.reshape(block_count, 128, group_size, DH)
        tile_k = tiles[head, :, :, :, :DH]
        tile_v = tiles[head, :, :, :, DH:]
        band_scores = (
            jnp.einsum("bqgd,kbtd->gbqkt", query_blocks, tile_k, preferred_element_type=jnp.float32)
            * scale_factor
        )
        band_mask = (
            in_band[None, None, :, None, :]
            & usable_tiles[head].transpose(1, 0, 2)[None, :, None, :, :]
        )
        band_scores = jnp.where(band_mask, band_scores, -jnp.inf)
        band_top = jnp.max(band_scores, axis=(-2, -1)).reshape(group_size, tok_count)
        top = jnp.maximum(jnp.max(vert_scores, axis=-1), band_top)
        vert_weight = jnp.exp(vert_scores - top[..., None])
        band_weight = jnp.exp(
            band_scores - top.reshape(group_size, block_count, 128)[..., None, None]
        )
        total = jnp.sum(vert_weight, axis=-1) + jnp.sum(band_weight, axis=(-2, -1)).reshape(
            group_size, tok_count
        )
        numer = jnp.einsum(
            "gsn,nd->gsd",
            vert_weight.astype(jnp.bfloat16),
            vert_v,
            preferred_element_type=jnp.float32,
        )
        band_numer = jnp.einsum(
            "gbqkt,kbtd->gbqd",
            band_weight.astype(jnp.bfloat16),
            tile_v,
            preferred_element_type=jnp.float32,
        )
        numer = numer + band_numer.reshape(group_size, tok_count, DH)
        results.append((numer / total[..., None]).transpose(1, 0, 2))
    stacked = jnp.stack(results, axis=1)
    return stacked.reshape(tok_count, head_count * group_size * DH).astype(jnp.bfloat16)


def solution(mesh):
    in_specs = (
        P(("ctx", "tp"), None),
        P(("ctx", "tp"), None),
        P(("ctx", "tp"), None),
        P("tp", None),
        P("tp", None),
    )
    out_specs = P("ctx", "tp")
    return jax.shard_map(shards, mesh=mesh, in_specs=in_specs, out_specs=out_specs, check_vma=False)
```

profile of v0, /device:TPU:12, one launch (start us, length us, event | category | flops | bytes accessed | tf_op | source)
XLA Modules:
  0.0 489.7 jit_solution(3583475559228568061)
XLA Ops:
  8.4 5.3 %all-to-all-start.1 = ((bf16[256,4,256]{2,0,1:T(8,128)(2,1)}), bf16[256,4,256]{2,0,1:T(8,128)(2,1)S(1)}, u32[]{:S(2)}, u32[]{:S(2)}) async-start(bf16[256,4,256]{2,0,1:T(8,128)(2,1)} %bitcast.248), calls=%async_computation.1 | async-start | bytes 1048576 | tf_op jit(solution)/shard_map/all_to_all | solution.py:32
  15.6 7.6 %all-to-all-done.1 = bf16[256,4,256]{2,0,1:T(8,128)(2,1)S(1)} async-done(((bf16[256,4,256]{2,0,1:T(8,128)(2,1)}), bf16[256,4,256]{2,0,1:T(8,128)(2,1)S(1)}, u32[]{:S(2)}, u32[]{:S(2)}) %all-to-all-start.1) | async-done | bytes 524320 | tf_op jit(solution)/shard_map/all_to_all | solution.py:32
  23.2 3.5 all-to-all-start
  26.9 8.0 %all-to-all-done = bf16[256,4,256]{2,0,1:T(8,128)(2,1)S(1)} async-done(((bf16[256,4,256]{2,0,1:T(8,128)(2,1)}), bf16[256,4,256]{2,0,1:T(8,128)(2,1)S(1)}, u32[]{:S(2)}, u32[]{:S(2)}) %all-to-all-start) | async-done | bytes 524320 | tf_op jit(solution)/shard_map/all_to_all | solution.py:31
  35.2 1.9 collective-permute-start
  49.0 2.4 collective-permute-done
  51.4 4.8 fusion.57
  59.7 2.0 collective-permute-start.1
  61.8 2.3 copy.135
  64.1 5.0 %all-to-all-start.2 = ((bf16[256,4,2048]{2,0,1:T(8,128)(2,1)}), bf16[256,4,2048]{2,0,1:T(8,128)(2,1)}, u32[]{:S(2)}, u32[]{:S(2)}) async-start(bf16[256,4,2048]{2,0,1:T(8,128)(2,1)} %bitcast.262), calls=%async_computation.2 | async-start | bytes 8388608 | tf_op jit(solution)/shard_map/all_to_all | solution.py:30
  69.6 8.8 %scatter_custom_fusion = s32[65536]{0:T(1024)} fusion(s32[2048]{0:T(1024)S(1)} %bitcast.282, s32[2048]{0:T(1024)S(1)} %broadcast.335, s32[]{:T(128)} %constant.59.clone.1), kind=kCustom, calls=%fused_computation.104 | custom fusion | bytes 262148
  80.4 8.6 %collective-permute-done.1 = bf16[2,2,1088,256]{3,2,1,0:T(8,128)(2,1)} collective-permute-done((bf16[2,2,1088,256]{3,2,1,0:T(8,128)(2,1)}, bf16[2,2,1088,256]{3,2,1,0:T(8,128)(2,1)}, u32[]{:S(2)}, u32[]{:S(2)}) %collective-permute-start.1) | collective-permute-done | bytes 2228256 | tf_op jit(solution)/shard_map/ppermute | solution.py:15
  88.9 3.5 broadcast_select_fusion
  92.4 3.6 collective-permute-start.2
  97.4 3.9 while.2
  101.5 4.7 gather_fusion
  106.9 38.8 %collective-permute-done.2 = bf16[2,2,1088,256]{3,2,1,0:T(8,128)(2,1)} collective-permute-done((bf16[2,2,1088,256]{3,2,1,0:T(8,128)(2,1)}, bf16[2,2,1088,256]{3,2,1,0:T(8,128)(2,1)}, u32[]{:S(2)}, u32[]{:S(2)}) %collective-permute-start.2) | collective-permute-done | bytes 2228256 | tf_op jit(solution)/shard_map/ppermute | solution.py:15
  145.7 4.1 broadcast_select_fusion.1
  149.8 5.6 %collective-permute-start.3 = (bf16[2,2,1088,256]{3,2,1,0:T(8,128)(2,1)}, bf16[2,2,1088,256]{3,2,1,0:T(8,128)(2,1)}, u32[]{:S(2)}, u32[]{:S(2)}) collective-permute-start(bf16[2,2,1088,256]{3,2,1,0:T(8,128)(2,1)} %broadcast_select_fusion.1), channel_id=1, source_target_pairs={{0,16},{4,20},{8,24},{12,28},{16,32},{20,36},{24,40},{28,44},{32,4... | collective-permute-start | bytes 6684680 | tf_op jit(solution)/shard_map/ppermute | solution.py:15
  164.4 17.5 %gather_fusion.1 = s32[2048]{0:T(1024)S(1)} fusion(s32[2,32]{1,0:T(2,128)S(1)} %convert_reduce_fusion, s32[2048]{0:T(1024)S(1)} %bitcast.261), kind=kCustom, calls=%fused_computation.1 | custom fusion | bytes 32768 | tf_op jit(solution)/shard_map/jit(take_along_axis)/gather | solution.py:125
  187.5 23.2 %collective-permute-done.3 = bf16[2,2,1088,256]{3,2,1,0:T(8,128)(2,1)} collective-permute-done((bf16[2,2,1088,256]{3,2,1,0:T(8,128)(2,1)}, bf16[2,2,1088,256]{3,2,1,0:T(8,128)(2,1)}, u32[]{:S(2)}, u32[]{:S(2)}) %collective-permute-start.3) | collective-permute-done | bytes 2228256 | tf_op jit(solution)/shard_map/ppermute | solution.py:15
  210.6 4.0 broadcast_select_fusion.2
  214.7 3.2 collective-permute-start.4
  218.1 3.3 broadcast_and_fusion.1
  221.4 2.3 broadcast_compare_fusion.1
  223.6 3.6 copy.91
  232.2 35.5 %gather_fusion.2 = bf16[2048,256]{1,0:T(8,128)(2,1)} fusion(bf16[2,3072,256]{2,1,0:T(8,128)(2,1)} %all-gather.2.cloned.1.call-done, s32[2048]{0:T(1024)S(1)} %bitcast.260), kind=kCustom, calls=%fused_computation.2 | custom fusion | bytes 2113536 | tf_op jit(solution)/shard_map/vmap()/gather | solution.py:127
  267.7 2.7 broadcast_select_fusion.3
  272.0 13.7 %fusion.5 = (f32[8,1024]{1,0:T(8,128)S(1)}, f32[1024,1024,8]{1,0,2:T(8,128)}) fusion(pred[1024,1024]{0,1:T(8,128)(4,1)S(1)} %copy-done.6, bf16[1024,1,8,128]{3,2,1,0:T(8,128)(2,1)S(1)} %copy-done.3, bf16[2,1024,256]{2,1,0:T(8,128)(2,1)S(1)} %bitcast.268), kind=kOutput, calls=%fused_computation.14 | convolution fusion | flops 2172641280 | bytes 36995072 | tf_op jit(solution)/shard_map/sgd,nd->gsn/dot_general | solution.py:136
  285.7 13.7 %fusion.4 = (f32[8,1024]{1,0:T(8,128)S(1)}, f32[1024,1024,8]{1,0,2:T(8,128)}) fusion(pred[1024,1024]{0,1:T(8,128)(4,1)S(1)} %copy-done.4, bf16[1024,1,8,128]{3,2,1,0:T(8,128)(2,1)S(1)} %copy-done.1, bf16[2,1024,256]{2,1,0:T(8,128)(2,1)S(1)} %bitcast.269), kind=kOutput, calls=%fused_computation.13 | convolution fusion | flops 2172641280 | bytes 36995072 | tf_op jit(solution)/shard_map/sgd,nd->gsn/dot_general | solution.py:136
  299.3 24.4 %collective-permute-done.5 = bf16[2,2,1088,256]{3,2,1,0:T(8,128)(2,1)} collective-permute-done((bf16[2,2,1088,256]{3,2,1,0:T(8,128)(2,1)S(1)}, bf16[2,2,1088,256]{3,2,1,0:T(8,128)(2,1)}, u32[]{:S(2)}, u32[]{:S(2)}) %collective-permute-start.5) | collective-permute-done | bytes 2228256 | tf_op jit(solution)/shard_map/ppermute | solution.py:15
  323.7 1.9 broadcast_select_fusion.4
  329.5 7.8 %fusion.17 = (f32[8,8,128]{2,0,1:T(8,128)S(1)}, f32[8,3,192,128,8]{3,2,4,1,0:T(8,128)}) fusion(pred[8,128,3,192]{1,3,2,0:T(8,128)(4,1)S(1)} %copy-done.15, bf16[8,128,8,128,1]{3,1,0,2,4:T(8,128)(2,1)S(1)} %bitcast.273, bf16[1,3,8,192,128]{4,3,2,1,0:T(8,128)(2,1)S(1)} %get-tuple-element.42), kind=kOutput, calls=%fused_computation.28 | convolution fusion | flops 1222107136 | bytes 22773760 | tf_op jit(solution)/shard_map/bqgd,kbtd->gbqkt/dot_general | solution.py:145
  337.3 8.2 %fusion.16 = (f32[8,8,128]{2,0,1:T(8,128)S(1)}, f32[8,3,192,128,8]{3,2,4,1,0:T(8,128)}) fusion(pred[8,128,3,192]{1,3,2,0:T(8,128)(4,1)S(1)} %copy-done.14, bf16[8,128,8,128,1]{3,1,0,2,4:T(8,128)(2,1)S(1)} %bitcast.272, bf16[1,3,8,192,128]{4,3,2,1,0:T(8,128)(2,1)S(1)} %get-tuple-element.40), kind=kOutput, calls=%fused_computation.27 | convolution fusion | flops 1222107136 | bytes 22773760 | tf_op jit(solution)/shard_map/bqgd,kbtd->gbqkt/dot_general | solution.py:145
  345.6 10.6 %fusion.14 = f32[8,8,128]{2,0,1:T(8,128)S(1)} fusion(f32[8,3,192,128,8]{3,2,4,1,0:T(8,128)} %get-tuple-element.96, f32[8,8,128]{2,0,1:T(8,128)S(1)} %bitcast_maximum_fusion, pred[8,128,3,192]{1,3,2,0:T(8,128)(4,1)S(1)} %copy-done.16), kind=kLoop, calls=%fused_computation.25 | loop fusion | flops 18866176 | bytes 19529728 | tf_op jit(solution)/shard_map/reduce_sum | solution.py:159
  356.2 10.3 %fusion.31 = f32[8,8,128,128]{3,2,0,1:T(8,128)} fusion(f32[8,3,192,128,8]{3,2,4,1,0:T(8,128)} %get-tuple-element.96, f32[8,8,128]{2,0,1:T(8,128)S(1)} %bitcast_maximum_fusion, pred[8,128,3,192]{1,3,2,0:T(8,128)(4,1)S(1)} %copy-done.16, bf16[1,3,8,192,128]{4,3,2,1,0:T(8,128)(2,1)S(1)} %copy-done.21), kind=kOutput, calls=%fused_computation.56 | convolution fusion | flops 1226833920 | bytes 24870912 | tf_op jit(solution)/shard_map/gbqkt,kbtd->gbqd/dot_general | solution.py:168
  366.4 5.3 %copy.58 = f32[8,8,128,128]{2,1,3,0:T(8,128)} copy(f32[8,8,128,128]{3,2,0,1:T(8,128)} %fusion.31) | data formatting | bytes 8388608 | tf_op jit(solution)/shard_map/gbqkt,kbtd->gbqd/transpose | solution.py:168
  371.8 5.3 %reshape.318 = f32[8,1024,128]{1,2,0:T(8,128)} reshape(f32[8,8,128,128]{2,1,3,0:T(8,128)} %copy.58) | data formatting | bytes 8388608 | tf_op jit(solution)/shard_map/reshape | solution.py:174
  377.1 10.6 %fusion.12 = f32[8,8,128]{2,0,1:T(8,128)S(1)} fusion(f32[8,3,192,128,8]{3,2,4,1,0:T(8,128)} %get-tuple-element.100, f32[8,8,128]{2,0,1:T(8,128)S(1)} %bitcast_maximum_fusion.2, pred[8,128,3,192]{1,3,2,0:T(8,128)(4,1)S(1)} %copy-done.14), kind=kLoop, calls=%fused_computation.23 | loop fusion | flops 18866176 | bytes 19529728 | tf_op jit(solution)/shard_map/reduce_sum | solution.py:159
  387.7 10.3 %fusion.28 = f32[8,8,128,128]{3,2,0,1:T(8,128)} fusion(f32[8,3,192,128,8]{3,2,4,1,0:T(8,128)} %get-tuple-element.100, f32[8,8,128]{2,0,1:T(8,128)S(1)} %bitcast_maximum_fusion.2, pred[8,128,3,192]{1,3,2,0:T(8,128)(4,1)S(1)} %copy-done.14, bf16[1,3,8,192,128]{4,3,2,1,0:T(8,128)(2,1)S(1)} %copy-done.20), kind=kOutput, calls=%fused_computation.55 | convolution fusion | flops 1226833920 | bytes 24870912 | tf_op jit(solution)/shard_map/gbqkt,kbtd->gbqd/dot_general | solution.py:168
  398.0 5.4 %copy.52 = f32[8,8,128,128]{2,1,3,0:T(8,128)} copy(f32[8,8,128,128]{3,2,0,1:T(8,128)} %fusion.28) | data formatting | bytes 8388608 | tf_op jit(solution)/shard_map/gbqkt,kbtd->gbqd/transpose | solution.py:168
  403.4 5.0 %reshape.315 = f32[8,1024,128]{1,2,0:T(8,128)} reshape(f32[8,8,128,128]{2,1,3,0:T(8,128)} %copy.52) | data formatting | bytes 8388608 | tf_op jit(solution)/shard_map/reshape | solution.py:174
  408.4 14.3 %fusion.2 = f32[8,1024]{1,0:T(8,128)S(1)} fusion(f32[1024,1024,8]{1,0,2:T(8,128)} %get-tuple-element.94, f32[8,1024]{1,0:T(8,128)S(1)} %bitcast_maximum_fusion.1, pred[1024,1024]{0,1:T(8,128)(4,1)S(1)} %copy-done.7), kind=kLoop, calls=%fused_computation.11 | loop fusion | flops 33546240 | bytes 34668544 | tf_op jit(solution)/shard_map/reduce_sum | solution.py:159
  422.7 17.6 %fusion.43 = bf16[1024,1,8,128]{0,3,2,1:T(8,128)(2,1)} fusion(f32[8,1024]{1,0:T(8,128)S(1)} %bitcast_add_fusion, f32[8,1024,128]{1,2,0:T(8,128)} %reshape.318, f32[1024,1024,8]{1,0,2:T(8,128)} %get-tuple-element.94, f32[8,1024]{1,0:T(8,128)S(1)} %bitcast_maximum_fusion.1, pred[1024,1024]{0,1:T(8,128)(4,1)S(1)} %copy-done.7, ...), kind=kOutput, calls=%fused_computation.70 | convolution fusion | flops 2184183808 | bytes 41222144 | tf_op jit(solution)/shard_map/gsn,nd->gsd/dot_general | solution.py:162
  440.3 14.2 %fusion = f32[8,1024]{1,0:T(8,128)S(1)} fusion(f32[1024,1024,8]{1,0,2:T(8,128)} %get-tuple-element.98, f32[8,1024]{1,0:T(8,128)S(1)} %bitcast_maximum_fusion.3, pred[1024,1024]{0,1:T(8,128)(4,1)S(1)} %copy-done.5), kind=kLoop, calls=%fused_computation.9 | loop fusion | flops 33546240 | bytes 34668544 | tf_op jit(solution)/shard_map/reduce_sum | solution.py:159
  454.5 17.2 %fusion.42 = bf16[1024,1,8,128]{0,3,2,1:T(8,128)(2,1)} fusion(f32[8,1024]{1,0:T(8,128)S(1)} %bitcast_add_fusion.1, f32[8,1024,128]{1,2,0:T(8,128)} %reshape.315, f32[1024,1024,8]{1,0,2:T(8,128)} %get-tuple-element.98, f32[8,1024]{1,0:T(8,128)S(1)} %bitcast_maximum_fusion.3, pred[1024,1024]{0,1:T(8,128)(4,1)S(1)} %copy-done.5, ...), kind=kOutput, calls=%fused_computation.69 | convolution fusion | flops 2184183808 | bytes 41222144 | tf_op jit(solution)/shard_map/gsn,nd->gsd/dot_general | solution.py:162
  471.7 4.5 pad_maximum_fusion
  476.2 6.4 %copy.59 = bf16[1024,2048]{1,0:T(8,128)(2,1)} copy(bf16[1024,2048]{0,1:T(8,128)(2,1)} %bitcast.264) | data formatting | bytes 8388608 | tf_op jit(solution)/shard_map/convert_element_type | solution.py:177
  (139 shorter events, 30.7 us)
Async XLA Ops:
  8.4 14.8 %all-to-all-start.1 = ((bf16[256,4,256]{2,0,1:T(8,128)(2,1)}), bf16[256,4,256]{2,0,1:T(8,128)(2,1)S(1)}, u32[]{:S(2)}, u32[]{:S(2)}) async-start(bf16[256,4,256]{2,0,1:T(8,128)(2,1)} %bitcast.248), calls=%async_computation.1 | async-start | bytes 1048576 | tf_op jit(solution)/shard_map/all_to_all | solution.py:32
  23.2 11.7 %all-to-all-start = ((bf16[256,4,256]{2,0,1:T(8,128)(2,1)}), bf16[256,4,256]{2,0,1:T(8,128)(2,1)S(1)}, u32[]{:S(2)}, u32[]{:S(2)}) async-start(bf16[256,4,256]{2,0,1:T(8,128)(2,1)} %bitcast.249), calls=%async_computation | async-start | bytes 1048576 | tf_op jit(solution)/shard_map/all_to_all | solution.py:31
  26.7 10.5 %copy-start.24 = (s32[2,3]{1,0:T(2,128)S(1)}, s32[2,3]{1,0:T(2,128)}, u32[]{:S(2)}) copy-start(s32[2,3]{1,0:T(2,128)} %param.9) | copy-start | bytes 76
  35.2 21.2 %copy-start.8 = (bf16[2,1024,256]{2,1,0:T(8,128)(2,1)}, bf16[2,1024,256]{2,1,0:T(8,128)(2,1)S(1)}, u32[]{:S(2)}) copy-start(bf16[2,1024,256]{2,1,0:T(8,128)(2,1)S(1)} %maximum_bitcast_fusion.2) | copy-start | bytes 3145732
  35.2 16.1 %collective-permute-start = (bf16[2,1024,256]{2,1,0:T(8,128)(2,1)S(1)}, bf16[2,1024,256]{2,1,0:T(8,128)(2,1)S(1)}, u32[]{:S(2)}, u32[]{:S(2)}) collective-permute-start(bf16[2,1024,256]{2,1,0:T(8,128)(2,1)S(1)} %maximum_bitcast_fusion.2), channel_id=1, source_target_pairs={{0,4},{4,8},{8,12},{12,16},{16,20},{20,24},{24,28},{28,32},{32,36}... | collective-permute-start | bytes 3145736 | tf_op jit(solution)/shard_map/ppermute | solution.py:15
  51.4 4.8 copy-start.9
  56.2 1.2 copy-start.10
  58.1 3.7 copy-start.11
  59.7 29.2 %collective-permute-start.1 = (bf16[2,2,1088,256]{3,2,1,0:T(8,128)(2,1)}, bf16[2,2,1088,256]{3,2,1,0:T(8,128)(2,1)}, u32[]{:S(2)}, u32[]{:S(2)}) collective-permute-start(bf16[2,2,1088,256]{3,2,1,0:T(8,128)(2,1)} %pad_maximum_fusion.1), channel_id=1, source_target_pairs={{0,4},{4,8},{8,12},{12,16},{16,20},{20,24},{24,28},{28,32},{32,36}... | collective-permute-start | bytes 6684680 | tf_op jit(solution)/shard_map/ppermute | solution.py:15
  64.1 5.1 %copy-start.23 = (s32[2,1024]{1,0:T(2,128)S(1)}, s32[2,1024]{1,0:T(2,128)}, u32[]{:S(2)}) copy-start(s32[2,1024]{1,0:T(2,128)} %param.8) | copy-start | bytes 24580
  64.1 5.2 %copy-start.25 = (s32[2]{0:T(128)S(1)}, s32[2]{0:T(128)}, u32[]{:S(2)}) copy-start(s32[2]{0:T(128)} %constant.136) | copy-start | bytes 28
  64.1 5.3 %copy-start.26 = (s32[2]{0:T(128)S(1)}, s32[2]{0:T(128)}, u32[]{:S(2)}) copy-start(s32[2]{0:T(128)} %constant.139) | copy-start | bytes 28
  64.1 159.5 %all-to-all-start.2 = ((bf16[256,4,2048]{2,0,1:T(8,128)(2,1)}), bf16[256,4,2048]{2,0,1:T(8,128)(2,1)}, u32[]{:S(2)}, u32[]{:S(2)}) async-start(bf16[256,4,2048]{2,0,1:T(8,128)(2,1)} %bitcast.262), calls=%async_computation.2 | async-start | bytes 8388608 | tf_op jit(solution)/shard_map/all_to_all | solution.py:30
  69.1 163.1 %all-gather.2.cloned.1.call-start = ((), (), s32[]{:S(2)}) async-start(), calls=%async_computation.3 | async-start | bytes 3244032 | tf_op jit(solution)/shard_map/all_gather | solution.py:115
  88.9 7.1 %copy-start.22 = (s32[2,32768]{1,0:T(2,128)S(1)}, s32[2,32768]{1,0:T(2,128)}, u32[]{:S(2)}) copy-start(s32[2,32768]{1,0:T(2,128)} %reshape.323) | copy-start | bytes 786436
  92.4 53.3 %collective-permute-start.2 = (bf16[2,2,1088,256]{3,2,1,0:T(8,128)(2,1)}, bf16[2,2,1088,256]{3,2,1,0:T(8,128)(2,1)}, u32[]{:S(2)}, u32[]{:S(2)}) collective-permute-start(bf16[2,2,1088,256]{3,2,1,0:T(8,128)(2,1)} %broadcast_select_fusion), channel_id=1, source_target_pairs={{0,8},{4,12},{8,16},{12,20},{16,24},{20,28},{24,32},{28,36},{32,40... | collective-permute-start | bytes 6684680 | tf_op jit(solution)/shard_map/ppermute | solution.py:15
  145.7 9.7 %copy-start.17 = (s32[2,65664]{1,0:T(2,128)S(1)}, s32[2,65664]{1,0:T(2,128)}, u32[]{:S(2)}) copy-start(s32[2,65664]{1,0:T(2,128)} %add_add_fusion) | copy-start | bytes 1575940
  149.8 60.8 %collective-permute-start.3 = (bf16[2,2,1088,256]{3,2,1,0:T(8,128)(2,1)}, bf16[2,2,1088,256]{3,2,1,0:T(8,128)(2,1)}, u32[]{:S(2)}, u32[]{:S(2)}) collective-permute-start(bf16[2,2,1088,256]{3,2,1,0:T(8,128)(2,1)} %broadcast_select_fusion.1), channel_id=1, source_target_pairs={{0,16},{4,20},{8,24},{12,28},{16,32},{20,36},{24,40},{28,44},{32,4... | collective-permute-start | bytes 6684680 | tf_op jit(solution)/shard_map/ppermute | solution.py:15
  214.7 53.0 %collective-permute-start.4 = (bf16[2,2,1088,256]{3,2,1,0:T(8,128)(2,1)}, bf16[2,2,1088,256]{3,2,1,0:T(8,128)(2,1)}, u32[]{:S(2)}, u32[]{:S(2)}) collective-permute-start(bf16[2,2,1088,256]{3,2,1,0:T(8,128)(2,1)} %broadcast_select_fusion.2), channel_id=1, source_target_pairs={{0,32},{4,36},{8,40},{12,44},{16,48},{20,52},{24,56},{28,60},{32,6... | collective-permute-start | bytes 6684680 | tf_op jit(solution)/shard_map/ppermute | solution.py:15
  227.5 1.3 copy-start.2
  227.5 3.0 copy-start
  267.7 4.3 copy-start.3
  267.7 4.3 copy-start.6
  267.7 4.3 copy-start.12
  270.4 53.3 %collective-permute-start.5 = (bf16[2,2,1088,256]{3,2,1,0:T(8,128)(2,1)S(1)}, bf16[2,2,1088,256]{3,2,1,0:T(8,128)(2,1)}, u32[]{:S(2)}, u32[]{:S(2)}) collective-permute-start(bf16[2,2,1088,256]{3,2,1,0:T(8,128)(2,1)S(1)} %broadcast_select_fusion.3), channel_id=1, source_target_pairs={{0,64},{4,68},{8,72},{12,76},{16,80},{20,84},{24,88},{28,92},{32,9... | collective-permute-start | bytes 6684680 | tf_op jit(solution)/shard_map/ppermute | solution.py:15
  272.0 13.7 %copy-start.1 = (bf16[1024,1,8,128]{3,2,1,0:T(8,128)(2,1)S(1)}, bf16[1024,1,8,128]{3,2,1,0:T(8,128)(2,1)}, u32[]{:S(2)}) copy-start(bf16[1024,1,8,128]{3,2,1,0:T(8,128)(2,1)} %copy-done) | copy-start | bytes 6291460
  272.0 13.7 %copy-start.4 = (pred[1024,1024]{0,1:T(8,128)(4,1)S(1)}, pred[1024,1024]{0,1:T(8,128)(4,1)}, u32[]{:S(2)}) copy-start(pred[1024,1024]{0,1:T(8,128)(4,1)} %get-tuple-element.70) | copy-start | bytes 3145732
  326.8 1.9 copy-start.15
  326.8 2.6 copy-start.19
  329.5 7.8 %copy-start.14 = (pred[8,128,3,192]{1,3,2,0:T(8,128)(4,1)S(1)}, pred[8,128,3,192]{1,3,2,0:T(8,128)(4,1)}, u32[]{:S(2)}) copy-start(pred[8,128,3,192]{1,3,2,0:T(8,128)(4,1)} %get-tuple-element.63) | copy-start | bytes 1769476
  329.5 7.8 %copy-start.18 = (bf16[1024,1,8,128]{3,0,2,1:T(8,128)(2,1)S(1)}, bf16[1024,1,8,128]{3,0,2,1:T(8,128)(2,1)}, u32[]{:S(2)}) copy-start(bf16[1024,1,8,128]{3,0,2,1:T(8,128)(2,1)} %copy.78) | copy-start | bytes 6291460
  337.3 8.2 %copy-start.16 = (pred[8,128,3,192]{1,3,2,0:T(8,128)(4,1)S(1)}, pred[8,128,3,192]{1,3,2,0:T(8,128)(4,1)}, u32[]{:S(2)}) copy-start(pred[8,128,3,192]{1,3,2,0:T(8,128)(4,1)} %get-tuple-element.64) | copy-start | bytes 1769476
  345.6 10.6 %copy-start.21 = (bf16[1,3,8,192,128]{4,3,2,1,0:T(8,128)(2,1)S(1)}, bf16[1,3,8,192,128]{4,3,2,1,0:T(8,128)(2,1)}, u32[]{:S(2)}) copy-start(bf16[1,3,8,192,128]{4,3,2,1,0:T(8,128)(2,1)} %get-tuple-element.41) | copy-start | bytes 3538948
  377.1 10.6 %copy-start.20 = (bf16[1,3,8,192,128]{4,3,2,1,0:T(8,128)(2,1)S(1)}, bf16[1,3,8,192,128]{4,3,2,1,0:T(8,128)(2,1)}, u32[]{:S(2)}) copy-start(bf16[1,3,8,192,128]{4,3,2,1,0:T(8,128)(2,1)} %get-tuple-element.39) | copy-start | bytes 3538948
  403.4 5.0 %copy-start.7 = (pred[1024,1024]{0,1:T(8,128)(4,1)S(1)}, pred[1024,1024]{0,1:T(8,128)(4,1)}, u32[]{:S(2)}) copy-start(pred[1024,1024]{0,1:T(8,128)(4,1)} %get-tuple-element.71) | copy-start | bytes 3145732
  408.4 14.3 %copy-start.13 = (bf16[2048,256]{1,0:T(8,128)(2,1)S(1)}, bf16[2048,256]{1,0:T(8,128)(2,1)}, u32[]{:S(2)}) copy-start(bf16[2048,256]{1,0:T(8,128)(2,1)} %gather_fusion.2) | copy-start | bytes 3145732
  422.7 17.6 %copy-start.5 = (pred[1024,1024]{0,1:T(8,128)(4,1)S(1)}, pred[1024,1024]{0,1:T(8,128)(4,1)}, u32[]{:S(2)}) copy-start(pred[1024,1024]{0,1:T(8,128)(4,1)} %get-tuple-element.70) | copy-start | bytes 3145732
Sparse Core Ops, SparseCore 0:
  107.0 64.2 all-gather.1
where the time goes:
time: 499 us; the launch traced here: 490 us
  local copies, waits for them, and re-layouts  122 us (24%)
  waiting for transfers between devices  113 us (23%)
  matrix products  98.6 us (20%)
  other arithmetic  88.1 us (18%)
  between operations  36.6 us (7%)
  starting transfers between devices  31.7 us (6%)
    ppermute x6, waiting for transfers between devices, shifted_2(): return lax.ppermute(block, axis, route)  97.3 us
    gather x1, local copies, waits for them, and re-layouts, shards(): table[where_at]  35.5 us
    dot_general x2, matrix products, shards(): jnp.einsum('gsn,nd->gsd', vert_weight.astype(jnp.bfloat16), vert_v, prefe...  34.7 us
    reduce_sum x2, other arithmetic, shards(): jnp.sum(vert_weight, axis=-1)  28.5 us
    dot_general x2, matrix products, shards(): jnp.einsum('sgd,nd->gsn', query_one, vert_k, preferred_element_type=jnp.f...  27.3 us
    reduce_sum x2, other arithmetic, shards(): jnp.sum(band_weight, axis=(-2, -1)).reshape(group_size, tok_count)  21.2 us
    dot_general x2, matrix products, shards(): jnp.einsum('gbqkt,kbtd->gbqd', band_weight.astype(jnp.bfloat16), tile_v,...  20.5 us
    unnamed x63, local copies, waits for them, and re-layouts  19 us
  transfers between devices with their start and end apart: 10, of which 7 were waited for; matrix products, arithmetic and copies ran while one was open for 28% of the time, Pallas kernels for 0%

commit v1 on v0

v1 whole, which is shorter than its diff:
```python
import functools

import jax
import jax.numpy as jnp
from jax import lax
from jax.experimental import pallas as pl
from jax.experimental.pallas import tpu as pltpu
from jax.sharding import PartitionSpec as P

HQ = 64
KVH = 8
DH = 128
NVERT = 1024
GROUP = HQ // KVH
BLOCK = 64
CAP = 96
NX, NY, NCORE, NTP = 4, 4, 2, 4
NCTX = NX * NY * NCORE
TOK = 1024
NBLK = TOK // BLOCK
PIECE = TOK // NTP
LOG2_SCALE = 1.4426950408889634 * DH**-0.5
NEG = -1e30
BF16 = jnp.bfloat16
F32 = jnp.float32
VMEM_LIMIT = 56 * 2**20


def params():
    return pltpu.CompilerParams(vmem_limit_bytes=VMEM_LIMIT)


def dot_t(left, right):
    return lax.dot_general(left, right, (((1,), (1,)), ((), ())), preferred_element_type=F32)


def tp_shift(block, distance):
    return lax.ppermute(block, "tp", [(i, (i + distance) % NTP) for i in range(NTP)])


def ctx_route(block, move):
    pairs = []
    for x in range(NX):
        for y in range(NY):
            for core in range(NCORE):
                to_x, to_y, to_core = move(x, y, core)
                source = (x * NY + y) * NCORE + core
                target = ((to_x % NX) * NY + to_y % NY) * NCORE + to_core % NCORE
                pairs.append((source, target))
    return lax.ppermute(block, "ctx", pairs)


def ctx_next(block):
    return lax.ppermute(block, "ctx", [(i, i + 1) for i in range(NCTX - 1)])


def join_kernel(rows_ref, keys_ref, p0, p1, p2, p3, out_ref, own_ref):
    for distance, piece in enumerate((p0, p1, p2, p3)):
        first = pl.multiple_of(rows_ref[distance] * PIECE, PIECE)
        out_ref[:, pl.ds(first, PIECE), :] = piece[...]
    spots = lax.broadcasted_iota(jnp.int32, (CAP, TOK), 1)
    for head in range(2):
        chosen = jnp.where(keys_ref[head] == spots, 1.0, 0.0).astype(BF16)
        own_ref[head] = jnp.dot(chosen, out_ref[head], preferred_element_type=F32).astype(BF16)


def join_pieces(rows, own_keys, pieces):
    vmem = pl.BlockSpec(memory_space=pltpu.VMEM)
    return pl.pallas_call(
        join_kernel,
        in_specs=[pl.BlockSpec(memory_space=pltpu.SMEM)] + [vmem] * 5,
        out_specs=[vmem, vmem],
        out_shape=[
            jax.ShapeDtypeStruct((2, TOK, 2 * DH), BF16),
            jax.ShapeDtypeStruct((2, CAP, 2 * DH), BF16),
        ],
        compiler_params=params(),
    )(rows, own_keys, *pieces)


def spread_kernel(shift_ref, table_ref, out_ref):
    group = pl.program_id(0)
    for i in range(8):
        for band in range(2):
            source = jnp.maximum(group * 8 + i - shift_ref[band], 0)
            out_ref[i, band] = table_ref[source]


def spread_windows(shifts, table):
    return pl.pallas_call(
        spread_kernel,
        grid_spec=pltpu.PrefetchScalarGridSpec(
            num_scalar_prefetch=1,
            grid=(NCTX // 8,),
            in_specs=[pl.BlockSpec((NCTX, BLOCK, 2 * DH), lambda g, s: (0, 0, 0))],
            out_specs=pl.BlockSpec((8, 2, BLOCK, 2 * DH), lambda g, s: (g, 0, 0, 0)),
        ),
        out_shape=jax.ShapeDtypeStruct((NCTX, 2, BLOCK, 2 * DH), BF16),
        compiler_params=params(),
    )(shifts, table)


def close_kernel(first_ref, *refs):
    sources, out_ref, total = refs[:8], refs[8], refs[9]
    head = pl.program_id(0)
    total[...] = jnp.zeros_like(total)
    for number, source in enumerate(sources):
        for i in range(4):
            first = first_ref[head, number * 4 + i]
            for half in range(2):
                columns = slice(half * DH, (half + 1) * DH)
                total[half, pl.ds(first, CAP), :] += source[i, 0, :, columns].astype(F32)
    for half in range(2):
        out_ref[0, :, half * DH : (half + 1) * DH] = total[half, :NVERT, :].astype(BF16)
    out_ref[0, :, 2 * DH :] = jnp.ones((NVERT, DH), BF16)


def close_up(firsts, gathered):
    return pl.pallas_call(
        close_kernel,
        grid_spec=pltpu.PrefetchScalarGridSpec(
            num_scalar_prefetch=1,
            grid=(2,),
            in_specs=[pl.BlockSpec((4, 1, CAP, 2 * DH), lambda h, s: (0, h, 0, 0))] * 8,
            out_specs=pl.BlockSpec((1, NVERT, 3 * DH), lambda h, s: (h, 0, 0)),
            scratch_shapes=[pltpu.VMEM((2, NVERT + CAP + 8, DH), F32)],
        ),
        out_shape=jax.ShapeDtypeStruct((2, NVERT, 3 * DH), BF16),
        compiler_params=params(),
    )(firsts, *gathered)


def stack_heads(ref, first):
    return jnp.concatenate(
        [ref[first : first + BLOCK, g * DH : (g + 1) * DH] for g in range(GROUP)], axis=0
    )


def band_bias():
    row = lax.broadcasted_iota(jnp.int32, (BLOCK, 2 * BLOCK), 0)
    column = lax.broadcasted_iota(jnp.int32, (BLOCK, 2 * BLOCK), 1)
    distance = row - column + BLOCK
    return jnp.where((distance >= 0) & (distance < BLOCK), 0.0, NEG)


def masked(scores, bias):
    width = scores.shape[1]
    return (scores.reshape(GROUP, BLOCK, width) + bias[None]).reshape(GROUP * BLOCK, width)


def near_kernel(piece_ref, q_ref, vert_ref, near_ref, spot_ref, mark_ref, *refs):
    out_ref, stat_ref, copy_ref = refs[-3:]
    tile = pl.program_id(1)
    ones = jnp.ones((2 * BLOCK, DH), BF16)
    lanes = lax.broadcasted_iota(jnp.int32, (BLOCK, DH), 1)
    bias = band_bias()
    copy_ref[...] = q_ref[...]
    subtiles = q_ref.shape[0] // BLOCK
    for sub in range(subtiles):
        block = piece_ref[0] * (PIECE // BLOCK) + tile * subtiles + sub
        query = stack_heads(q_ref, sub * BLOCK)
        near = near_ref[0, pl.ds(pl.multiple_of(block * BLOCK, BLOCK), 2 * BLOCK), :]
        position = block * BLOCK + lax.broadcasted_iota(jnp.int32, (BLOCK, NVERT), 0)
        vert_bias = jnp.where(spot_ref[0] <= position, 0.0, NEG)
        near_bias = bias + mark_ref[0, 0, pl.ds(block, 1), :]
        vert_s = masked(dot_t(query, vert_ref[0, :, :DH]), vert_bias)
        near_s = masked(dot_t(query, near[:, :DH]), near_bias)
        top = jnp.maximum(
            jnp.max(vert_s, axis=-1, keepdims=True), jnp.max(near_s, axis=-1, keepdims=True)
        )
        top = top * LOG2_SCALE
        vert_w = jnp.exp2(vert_s * LOG2_SCALE - top).astype(BF16)
        near_w = jnp.exp2(near_s * LOG2_SCALE - top).astype(BF16)
        both = jnp.dot(vert_w, vert_ref[0, :, DH:], preferred_element_type=F32)
        both = both + jnp.dot(
            near_w, jnp.concatenate([near[:, DH:], ones], axis=1), preferred_element_type=F32
        )
        total = both[:, DH:]
        out = both[:, :DH] / total
        level = top + jnp.log2(total)
        stat = jnp.zeros((BLOCK, DH), F32)
        for g in range(GROUP):
            rows = slice(g * BLOCK, (g + 1) * BLOCK)
            out_ref[sub * BLOCK : (sub + 1) * BLOCK, g * DH : (g + 1) * DH] = out[rows]
            stat = jnp.where(lanes == g, level[rows], stat)
        stat_ref[sub * BLOCK : (sub + 1) * BLOCK, :] = stat


def near_attention(piece, query, vert, near, spots, marks, state):
    tile = 128
    tiles = PIECE // tile
    wide = GROUP * DH
    at_piece = lambda h, t, s: (s[0] * tiles + t, h)
    shapes = [
        jax.ShapeDtypeStruct((TOK, 2 * wide), F32),
        jax.ShapeDtypeStruct((TOK, 2 * DH), F32),
        jax.ShapeDtypeStruct((TOK, 2 * wide), BF16),
    ]
    state_specs = [pl.BlockSpec(memory_space=pl.ANY)] * len(state)
    rows = PIECE * 2 * GROUP
    return pl.pallas_call(
        near_kernel,
        grid_spec=pltpu.PrefetchScalarGridSpec(
            num_scalar_prefetch=1,
            grid=(2, tiles),
            in_specs=[
                pl.BlockSpec((tile, wide), lambda h, t, s: (t, h)),
                pl.BlockSpec((1, NVERT, 3 * DH), lambda h, t, s: (h, 0, 0)),
                pl.BlockSpec((1, TOK + BLOCK, 2 * DH), lambda h, t, s: (h, 0, 0)),
                pl.BlockSpec((1, 1, NVERT), lambda h, t, s: (h, 0, 0)),
                pl.BlockSpec((1, 1, NBLK, 2 * BLOCK), lambda h, t, s: (h, 0, 0, 0)),
            ]
            + state_specs,
            out_specs=[
                pl.BlockSpec((tile, wide), at_piece),
                pl.BlockSpec((tile, DH), at_piece),
                pl.BlockSpec((tile, wide), at_piece),
            ],
        ),
        out_shape=shapes,
        input_output_aliases={6 + i: i for i in range(len(state))},
        cost_estimate=pl.CostEstimate(
            flops=rows * (NVERT + 2 * BLOCK) * 4 * 2 * DH,
            bytes_accessed=8 * 2**20,
            transcendentals=rows * (NVERT + 2 * BLOCK),
        ),
        compiler_params=params(),
    )(piece, query, vert, near, spots, marks, *state)


def far_kernel(order_ref, q_ref, prior_ref, stat_ref, far_ref, halo_ref, mark_ref, out_ref, keys):
    head = pl.program_id(0)
    tile = pl.program_id(1)

    @pl.when(tile == 0)
    def _():
        for band in range(2):
            keys[band, :BLOCK, :] = halo_ref[0, band]
            for block in range(NBLK):
                source = lax.rem(block + NBLK - order_ref[head * 2 + band], NBLK)
                keys[band, (block + 1) * BLOCK : (block + 2) * BLOCK, :] = far_ref[0, source, band]

    ones = jnp.ones((4 * BLOCK, DH), BF16)
    bias = band_bias()
    subtiles = q_ref.shape[0] // BLOCK
    for sub in range(subtiles):
        block = tile * subtiles + sub
        first = pl.multiple_of(block * BLOCK, BLOCK)
        query = stack_heads(q_ref, sub * BLOCK)
        near = jnp.concatenate([keys[band, pl.ds(first, 2 * BLOCK), :] for band in range(2)], axis=0)
        both_bias = jnp.concatenate(
            [bias + mark_ref[0, 1 + band, pl.ds(block, 1), :] for band in range(2)], axis=1
        )
        scores = masked(dot_t(query, near[:, :DH]), both_bias)
        stat = stat_ref[sub * BLOCK : (sub + 1) * BLOCK, :]
        level = jnp.concatenate([stat[:, g : g + 1] for g in range(GROUP)], axis=0)
        top = jnp.maximum(jnp.max(scores, axis=-1, keepdims=True) * LOG2_SCALE, level)
        weight = jnp.exp2(scores * LOG2_SCALE - top).astype(BF16)
        both = jnp.dot(
            weight, jnp.concatenate([near[:, DH:], ones], axis=1), preferred_element_type=F32
        )
        prior_w = jnp.exp2(level - top)
        total = both[:, DH:] + prior_w
        prior = jnp.concatenate(
            [
                prior_ref[sub * BLOCK : (sub + 1) * BLOCK, g * DH : (g + 1) * DH]
                for g in range(GROUP)
            ],
            axis=0,
        )
        out = ((both[:, :DH] + prior * prior_w) / total).astype(BF16)
        for g in range(GROUP):
            out_ref[sub * BLOCK : (sub + 1) * BLOCK, g * DH : (g + 1) * DH] = out[
                g * BLOCK : (g + 1) * BLOCK
            ]


def far_attention(orders, query, prior, stats, far, halo, marks):
    tile = 128
    wide = GROUP * DH
    rows = TOK * 2 * GROUP
    return pl.pallas_call(
        far_kernel,
        grid_spec=pltpu.PrefetchScalarGridSpec(
            num_scalar_prefetch=1,
            grid=(2, TOK // tile),
            in_specs=[
                pl.BlockSpec((tile, wide), lambda h, t, s: (t, h)),
                pl.BlockSpec((tile, wide), lambda h, t, s: (t, h)),
                pl.BlockSpec((tile, DH), lambda h, t, s: (t, h)),
                pl.BlockSpec((1, NBLK, 2, BLOCK, 2 * DH), lambda h, t, s: (h, 0, 0, 0, 0)),
                pl.BlockSpec((1, 2, BLOCK, 2 * DH), lambda h, t, s: (h, 0, 0, 0)),
                pl.BlockSpec((1, 3, NBLK, 2 * BLOCK), lambda h, t, s: (h, 0, 0, 0)),
            ],
            out_specs=pl.BlockSpec((tile, wide), lambda h, t, s: (t, h)),
            scratch_shapes=[pltpu.VMEM((2, TOK + BLOCK, 2 * DH), BF16)],
        ),
        out_shape=jax.ShapeDtypeStruct((TOK, 2 * wide), BF16),
        cost_estimate=pl.CostEstimate(
            flops=rows * 4 * BLOCK * 4 * 2 * DH,
            bytes_accessed=20 * 2**20,
            transcendentals=rows * 4 * BLOCK,
        ),
        compiler_params=params(),
    )(orders, query, prior, stats, far, halo, marks)


def shards(queries, key_rows, value_rows, vertical_keys, slash_offsets):
    tp = lax.axis_index("tp")
    ctx = lax.axis_index("ctx")
    base = ctx * TOK
    heads = vertical_keys.shape[0]

    kv = jnp.concatenate(
        (key_rows.reshape(PIECE, KVH, DH), value_rows.reshape(PIECE, KVH, DH)), axis=2
    ).transpose(1, 0, 2)
    kv_pieces = []
    for distance in range(NTP):
        part = lax.dynamic_slice_in_dim(kv, heads * ((tp + distance) % NTP), heads, 0)
        kv_pieces.append(tp_shift(part, distance) if distance else part)
    kv_pieces[1:], queries = lax.optimization_barrier((kv_pieces[1:], queries))

    first_own = jnp.sum(vertical_keys < base, axis=1)
    own_count = jnp.sum(vertical_keys < base + TOK, axis=1) - first_own
    extended = jnp.concatenate((vertical_keys, jnp.zeros((heads, CAP), jnp.int32)), axis=1)
    own_keys = jnp.stack(
        [lax.dynamic_slice_in_dim(extended[h], first_own[h], CAP, 0) for h in range(heads)]
    )
    live = jnp.arange(CAP, dtype=jnp.int32)[None, :] < own_count[:, None]
    own_keys = jnp.where(live, own_keys - base, -1)
    piece_rows = (tp + NTP - jnp.arange(NTP, dtype=jnp.int32)) % NTP
    local, own = join_pieces(piece_rows, own_keys[:, :, None], kv_pieces)

    table = lax.all_to_all(
        local.reshape(NCTX, BLOCK, 2 * DH), "ctx", split_axis=0, concat_axis=0, tiled=True
    )

    q_pieces = []
    for distance in range(NTP):
        wide = queries.shape[1] // NTP
        part = lax.dynamic_slice_in_dim(queries, wide * ((tp + distance) % NTP), wide, 1)
        q_pieces.append(tp_shift(part, distance) if distance else part)

    along_y = [own]
    for step in (1, 2, 3):
        along_y.append(ctx_route(own, lambda x, y, core, step=step: (x, y + step, core)))
    along_y = jnp.stack(along_y)
    along_x = [along_y]
    for step in (1, 2, 3):
        along_x.append(ctx_route(along_y, lambda x, y, core, step=step: (x + step, y, core)))
    across = [ctx_route(part, lambda x, y, core: (x, y, core + 1)) for part in along_x]
    slots = jnp.arange(NCTX, dtype=jnp.int32)
    slot_core, slot_x, slot_y = slots // 16, (slots // 4) % 4, slots % 4
    x, y, core = ctx // 8, (ctx // 2) % 4, ctx % 2
    owners = ((x + 4 - slot_x) % 4) * 8 + ((y + 4 - slot_y) % 4) * 2 + (core + slot_core) % 2
    firsts = jnp.sum(
        vertical_keys[:, None, :] < (owners * TOK)[None, :, None], axis=2, dtype=jnp.int32
    )
    vert = close_up(firsts, along_x + across)

    high = (vertical_keys[:, :, None] // BLOCK == jnp.arange(NCTX * NBLK)).astype(BF16)
    low = (vertical_keys[:, :, None] % BLOCK == jnp.arange(BLOCK)).astype(BF16)
    marked = jnp.einsum("hnb,hnl->hbl", high, low, preferred_element_type=F32)
    closed = jnp.where(marked > 0.5, NEG, 0.0)
    closed = jnp.concatenate(
        (jnp.full((heads, NCTX * NBLK + 1, BLOCK), NEG, F32), closed), axis=1
    )
    hops = slash_offsets // BLOCK
    marks = jnp.stack(
        [
            jnp.stack(
                [
                    lax.dynamic_slice_in_dim(
                        closed[h], ctx * NBLK - hops[h, band] + NCTX * NBLK, NBLK + 1, 0
                    )
                    for band in range(3)
                ]
            )
            for h in range(heads)
        ]
    )
    marks = jnp.concatenate((marks[:, :, :-1], marks[:, :, 1:]), axis=3)

    near = jnp.concatenate((ctx_next(local[:, TOK - BLOCK :]), local), axis=1)
    spots = (vertical_keys - base)[:, None, :]
    state = []
    for distance in (0, 1, 3, 2):
        state = near_attention(
            piece_rows[distance : distance + 1], q_pieces[distance], vert, near, spots, marks, state
        )

    far_hops = hops[:, 1:]
    shifts = (ctx % NBLK + lax.dynamic_index_in_dim(far_hops, ctx // NBLK, 0, False)) // NBLK
    windows = lax.all_to_all(
        spread_windows(shifts, table), "ctx", split_axis=0, concat_axis=0, tiled=True
    ).reshape(heads, NBLK, 2, BLOCK, 2 * DH)
    orders = far_hops % NBLK
    last = jnp.stack(
        [
            jnp.stack(
                [
                    lax.dynamic_index_in_dim(
                        windows[h, :, band], (2 * NBLK - 1 - orders[h, band]) % NBLK, 0, False
                    )
                    for band in range(2)
                ]
            )
            for h in range(heads)
        ]
    )
    halo = ctx_next(last)
    prior, stats, query = state
    return far_attention(orders.reshape(-1), query, prior, stats, windows, halo, marks)


def solution(mesh):
    in_specs = (
        P(("ctx", "tp"), None),
        P(("ctx", "tp"), None),
        P(("ctx", "tp"), None),
        P("tp", None),
        P("tp", None),
    )
    out_specs = P("ctx", "tp")
    return jax.shard_map(shards, mesh=mesh, in_specs=in_specs, out_specs=out_specs, check_vma=False)
```

time: 499 us -> 190 us (0.38)
  the two profiles are of different devices: /device:TPU:12 before, /device:TPU:6 now
where the time goes in v1:
time: 190 us; the launch traced here: 187 us
  Pallas kernels  79.7 us (42%)
  starting transfers between devices  38.1 us (20%)
  waiting for transfers between devices  32.9 us (17%)
  local copies, waits for them, and re-layouts  18.6 us (10%)
  between operations  10.5 us (6%)
  other arithmetic  5.76 us (3%)
    pallas_call x4, Pallas kernels, near_attention(): pl.pallas_call(near_kernel, grid_spec=pltpu.PrefetchScalarGridSpec(num_sc...  41.6 us
    pallas_call x1, Pallas kernels, far_attention(): pl.pallas_call(far_kernel, grid_spec=pltpu.PrefetchScalarGridSpec(num_sca...  27.9 us
    ppermute x6, waiting for transfers between devices, tp_shift(): lax.ppermute(block, 'tp', [(i, (i + distance) % NTP) for i in range(NTP)])  22.6 us
    ppermute x6, starting transfers between devices, tp_shift(): lax.ppermute(block, 'tp', [(i, (i + distance) % NTP) for i in range(NTP)])  10.3 us
    ppermute x10, waiting for transfers between devices, ctx_route(): return lax.ppermute(block, 'ctx', pairs)  10.3 us
    ppermute x10, starting transfers between devices, ctx_route(): return lax.ppermute(block, 'ctx', pairs)  9.16 us
    unnamed x37, local copies, waits for them, and re-layouts  7.9 us
    all_to_all x1, starting transfers between devices, shards(): lax.all_to_all(local.reshape(NCTX, BLOCK, 2 * DH), 'ctx', split_axis=0, c...  7.75 us
  transfers between devices with their start and end apart: 20, of which 2 were waited for; matrix products, arithmetic and copies ran while one was open for 9% of the time, Pallas kernels for 26%

profile of v1, /device:TPU:6, one launch (start us, length us, event | category | flops | bytes accessed | tf_op | source)
XLA Modules:
  0.0 187.1 jit_solution(3015438804197100122)
XLA Ops:
  0.0 1.3 copy.43
  2.1 0.8 fusion.11
  3.0 1.9 %collective-permute-start = (bf16[2,256,256]{2,1,0:T(8,128)(2,1)S(1)}, bf16[2,256,256]{2,1,0:T(8,128)(2,1)S(1)}, u32[]{:S(2)}, u32[]{:S(2)}) collective-permute-start(bf16[2,256,256]{2,1,0:T(8,128)(2,1)S(1)} %get-tuple-element.52), channel_id=1, source_target_pairs={{0,1},{1,2},{2,3},{3,0},{4,5},{5,6},{6,7},{7,4},{8,9},{9,10},{10,1... | collective-permute-start | bytes 786440 | tf_op jit(solution)/shard_map/ppermute | solution.py:38
  4.9 3.6 %collective-permute-start.1 = (bf16[2,256,256]{2,1,0:T(8,128)(2,1)S(1)}, bf16[2,256,256]{2,1,0:T(8,128)(2,1)S(1)}, u32[]{:S(2)}, u32[]{:S(2)}) collective-permute-start(bf16[2,256,256]{2,1,0:T(8,128)(2,1)S(1)} %get-tuple-element.53), channel_id=1, source_target_pairs={{0,2},{1,3},{2,0},{3,1},{4,6},{5,7},{6,4},{7,5},{8,10},{9,11},{10,... | collective-permute-start | bytes 786440 | tf_op jit(solution)/shard_map/ppermute | solution.py:38
  8.5 1.0 collective-permute-start.2
  9.6 0.6 fusion.47
  12.9 0.7 fusion.45
  15.1 0.7 fusion.43
  15.8 0.7 fusion.19.keys_ref
  16.5 0.6 and_select_fusion.10.rows_ref
  20.9 1.5 fusion.7
  22.5 0.7 copy-done.5
  23.4 2.3 %shard_map.55 = (bf16[2,1024,256]{2,1,0:T(8,128)(2,1)}, bf16[2,96,256]{2,1,0:T(8,128)(2,1)}) custom-call(s32[4]{0:T(128)} %and_select_fusion.10.rows_ref, s32[2,96,1]{2,1,0:T(8,128)} %fusion.19.keys_ref, bf16[2,256,256]{2,1,0:T(8,128)(2,1)} %get-tuple-element.51.p0, bf16[2,256,256]{2,1,0:T(8,128)(2,1)} %copy-done.5, bf16[2,256,256]{2,1,0:T(8,128)(2,1)} %copy-done.6, ...), custom_call_target="tpu_custom_call" | custom-call | tf_op jit(solution)/shard_map/pallas_call | solution.py:69
  25.7 7.7 %all-to-all-start = ((bf16[32,64,256]{2,1,0:T(8,128)(2,1)}), bf16[32,64,256]{2,1,0:T(8,128)(2,1)S(1)}, u32[]{:S(2)}, u32[]{:S(2)}) async-start(bf16[32,64,256]{2,1,0:T(8,128)(2,1)} %bitcast.58), calls=%async_computation | async-start | bytes 2097152 | tf_op jit(solution)/shard_map/all_to_all | solution.py:334
  33.6 0.7 fusion.21.mark_ref
  34.4 1.5 collective-permute-start.4
  35.8 2.7 %collective-permute-start.5 = (bf16[2,96,256]{2,1,0:T(8,128)(2,1)S(1)}, bf16[2,96,256]{2,1,0:T(8,128)(2,1)S(1)}, u32[]{:S(2)}, u32[]{:S(2)}) collective-permute-start(bf16[2,96,256]{2,1,0:T(8,128)(2,1)S(1)} %copy-done.9), channel_id=1, source_target_pairs={{0,16},{4,20},{8,24},{12,28},{16,0},{20,4},{24,8},{28,12},{32,48},... | collective-permute-start | bytes 294920 | tf_op jit(solution)/shard_map/ppermute | solution.py:50
  38.5 1.4 collective-permute-start.6
  40.0 0.6 and_select_fusion.2.shift_ref
  40.6 0.6 slice.94
  41.2 1.9 %collective-permute-start.14 = (bf16[2,64,256]{2,1,0:T(8,128)(2,1)}, bf16[2,64,256]{2,1,0:T(8,128)(2,1)}, u32[]{:S(2)}, u32[]{:S(2)}) collective-permute-start(bf16[2,64,256]{2,1,0:T(8,128)(2,1)} %slice.94), channel_id=1, source_target_pairs={{0,4},{4,8},{8,12},{12,16},{16,20},{20,24},{24,28},{28,32},{32,36}... | collective-permute-start | bytes 196616 | tf_op jit(solution)/shard_map/ppermute | solution.py:54
  43.1 10.3 %collective-permute-done.4 = bf16[2,96,256]{2,1,0:T(8,128)(2,1)S(1)} collective-permute-done((bf16[2,96,256]{2,1,0:T(8,128)(2,1)S(1)}, bf16[2,96,256]{2,1,0:T(8,128)(2,1)S(1)}, u32[]{:S(2)}, u32[]{:S(2)}) %collective-permute-start.4) | collective-permute-done | bytes 98336 | tf_op jit(solution)/shard_map/ppermute | solution.py:50
  53.5 0.6 collective-permute-start.7
  54.1 2.3 %collective-permute-start.8 = (bf16[4,2,96,256]{3,2,1,0:T(8,128)(2,1)S(1)}, bf16[4,2,96,256]{3,2,1,0:T(8,128)(2,1)}, u32[]{:S(2)}, u32[]{:S(2)}) collective-permute-start(bf16[4,2,96,256]{3,2,1,0:T(8,128)(2,1)S(1)} %pad_maximum_fusion.refs_0_), channel_id=1, source_target_pairs={{0,64},{4,68},{8,72},{12,76},{16,80},{20,84},{24,88},{28,92},{32,9... | collective-permute-start | bytes 1179656 | tf_op jit(solution)/shard_map/ppermute | solution.py:50
  56.5 1.0 copy-done.2
  57.5 3.7 %shard_map.61 = bf16[32,2,64,256]{3,2,1,0:T(8,128)(2,1)} custom-call(s32[2]{0:T(128)} %and_select_fusion.2.shift_ref, bf16[32,64,256]{2,1,0:T(8,128)(2,1)} %copy-done.2), custom_call_target="tpu_custom_call" | custom-call | tf_op jit(solution)/shard_map/pallas_call | solution.py:90
  61.2 7.1 %all-to-all-start.1 = ((bf16[32,2,64,256]{3,2,1,0:T(8,128)(2,1)}), bf16[32,2,64,256]{3,2,1,0:T(8,128)(2,1)S(1)}, u32[]{:S(2)}, u32[]{:S(2)}) async-start(bf16[32,2,64,256]{3,2,1,0:T(8,128)(2,1)} %shard_map.61), calls=%async_computation.1 | async-start | bytes 4194304 | tf_op jit(solution)/shard_map/all_to_all | solution.py:394
  68.3 4.4 %constant_dynamic-slice_fusion.1 = (bf16[256,2048]{1,0:T(8,128)(2,1)}, bf16[256,2048]{1,0:T(8,128)(2,1)}, bf16[256,2048]{1,0:T(8,128)(2,1)}, bf16[256,2048]{1,0:T(8,128)(2,1)}) fusion(bf16[256,8192]{1,0:T(8,128)(2,1)} %param.5, s32[]{:T(128)S(6)} %select_n.275, s32[]{:T(128)S(6)} %select_n.274, s32[]{:T(128)S(6)} %select_n.273, s32[]{:T(128)S(6)} %select_n.247), kind=kLoop, calls=%fused_computation.56 | loop fusion | bytes 8388624 | tf_op jit(solution)/shard_map/dynamic_slice | solution.py:341
  72.7 1.1 collective-permute-start.16
  73.8 0.7 fusion.46
  75.0 0.5 fusion.36
  78.0 1.3 reshape.219.order_ref
  79.3 0.6 broadcast_in_dim.13.spot_ref
  79.9 1.4 convert_reduce_fusion.first_ref
  81.3 2.2 %collective-permute-start.15 = (bf16[256,2048]{1,0:T(8,128)(2,1)}, bf16[256,2048]{1,0:T(8,128)(2,1)S(1)}, u32[]{:S(2)}, u32[]{:S(2)}) collective-permute-start(bf16[256,2048]{1,0:T(8,128)(2,1)} %get-tuple-element.45), channel_id=1, source_target_pairs={{0,3},{1,0},{2,1},{3,2},{4,7},{5,4},{6,5},{7,6},{8,11},{9,8},{10,9... | collective-permute-start | bytes 3145736 | tf_op jit(solution)/shard_map/ppermute | solution.py:38
  83.5 0.8 constant_dynamic-update-slice_fusion.1
  85.0 4.1 %shard_map.56.vert_ref = bf16[2,1024,384]{2,1,0:T(8,128)(2,1)} custom-call(s32[2,32]{1,0:T(2,128)} %convert_reduce_fusion.first_ref, bf16[4,2,96,256]{3,2,1,0:T(8,128)(2,1)} %copy-done.3, bf16[4,2,96,256]{3,2,1,0:T(8,128)(2,1)} %collective-permute-done.7.refs_1_, bf16[4,2,96,256]{3,2,1,0:T(8,128)(2,1)} %collective-permute-done.8.refs_2_, ...), custom_call_target="tpu_custom_call" | custom-call | tf_op jit(solution)/shard_map/pallas_call | solution.py:119
  89.1 10.3 %shard_map.57 = (f32[1024,2048]{1,0:T(8,128)}, f32[1024,256]{1,0:T(8,128)}, bf16[1024,2048]{1,0:T(8,128)(2,1)}) custom-call(s32[1]{0:T(128)} %get-tuple-element.82.piece_ref, bf16[256,2048]{1,0:T(8,128)(2,1)} %get-tuple-element.43.q_ref, bf16[2,1024,384]{2,1,0:T(8,128)(2,1)} %shard_map.56.vert_ref, bf16[2,1088,256]{2,1,0:T(8,128)(2,1)} %copy-done.13, ...), custom_call_target="tpu_custom_call" | custom-call | flops 4831838208 | bytes 8388608 | tf_op jit(solution)/shard_map/pallas_call | solution.py:201
  99.4 22.5 %collective-permute-done.16.q_ref = bf16[256,2048]{1,0:T(8,128)(2,1)} collective-permute-done((bf16[256,2048]{1,0:T(8,128)(2,1)}, bf16[256,2048]{1,0:T(8,128)(2,1)}, u32[]{:S(2)}, u32[]{:S(2)}) %collective-permute-start.16) | collective-permute-done | bytes 1048608 | tf_op jit(solution)/shard_map/ppermute | solution.py:38
  121.9 10.5 %shard_map.58 = (f32[1024,2048]{1,0:T(8,128)}, f32[1024,256]{1,0:T(8,128)}, bf16[1024,2048]{1,0:T(8,128)(2,1)}) custom-call(s32[1]{0:T(128)} %get-tuple-element.83.piece_ref, bf16[256,2048]{1,0:T(8,128)(2,1)} %collective-permute-done.16.q_ref, bf16[2,1024,384]{2,1,0:T(8,128)(2,1)} %shard_map.56.vert_ref, ...), custom_call_target="tpu_custom_call", output_to_operand_aliasing={{0}: (6, {}), {1}: (7, {}), {2}: (8, {})} | custom-call | flops 4831838208 | bytes 8388608 | tf_op jit(solution)/shard_map/pallas_call | solution.py:201
  132.4 1.0 copy-done.16
  133.4 10.4 %shard_map.59 = (f32[1024,2048]{1,0:T(8,128)}, f32[1024,256]{1,0:T(8,128)}, bf16[1024,2048]{1,0:T(8,128)(2,1)}) custom-call(s32[1]{0:T(128)} %get-tuple-element.84.piece_ref, bf16[256,2048]{1,0:T(8,128)(2,1)} %copy-done.16, bf16[2,1024,384]{2,1,0:T(8,128)(2,1)} %shard_map.56.vert_ref, ...), custom_call_target="tpu_custom_call", output_to_operand_aliasing={{0}: (6, {}), {1}: (7, {}), {2}: (8, {})} | custom-call | flops 4831838208 | bytes 8388608 | tf_op jit(solution)/shard_map/pallas_call | solution.py:201
  144.1 1.1 copy-done
  145.2 1.9 %collective-permute-start.17 = (bf16[2,2,64,256]{3,2,1,0:T(8,128)(2,1)S(1)}, bf16[2,2,64,256]{3,2,1,0:T(8,128)(2,1)S(1)}, u32[]{:S(2)}, u32[]{:S(2)}) collective-permute-start(bf16[2,2,64,256]{3,2,1,0:T(8,128)(2,1)S(1)} %pad_maximum_fusion.1), channel_id=1, source_target_pairs={{0,4},{4,8},{8,12},{12,16},{16,20},{20,24},{24,28},{28,32},{32,36}... | collective-permute-start | bytes 393224 | tf_op jit(solution)/shard_map/ppermute | solution.py:54
  147.2 1.0 copy-done.15
  148.1 10.4 %shard_map.60 = (f32[1024,2048]{1,0:T(8,128)}, f32[1024,256]{1,0:T(8,128)}, bf16[1024,2048]{1,0:T(8,128)(2,1)}) custom-call(s32[1]{0:T(128)} %get-tuple-element.85.piece_ref, bf16[256,2048]{1,0:T(8,128)(2,1)} %copy-done.15, bf16[2,1024,384]{2,1,0:T(8,128)(2,1)} %shard_map.56.vert_ref, ...), custom_call_target="tpu_custom_call", output_to_operand_aliasing={{0}: (6, {}), {1}: (7, {}), {2}: (8, {})} | custom-call | flops 4831838208 | bytes 8388608 | tf_op jit(solution)/shard_map/pallas_call | solution.py:201
  158.5 0.6 copy-done.8
  159.2 27.9 %shard_map.62 = bf16[1024,2048]{1,0:T(8,128)(2,1)} custom-call(s32[4]{0:T(128)} %reshape.219.order_ref, bf16[1024,2048]{1,0:T(8,128)(2,1)} %get-tuple-element.38.q_ref, f32[1024,2048]{1,0:T(8,128)} %get-tuple-element.39.prior_ref, f32[1024,256]{1,0:T(8,128)} %get-tuple-element.40.stat_ref, bf16[2,16,2,64,256]{4,3,2,1,0:T(8,128)(2,1)} %bitcast.57, ...), custom_call_target="tpu_custom_call" | custom-call | flops 4294967296 | bytes 20971520 | tf_op jit(solution)/shard_map/pallas_call | solution.py:282
  (78 shorter events, 3.2 us)
Async XLA Ops:
  0.0 1.6 copy-start.4
  1.6 7.9 %copy-start.10 = (s32[2,1024]{1,0:T(2,128)S(1)}, s32[2,1024]{1,0:T(2,128)}, u32[]{:S(2)}) copy-start(s32[2,1024]{1,0:T(2,128)} %param.8) | copy-start | bytes 24580
  1.6 11.2 %copy-start.14 = (s32[2,3]{1,0:T(2,128)S(1)}, s32[2,3]{1,0:T(2,128)}, u32[]{:S(2)}) copy-start(s32[2,3]{1,0:T(2,128)} %param.9) | copy-start | bytes 76
  3.0 19.5 %collective-permute-start = (bf16[2,256,256]{2,1,0:T(8,128)(2,1)S(1)}, bf16[2,256,256]{2,1,0:T(8,128)(2,1)S(1)}, u32[]{:S(2)}, u32[]{:S(2)}) collective-permute-start(bf16[2,256,256]{2,1,0:T(8,128)(2,1)S(1)} %get-tuple-element.52), channel_id=1, source_target_pairs={{0,1},{1,2},{2,3},{3,0},{4,5},{5,6},{6,7},{7,4},{8,9},{9,10},{10,1... | collective-permute-start | bytes 786440 | tf_op jit(solution)/shard_map/ppermute | solution.py:38
  4.9 17.6 %collective-permute-start.1 = (bf16[2,256,256]{2,1,0:T(8,128)(2,1)S(1)}, bf16[2,256,256]{2,1,0:T(8,128)(2,1)S(1)}, u32[]{:S(2)}, u32[]{:S(2)}) collective-permute-start(bf16[2,256,256]{2,1,0:T(8,128)(2,1)S(1)} %get-tuple-element.53), channel_id=1, source_target_pairs={{0,2},{1,3},{2,0},{3,1},{4,6},{5,7},{6,4},{7,5},{8,10},{9,11},{10,... | collective-permute-start | bytes 786440 | tf_op jit(solution)/shard_map/ppermute | solution.py:38
  8.5 14.0 %collective-permute-start.2 = (bf16[2,256,256]{2,1,0:T(8,128)(2,1)S(1)}, bf16[2,256,256]{2,1,0:T(8,128)(2,1)S(1)}, u32[]{:S(2)}, u32[]{:S(2)}) collective-permute-start(bf16[2,256,256]{2,1,0:T(8,128)(2,1)S(1)} %get-tuple-element.54), channel_id=1, source_target_pairs={{0,3},{1,0},{2,1},{3,2},{4,7},{5,4},{6,5},{7,6},{8,11},{9,8},{10,9... | collective-permute-start | bytes 786440 | tf_op jit(solution)/shard_map/ppermute | solution.py:38
  13.6 12.1 %copy-start.12 = (s32[2,2]{1,0:T(2,128)}, s32[2,2]{1,0:T(2,128)S(1)}, u32[]{:S(2)}) copy-start(s32[2,2]{1,0:T(2,128)S(1)} %get-tuple-element.75) | copy-start | bytes 52
  22.5 0.7 copy-start.5
  22.5 0.8 copy-start.6
  22.5 0.9 copy-start.7
  25.7 8.7 %copy-start.9 = (bf16[2,96,256]{2,1,0:T(8,128)(2,1)S(1)}, bf16[2,96,256]{2,1,0:T(8,128)(2,1)}, u32[]{:S(2)}) copy-start(bf16[2,96,256]{2,1,0:T(8,128)(2,1)} %get-tuple-element.27) | copy-start | bytes 294916
  25.7 14.9 %copy-start.1 = (bf16[2,1024,256]{2,1,0:T(8,128)(2,1)S(1)}, bf16[2,1024,256]{2,1,0:T(8,128)(2,1)}, u32[]{:S(2)}) copy-start(bf16[2,1024,256]{2,1,0:T(8,128)(2,1)} %get-tuple-element.28) | copy-start | bytes 3145732
  25.7 30.7 %all-to-all-start = ((bf16[32,64,256]{2,1,0:T(8,128)(2,1)}), bf16[32,64,256]{2,1,0:T(8,128)(2,1)S(1)}, u32[]{:S(2)}, u32[]{:S(2)}) async-start(bf16[32,64,256]{2,1,0:T(8,128)(2,1)} %bitcast.58), calls=%async_computation | async-start | bytes 2097152 | tf_op jit(solution)/shard_map/all_to_all | solution.py:334
  34.4 19.1 %collective-permute-start.4 = (bf16[2,96,256]{2,1,0:T(8,128)(2,1)S(1)}, bf16[2,96,256]{2,1,0:T(8,128)(2,1)S(1)}, u32[]{:S(2)}, u32[]{:S(2)}) collective-permute-start(bf16[2,96,256]{2,1,0:T(8,128)(2,1)S(1)} %copy-done.9), channel_id=1, source_target_pairs={{0,8},{4,12},{8,16},{12,20},{16,24},{20,28},{24,0},{28,4},{32,40},... | collective-permute-start | bytes 294920 | tf_op jit(solution)/shard_map/ppermute | solution.py:50
  35.8 17.6 %collective-permute-start.5 = (bf16[2,96,256]{2,1,0:T(8,128)(2,1)S(1)}, bf16[2,96,256]{2,1,0:T(8,128)(2,1)S(1)}, u32[]{:S(2)}, u32[]{:S(2)}) collective-permute-start(bf16[2,96,256]{2,1,0:T(8,128)(2,1)S(1)} %copy-done.9), channel_id=1, source_target_pairs={{0,16},{4,20},{8,24},{12,28},{16,0},{20,4},{24,8},{28,12},{32,48},... | collective-permute-start | bytes 294920 | tf_op jit(solution)/shard_map/ppermute | solution.py:50
  38.5 14.9 %collective-permute-start.6 = (bf16[2,96,256]{2,1,0:T(8,128)(2,1)S(1)}, bf16[2,96,256]{2,1,0:T(8,128)(2,1)S(1)}, u32[]{:S(2)}, u32[]{:S(2)}) collective-permute-start(bf16[2,96,256]{2,1,0:T(8,128)(2,1)S(1)} %copy-done.9), channel_id=1, source_target_pairs={{0,24},{4,28},{8,0},{12,4},{16,8},{20,12},{24,16},{28,20},{32,56},... | collective-permute-start | bytes 294920 | tf_op jit(solution)/shard_map/ppermute | solution.py:50
  41.2 31.5 %collective-permute-start.14 = (bf16[2,64,256]{2,1,0:T(8,128)(2,1)}, bf16[2,64,256]{2,1,0:T(8,128)(2,1)}, u32[]{:S(2)}, u32[]{:S(2)}) collective-permute-start(bf16[2,64,256]{2,1,0:T(8,128)(2,1)} %slice.94), channel_id=1, source_target_pairs={{0,4},{4,8},{8,12},{12,16},{16,20},{20,24},{24,28},{28,32},{32,36}... | collective-permute-start | bytes 196616 | tf_op jit(solution)/shard_map/ppermute | solution.py:54
  53.5 19.2 %copy-start.3 = (bf16[4,2,96,256]{3,2,1,0:T(8,128)(2,1)}, bf16[4,2,96,256]{3,2,1,0:T(8,128)(2,1)S(1)}, u32[]{:S(2)}) copy-start(bf16[4,2,96,256]{3,2,1,0:T(8,128)(2,1)S(1)} %pad_maximum_fusion.refs_0_) | copy-start | bytes 1179652
  53.5 20.9 %collective-permute-start.7 = (bf16[4,2,96,256]{3,2,1,0:T(8,128)(2,1)S(1)}, bf16[4,2,96,256]{3,2,1,0:T(8,128)(2,1)}, u32[]{:S(2)}, u32[]{:S(2)}) collective-permute-start(bf16[4,2,96,256]{3,2,1,0:T(8,128)(2,1)S(1)} %pad_maximum_fusion.refs_0_), channel_id=1, source_target_pairs={{0,32},{4,36},{8,40},{12,44},{16,48},{20,52},{24,56},{28,60},{32,6... | collective-permute-start | bytes 1179656 | tf_op jit(solution)/shard_map/ppermute | solution.py:50
  54.1 20.3 %collective-permute-start.8 = (bf16[4,2,96,256]{3,2,1,0:T(8,128)(2,1)S(1)}, bf16[4,2,96,256]{3,2,1,0:T(8,128)(2,1)}, u32[]{:S(2)}, u32[]{:S(2)}) collective-permute-start(bf16[4,2,96,256]{3,2,1,0:T(8,128)(2,1)S(1)} %pad_maximum_fusion.refs_0_), channel_id=1, source_target_pairs={{0,64},{4,68},{8,72},{12,76},{16,80},{20,84},{24,88},{28,92},{32,9... | collective-permute-start | bytes 1179656 | tf_op jit(solution)/shard_map/ppermute | solution.py:50
  56.4 18.5 %collective-permute-start.9 = (bf16[4,2,96,256]{3,2,1,0:T(8,128)(2,1)S(1)}, bf16[4,2,96,256]{3,2,1,0:T(8,128)(2,1)}, u32[]{:S(2)}, u32[]{:S(2)}) collective-permute-start(bf16[4,2,96,256]{3,2,1,0:T(8,128)(2,1)S(1)} %pad_maximum_fusion.refs_0_), channel_id=1, source_target_pairs={{0,96},{4,100},{8,104},{12,108},{16,112},{20,116},{24,120},{28,124... | collective-permute-start | bytes 1179656 | tf_op jit(solution)/shard_map/ppermute | solution.py:50
  56.4 24.8 %collective-permute-start.10 = (bf16[4,2,96,256]{3,2,1,0:T(8,128)(2,1)S(1)}, bf16[4,2,96,256]{3,2,1,0:T(8,128)(2,1)}, u32[]{:S(2)}, u32[]{:S(2)}) collective-permute-start(bf16[4,2,96,256]{3,2,1,0:T(8,128)(2,1)S(1)} %pad_maximum_fusion.refs_0_), channel_id=1, source_target_pairs={{0,4},{4,0},{8,12},{12,8},{16,20},{20,16},{24,28},{28,24},{32,36},... | collective-permute-start | bytes 1179656 | tf_op jit(solution)/shard_map/ppermute | solution.py:50
  56.5 1.0 copy-start.2
  61.2 82.6 %all-to-all-start.1 = ((bf16[32,2,64,256]{3,2,1,0:T(8,128)(2,1)}), bf16[32,2,64,256]{3,2,1,0:T(8,128)(2,1)S(1)}, u32[]{:S(2)}, u32[]{:S(2)}) async-start(bf16[32,2,64,256]{3,2,1,0:T(8,128)(2,1)} %shard_map.61), calls=%async_computation.1 | async-start | bytes 4194304 | tf_op jit(solution)/shard_map/all_to_all | solution.py:394
  68.3 5.5 %copy-start.11 = (s32[4]{0:T(128)S(1)}, s32[4]{0:T(128)}, u32[]{:S(2)}) copy-start(s32[4]{0:T(128)} %and_select_fusion.10.rows_ref) | copy-start | bytes 52
  72.7 49.3 %collective-permute-start.16 = (bf16[256,2048]{1,0:T(8,128)(2,1)}, bf16[256,2048]{1,0:T(8,128)(2,1)}, u32[]{:S(2)}, u32[]{:S(2)}) collective-permute-start(bf16[256,2048]{1,0:T(8,128)(2,1)} %get-tuple-element.44), channel_id=1, source_target_pairs={{0,1},{1,2},{2,3},{3,0},{4,5},{5,6},{6,7},{7,4},{8,9},{9,10},{10,1... | collective-permute-start | bytes 3145736 | tf_op jit(solution)/shard_map/ppermute | solution.py:38
  74.4 10.0 %collective-permute-start.11 = (bf16[4,2,96,256]{3,2,1,0:T(8,128)(2,1)}, bf16[4,2,96,256]{3,2,1,0:T(8,128)(2,1)}, u32[]{:S(2)}, u32[]{:S(2)}) collective-permute-start(bf16[4,2,96,256]{3,2,1,0:T(8,128)(2,1)} %collective-permute-done.7.refs_1_), channel_id=1, source_target_pairs={{0,4},{4,0},{8,12},{12,8},{16,20},{20,16},{24,28},{28,24},{32,36},... | collective-permute-start | bytes 1179656 | tf_op jit(solution)/shard_map/ppermute | solution.py:50
  74.4 10.5 %collective-permute-start.12 = (bf16[4,2,96,256]{3,2,1,0:T(8,128)(2,1)}, bf16[4,2,96,256]{3,2,1,0:T(8,128)(2,1)}, u32[]{:S(2)}, u32[]{:S(2)}) collective-permute-start(bf16[4,2,96,256]{3,2,1,0:T(8,128)(2,1)} %collective-permute-done.8.refs_2_), channel_id=1, source_target_pairs={{0,4},{4,0},{8,12},{12,8},{16,20},{20,16},{24,28},{28,24},{32,36},... | collective-permute-start | bytes 1179656 | tf_op jit(solution)/shard_map/ppermute | solution.py:50
  75.0 10.0 %collective-permute-start.13 = (bf16[4,2,96,256]{3,2,1,0:T(8,128)(2,1)}, bf16[4,2,96,256]{3,2,1,0:T(8,128)(2,1)}, u32[]{:S(2)}, u32[]{:S(2)}) collective-permute-start(bf16[4,2,96,256]{3,2,1,0:T(8,128)(2,1)} %collective-permute-done.9.refs_3_), channel_id=1, source_target_pairs={{0,4},{4,0},{8,12},{12,8},{16,20},{20,16},{24,28},{28,24},{32,36},... | collective-permute-start | bytes 1179656 | tf_op jit(solution)/shard_map/ppermute | solution.py:50
  81.3 51.1 %collective-permute-start.15 = (bf16[256,2048]{1,0:T(8,128)(2,1)}, bf16[256,2048]{1,0:T(8,128)(2,1)S(1)}, u32[]{:S(2)}, u32[]{:S(2)}) collective-permute-start(bf16[256,2048]{1,0:T(8,128)(2,1)} %get-tuple-element.45), channel_id=1, source_target_pairs={{0,3},{1,0},{2,1},{3,2},{4,7},{5,4},{6,5},{7,6},{8,11},{9,8},{10,9... | collective-permute-start | bytes 3145736 | tf_op jit(solution)/shard_map/ppermute | solution.py:38
  84.4 4.7 %copy-start.13 = (bf16[2,1088,256]{2,1,0:T(8,128)(2,1)}, bf16[2,1088,256]{2,1,0:T(8,128)(2,1)S(1)}, u32[]{:S(2)}) copy-start(bf16[2,1088,256]{2,1,0:T(8,128)(2,1)S(1)} %constant_dynamic-update-slice_fusion.near_ref) | copy-start | bytes 3342340
  84.4 62.7 %collective-permute-start.3 = (bf16[256,2048]{1,0:T(8,128)(2,1)}, bf16[256,2048]{1,0:T(8,128)(2,1)S(1)}, u32[]{:S(2)}, u32[]{:S(2)}) collective-permute-start(bf16[256,2048]{1,0:T(8,128)(2,1)} %get-tuple-element.46), channel_id=1, source_target_pairs={{0,2},{1,3},{2,0},{3,1},{4,6},{5,7},{6,4},{7,5},{8,10},{9,11},{10,... | collective-permute-start | bytes 3145736 | tf_op jit(solution)/shard_map/ppermute | solution.py:38
  132.4 1.0 copy-start.16
  143.8 1.3 copy-start
  145.2 13.3 %collective-permute-start.17 = (bf16[2,2,64,256]{3,2,1,0:T(8,128)(2,1)S(1)}, bf16[2,2,64,256]{3,2,1,0:T(8,128)(2,1)S(1)}, u32[]{:S(2)}, u32[]{:S(2)}) collective-permute-start(bf16[2,2,64,256]{3,2,1,0:T(8,128)(2,1)S(1)} %pad_maximum_fusion.1), channel_id=1, source_target_pairs={{0,4},{4,8},{8,12},{12,16},{16,20},{20,24},{24,28},{28,32},{32,36}... | collective-permute-start | bytes 393224 | tf_op jit(solution)/shard_map/ppermute | solution.py:54
  147.2 1.0 copy-start.15
  158.5 0.7 copy-start.8

commit v2 on v1

v2 whole, which is shorter than its diff:
```python
import functools

import jax
import jax.numpy as jnp
from jax import lax
from jax.experimental import pallas as pl
from jax.experimental.pallas import tpu as pltpu
from jax.sharding import PartitionSpec as P

HQ = 64
KVH = 8
DH = 128
NVERT = 1024
GROUP = HQ // KVH
BLOCK = 64
CAP = 96
SLOTS = 8
NX, NY, NCORE, NTP = 4, 4, 2, 4
NCTX = NX * NY * NCORE
TOK = 1024
NBLK = TOK // BLOCK
KEPT = NVERT // NCTX
PIECE = TOK // NTP
LOG2_SCALE = 1.4426950408889634 * DH**-0.5
NEG = -1e30
BF16 = jnp.bfloat16
F32 = jnp.float32
VMEM_LIMIT = 60 * 2**20


def params():
    return pltpu.CompilerParams(vmem_limit_bytes=VMEM_LIMIT)


def dot_t(left, right):
    return lax.dot_general(left, right, (((1,), (1,)), ((), ())), preferred_element_type=F32)


def tp_shift(block, distance):
    return lax.ppermute(block, "tp", [(i, (i + distance) % NTP) for i in range(NTP)])


def ctx_route(block, move):
    pairs = []
    for x in range(NX):
        for y in range(NY):
            for core in range(NCORE):
                to_x, to_y, to_core = move(x, y, core)
                source = (x * NY + y) * NCORE + core
                target = ((to_x % NX) * NY + to_y % NY) * NCORE + to_core % NCORE
                pairs.append((source, target))
    return lax.ppermute(block, "ctx", pairs)


def ctx_next(block):
    return lax.ppermute(block, "ctx", [(i, i + 1) for i in range(NCTX - 1)])


def join_kernel(rows_ref, keys_ref, p0, p1, p2, p3, local_ref, send_ref):
    for distance, piece in enumerate((p0, p1, p2, p3)):
        first = pl.multiple_of(rows_ref[distance] * PIECE, PIECE)
        local_ref[:, pl.ds(first, PIECE), :] = piece[...]
    spots = lax.broadcasted_iota(jnp.int32, (NCTX * SLOTS, TOK), 1)
    chosen = []
    for head in range(2):
        pick = jnp.where(keys_ref[head] == spots, 1.0, 0.0).astype(BF16)
        rows = jnp.dot(pick, local_ref[head], preferred_element_type=F32)
        chosen.append(rows.reshape(NCTX, SLOTS, 2 * DH))
        for block in range(NBLK):
            send_ref[head * NBLK + block, :BLOCK, :] = local_ref[
                head, block * BLOCK : (block + 1) * BLOCK, :
            ]
    send_ref[:, BLOCK:, :] = jnp.concatenate(chosen, axis=1).astype(BF16)


def join_pieces(rows, keys, pieces):
    vmem = pl.BlockSpec(memory_space=pltpu.VMEM)
    return pl.pallas_call(
        join_kernel,
        in_specs=[pl.BlockSpec(memory_space=pltpu.SMEM)] + [vmem] * 5,
        out_specs=[vmem, vmem],
        out_shape=[
            jax.ShapeDtypeStruct((2, TOK, 2 * DH), BF16),
            jax.ShapeDtypeStruct((NCTX, BLOCK + 2 * SLOTS, 2 * DH), BF16),
        ],
        compiler_params=params(),
    )(rows, keys, *pieces)


def last_kernel(order_ref, *refs):
    for i in range(4):
        refs[4][i // 2, i % 2] = refs[i][0, 0, 0]


def last_blocks(orders, windows):
    def block(i):
        return pl.BlockSpec((1, 1, 1, BLOCK, 2 * DH), lambda g, s: (i // 2, s[i], i % 2, 0, 0))

    return pl.pallas_call(
        last_kernel,
        grid_spec=pltpu.PrefetchScalarGridSpec(
            num_scalar_prefetch=1,
            grid=(1,),
            in_specs=[block(i) for i in range(4)],
            out_specs=pl.BlockSpec((2, 2, BLOCK, 2 * DH), lambda g, s: (0, 0, 0, 0)),
        ),
        out_shape=jax.ShapeDtypeStruct((2, 2, BLOCK, 2 * DH), BF16),
        compiler_params=params(),
    )(orders, windows, windows, windows, windows)


def keep_kernel(first_ref, rows_ref, out_ref, total):
    total[...] = jnp.zeros_like(total)
    slot = lax.broadcasted_iota(jnp.int32, (SLOTS, 2 * DH), 0)
    for source in range(NCTX):
        for head in range(2):
            first = first_ref[head, source]
            rows = rows_ref[source].astype(F32)[head * SLOTS : (head + 1) * SLOTS]
            group = pl.multiple_of(first // SLOTS * SLOTS, SLOTS)
            late = slot >= lax.rem(first, SLOTS)
            total[head, pl.ds(group, SLOTS), :] += jnp.where(late, rows, 0.0)
            total[head, pl.ds(group + SLOTS, SLOTS), :] += jnp.where(late, 0.0, rows)
    out_ref[...] = total[:, :KEPT, :].astype(BF16)


def keep_verticals(firsts, table):
    return pl.pallas_call(
        keep_kernel,
        grid_spec=pltpu.PrefetchScalarGridSpec(
            num_scalar_prefetch=1,
            grid=(1,),
            in_specs=[pl.BlockSpec((NCTX, 2 * SLOTS, 2 * DH), lambda i, s: (0, BLOCK // 16, 0))],
            out_specs=pl.BlockSpec((2, KEPT, 2 * DH), lambda i, s: (0, 0, 0)),
            scratch_shapes=[pltpu.VMEM((2, KEPT + 2 * SLOTS, 2 * DH), F32)],
        ),
        out_shape=jax.ShapeDtypeStruct((2, KEPT, 2 * DH), BF16),
        compiler_params=params(),
    )(firsts, table)


def spread_kernel(shift_ref, table_ref, out_ref):
    group = pl.program_id(0)
    for i in range(8):
        for band in range(2):
            source = jnp.maximum(group * 8 + i - shift_ref[band], 0)
            out_ref[i, band] = table_ref[source, :BLOCK, :]


def spread_windows(shifts, table):
    return pl.pallas_call(
        spread_kernel,
        grid_spec=pltpu.PrefetchScalarGridSpec(
            num_scalar_prefetch=1,
            grid=(NCTX // 8,),
            in_specs=[pl.BlockSpec(table.shape, lambda g, s: (0, 0, 0))],
            out_specs=pl.BlockSpec((8, 2, BLOCK, 2 * DH), lambda g, s: (g, 0, 0, 0)),
        ),
        out_shape=jax.ShapeDtypeStruct((NCTX, 2, BLOCK, 2 * DH), BF16),
        compiler_params=params(),
    )(shifts, table)


def stack_heads(ref, first):
    return jnp.concatenate(
        [ref[first : first + BLOCK, g * DH : (g + 1) * DH] for g in range(GROUP)], axis=0
    )


def band_bias():
    row = lax.broadcasted_iota(jnp.int32, (BLOCK, 2 * BLOCK), 0)
    column = lax.broadcasted_iota(jnp.int32, (BLOCK, 2 * BLOCK), 1)
    distance = row - column + BLOCK
    return jnp.where((distance >= 0) & (distance < BLOCK), 0.0, NEG)


def masked(scores, bias):
    width = scores.shape[1]
    return (scores.reshape(GROUP, BLOCK, width) + bias[None]).reshape(GROUP * BLOCK, width)


def pack_levels(levels):
    lanes = lax.broadcasted_iota(jnp.int32, (BLOCK, DH), 1)
    packed = jnp.zeros((BLOCK, DH), F32)
    for g in range(GROUP):
        packed = jnp.where(lanes == g, levels[g * BLOCK : (g + 1) * BLOCK], packed)
    high = packed.astype(BF16)
    rest = packed - high.astype(F32)
    middle = rest.astype(BF16)
    low = (rest - middle.astype(F32)).astype(BF16)
    terms = high.astype(F32) + pltpu.roll(middle.astype(F32), GROUP, 1)
    return (terms + pltpu.roll(low.astype(F32), 2 * GROUP, 1)).astype(BF16)


def level_picks():
    lane = lax.broadcasted_iota(jnp.int32, (DH, GROUP * DH), 0)
    head = lax.broadcasted_iota(jnp.int32, (DH, GROUP * DH), 1) // DH
    pick = (lane < 3 * GROUP) & (lane % GROUP == head)
    return jnp.where(pick, 1.0, 0.0).astype(BF16)


def spread_levels(packed, picks):
    spread = jnp.dot(packed, picks, preferred_element_type=F32)
    return jnp.concatenate([spread[:, g * DH : (g + 1) * DH] for g in range(GROUP)], axis=0)


def near_kernel(rows_ref, *refs):
    q_refs, vert_refs = refs[:NTP], refs[NTP : NTP + 8]
    near_ref, spot_ref, mark_ref = refs[NTP + 8 : NTP + 11]
    out_ref, stat_ref, copy_ref, vert_ref, band_ref = refs[-5:]
    piece = pl.program_id(0)
    for i in range(NTP):

        @pl.when(piece == i)
        def _():
            copy_ref[0] = q_refs[i][...]

    @pl.when(piece == 0)
    def _():
        for number, part in enumerate(vert_refs):
            for i in range(4):
                first = (number * 4 + i) * KEPT
                vert_ref[first : first + KEPT, : 2 * DH] = part[i, 0]
        vert_ref[:, 2 * DH :] = jnp.ones((NVERT, DH), BF16)
        band_ref[:, : 2 * DH] = near_ref[0]
        band_ref[:, 2 * DH :] = jnp.ones((TOK + BLOCK, DH), BF16)

    bias = band_bias()

    def score(sub):
        block = rows_ref[piece] * (PIECE // BLOCK) + sub
        query = stack_heads(copy_ref.at[0], sub * BLOCK)
        first = pl.multiple_of(block * BLOCK, BLOCK)
        near = jnp.concatenate(
            [band_ref[pl.ds(first, BLOCK), :], band_ref[pl.ds(first + BLOCK, BLOCK), :]], axis=0
        )
        return block, near, dot_t(query, vert_ref[:, :DH]), dot_t(query, near[:, :DH])

    def weigh(block, near, vert_s, near_s):
        position = block * BLOCK + lax.broadcasted_iota(jnp.int32, (BLOCK, NVERT), 0)
        vert_s = masked(vert_s, jnp.where(spot_ref[0] <= position, 0.0, NEG))
        near_s = masked(near_s, bias + mark_ref[0, 0, pl.ds(block, 1), :])
        top = near_s
        for first in range(0, NVERT, DH):
            top = jnp.maximum(top, vert_s[:, first : first + DH])
        top = jnp.max(top, axis=-1, keepdims=True) * LOG2_SCALE
        vert_w = jnp.exp2(vert_s * LOG2_SCALE - top).astype(BF16)
        near_w = jnp.exp2(near_s * LOG2_SCALE - top).astype(BF16)
        return near, top, vert_w, near_w

    def finish(sub, near, top, vert_w, near_w):
        both = jnp.dot(vert_w, vert_ref[:, DH:], preferred_element_type=F32)
        both = both + jnp.dot(
            near_w, near[:, DH:], preferred_element_type=F32
        )
        total = both[:, DH:]
        out = (both[:, :DH] / total).astype(BF16)
        rows = slice(sub * BLOCK, (sub + 1) * BLOCK)
        stat_ref[0, rows, :] = pack_levels(top + jnp.log2(total))
        for g in range(GROUP):
            out_ref[0, rows, g * DH : (g + 1) * DH] = out[g * BLOCK : (g + 1) * BLOCK]

    subtiles = PIECE // BLOCK
    scored, weighed = score(0), None
    for sub in range(subtiles):
        following = score(sub + 1) if sub + 1 < subtiles else None
        current = weigh(*scored)
        if weighed is not None:
            finish(sub - 1, *weighed)
        scored, weighed = following, current
    finish(subtiles - 1, *weighed)


def near_attention(head, rows, queries, vert, near, spots, marks):
    wide = GROUP * DH
    here = lambda p, s: (p, 0, 0)
    return pl.pallas_call(
        near_kernel,
        grid_spec=pltpu.PrefetchScalarGridSpec(
            num_scalar_prefetch=1,
            grid=(NTP,),
            in_specs=[pl.BlockSpec((PIECE, wide), lambda p, s: (0, 0))] * NTP
            + [pl.BlockSpec((4, 1, KEPT, 2 * DH), lambda p, s: (0, head, 0, 0))] * 8
            + [
                pl.BlockSpec((1, TOK + BLOCK, 2 * DH), lambda p, s: (head, 0, 0)),
                pl.BlockSpec((1, 1, NVERT), lambda p, s: (head, 0, 0)),
                pl.BlockSpec((1, 1, NBLK, 2 * BLOCK), lambda p, s: (head, 0, 0, 0)),
            ],
            out_specs=[
                pl.BlockSpec((1, PIECE, wide), here),
                pl.BlockSpec((1, PIECE, DH), here),
                pl.BlockSpec((1, PIECE, wide), here),
            ],
            scratch_shapes=[
                pltpu.VMEM((NVERT, 3 * DH), BF16),
                pltpu.VMEM((TOK + BLOCK, 3 * DH), BF16),
            ],
        ),
        out_shape=[
            jax.ShapeDtypeStruct((NTP, PIECE, wide), BF16),
            jax.ShapeDtypeStruct((NTP, PIECE, DH), BF16),
            jax.ShapeDtypeStruct((NTP, PIECE, wide), BF16),
        ],
        cost_estimate=pl.CostEstimate(flops=10**9, bytes_accessed=2**20, transcendentals=0),
        compiler_params=params(),
    )(rows, *queries, *vert, near, spots, marks)


def far_kernel(
    rows_ref,
    order_ref,
    q_ref,
    prior_ref,
    stat_ref,
    far_ref,
    halo_ref,
    mark_ref,
    done_ref,
    out_ref,
    keys,
    picks,
):
    piece = pl.program_id(0)

    @pl.when(piece == 0)
    def _():
        picks[...] = level_picks()
        for band in range(2):
            keys[band, :BLOCK, :] = halo_ref[0, band]
            for block in range(NBLK):
                source = lax.rem(block + NBLK - order_ref[band], NBLK)
                keys[band, (block + 1) * BLOCK : (block + 2) * BLOCK, :] = far_ref[0, source, band]

    ones = jnp.ones((4 * BLOCK, DH), BF16)
    bias = band_bias()
    for sub in range(PIECE // BLOCK):
        block = rows_ref[piece] * (PIECE // BLOCK) + sub
        first = pl.multiple_of(block * BLOCK, BLOCK)
        rows = slice(sub * BLOCK, (sub + 1) * BLOCK)
        query = stack_heads(q_ref.at[0], sub * BLOCK)
        near = jnp.concatenate([keys[band, pl.ds(first, 2 * BLOCK), :] for band in range(2)], axis=0)
        scores = dot_t(query, near[:, :DH])
        halves = [
            masked(
                scores[:, band * DH : (band + 1) * DH],
                bias + mark_ref[0, 1 + band, pl.ds(block, 1), :],
            )
            for band in range(2)
        ]
        level = spread_levels(stat_ref[0, rows, :], picks[...])
        top = jnp.max(jnp.maximum(halves[0], halves[1]), axis=-1, keepdims=True) * LOG2_SCALE
        top = jnp.maximum(top, level)
        weight = jnp.concatenate(
            [jnp.exp2(half * LOG2_SCALE - top).astype(BF16) for half in halves], axis=1
        )
        both = jnp.dot(
            weight, jnp.concatenate([near[:, DH:], ones], axis=1), preferred_element_type=F32
        )
        prior_w = jnp.exp2(level - top)
        total = both[:, DH:] + prior_w
        prior = stack_heads(prior_ref.at[0], sub * BLOCK).astype(F32)
        out = ((both[:, :DH] + prior * prior_w) / total).astype(BF16)
        for g in range(GROUP):
            out_ref[rows, g * DH : (g + 1) * DH] = out[g * BLOCK : (g + 1) * BLOCK]


def far_attention(head, rows, orders, query, prior, stats, far, halo, marks, done):
    wide = GROUP * DH
    here = lambda p, s, o: (p, 0, 0)
    return pl.pallas_call(
        far_kernel,
        grid_spec=pltpu.PrefetchScalarGridSpec(
            num_scalar_prefetch=2,
            grid=(NTP,),
            in_specs=[
                pl.BlockSpec((1, PIECE, wide), here),
                pl.BlockSpec((1, PIECE, wide), here),
                pl.BlockSpec((1, PIECE, DH), here),
                pl.BlockSpec((1, NBLK, 2, BLOCK, 2 * DH), lambda p, s, o: (head, 0, 0, 0, 0)),
                pl.BlockSpec((1, 2, BLOCK, 2 * DH), lambda p, s, o: (head, 0, 0, 0)),
                pl.BlockSpec((1, 3, NBLK, 2 * BLOCK), lambda p, s, o: (head, 0, 0, 0)),
                pl.BlockSpec(memory_space=pl.ANY),
            ],
            out_specs=pl.BlockSpec((PIECE, wide), lambda p, s, o: (s[p], head)),
            scratch_shapes=[
                pltpu.VMEM((2, TOK + BLOCK, 2 * DH), BF16),
                pltpu.VMEM((DH, GROUP * DH), BF16),
            ],
        ),
        out_shape=jax.ShapeDtypeStruct((TOK, 2 * wide), BF16),
        input_output_aliases={8: 0},
        compiler_params=params(),
    )(rows, orders, query, prior, stats, far, halo, marks, done)


def attend_kernel(rows_ref, order_ref, *refs):
    q_refs, vert_refs = refs[:NTP], refs[NTP : NTP + 8]
    near_ref, far_ref, halo_ref, spot_ref, mark_ref = refs[NTP + 8 : NTP + 13]
    out_ref, query_ref, vert_ref, band_ref = refs[-4:]
    piece = pl.program_id(0)
    for i in range(NTP):

        @pl.when(piece == i)
        def _():
            query_ref[...] = q_refs[i][...]

    @pl.when(piece == 0)
    def _():
        for number, part in enumerate(vert_refs):
            for i in range(4):
                first = (number * 4 + i) * KEPT
                vert_ref[first : first + KEPT, : 2 * DH] = part[i, 0]
        vert_ref[:, 2 * DH :] = jnp.ones((NVERT, DH), BF16)
        for band in range(2):
            band_ref[band, :BLOCK, :] = halo_ref[0, band]
            for block in range(NBLK):
                source = lax.rem(block + NBLK - order_ref[band], NBLK)
                band_ref[band, (block + 1) * BLOCK : (block + 2) * BLOCK, :] = far_ref[
                    0, source, band
                ]

    ones = jnp.ones((6 * BLOCK, DH), BF16)
    bias = band_bias()

    def score(sub):
        block = rows_ref[piece] * (PIECE // BLOCK) + sub
        query = stack_heads(query_ref, sub * BLOCK)
        window = pl.ds(pl.multiple_of(block * BLOCK, BLOCK), 2 * BLOCK)
        band = jnp.concatenate(
            [near_ref[0, window, :], band_ref[0, window, :], band_ref[1, window, :]], axis=0
        )
        return block, band, dot_t(query, vert_ref[:, :DH]), dot_t(query, band[:, :DH])

    def weigh(block, band, vert_s, band_s):
        position = block * BLOCK + lax.broadcasted_iota(jnp.int32, (BLOCK, NVERT), 0)
        vert_s = masked(vert_s, jnp.where(spot_ref[0] <= position, 0.0, NEG))
        band_bias_s = jnp.concatenate(
            [bias + mark_ref[0, i, pl.ds(block, 1), :] for i in range(3)], axis=1
        )
        band_s = masked(band_s, band_bias_s)
        top = band_s[:, :DH]
        for first in range(DH, 3 * DH, DH):
            top = jnp.maximum(top, band_s[:, first : first + DH])
        for first in range(0, NVERT, DH):
            top = jnp.maximum(top, vert_s[:, first : first + DH])
        top = jnp.max(top, axis=-1, keepdims=True) * LOG2_SCALE
        vert_w = jnp.exp2(vert_s * LOG2_SCALE - top).astype(BF16)
        band_w = jnp.exp2(band_s * LOG2_SCALE - top).astype(BF16)
        return band, vert_w, band_w

    def finish(sub, band, vert_w, band_w):
        both = jnp.dot(vert_w, vert_ref[:, DH:], preferred_element_type=F32)
        both = both + jnp.dot(
            band_w, jnp.concatenate([band[:, DH:], ones], axis=1), preferred_element_type=F32
        )
        out = (both[:, :DH] / both[:, DH:]).astype(BF16)
        rows = slice(sub * BLOCK, (sub + 1) * BLOCK)
        for g in range(GROUP):
            out_ref[rows, g * DH : (g + 1) * DH] = out[g * BLOCK : (g + 1) * BLOCK]

    subtiles = PIECE // BLOCK
    scored, weighed = score(0), None
    for sub in range(subtiles):
        following = score(sub + 1) if sub + 1 < subtiles else None
        current = weigh(*scored)
        if weighed is not None:
            finish(sub - 1, *weighed)
        scored, weighed = following, current
    finish(subtiles - 1, *weighed)


def attend(head, rows, orders, queries, vert, near, far, halo, spots, marks):
    wide = GROUP * DH
    scored = TOK * GROUP * (NVERT + 6 * BLOCK)
    return pl.pallas_call(
        attend_kernel,
        grid_spec=pltpu.PrefetchScalarGridSpec(
            num_scalar_prefetch=2,
            grid=(NTP,),
            in_specs=[pl.BlockSpec((PIECE, wide), lambda p, s, o: (0, 0))] * NTP
            + [pl.BlockSpec((4, 1, KEPT, 2 * DH), lambda p, s, o: (0, head, 0, 0))] * 8
            + [
                pl.BlockSpec((1, TOK + BLOCK, 2 * DH), lambda p, s, o: (head, 0, 0)),
                pl.BlockSpec((1, NBLK, 2, BLOCK, 2 * DH), lambda p, s, o: (head, 0, 0, 0, 0)),
                pl.BlockSpec((1, 2, BLOCK, 2 * DH), lambda p, s, o: (head, 0, 0, 0)),
                pl.BlockSpec((1, 1, NVERT), lambda p, s, o: (head, 0, 0)),
                pl.BlockSpec((1, 3, NBLK, 2 * BLOCK), lambda p, s, o: (head, 0, 0, 0)),
            ],
            out_specs=pl.BlockSpec((PIECE, wide), lambda p, s, o: (s[p], head)),
            scratch_shapes=[
                pltpu.VMEM((PIECE, wide), BF16),
                pltpu.VMEM((NVERT, 3 * DH), BF16),
                pltpu.VMEM((2, TOK + BLOCK, 2 * DH), BF16),
            ],
        ),
        out_shape=jax.ShapeDtypeStruct((TOK, 2 * wide), BF16),
        cost_estimate=pl.CostEstimate(
            flops=scored * 4 * 2 * DH, bytes_accessed=6 * 2**20, transcendentals=scored
        ),
        compiler_params=params(),
    )(rows, orders, *queries, *vert, near, far, halo, spots, marks)


def shards(queries, key_rows, value_rows, vertical_keys, slash_offsets):
    tp = lax.axis_index("tp")
    ctx = lax.axis_index("ctx")
    base = ctx * TOK
    heads = vertical_keys.shape[0]
    hops = slash_offsets // BLOCK
    far_hops = hops[:, 1:]

    kv = jnp.concatenate(
        (key_rows.reshape(PIECE, KVH, DH), value_rows.reshape(PIECE, KVH, DH)), axis=2
    ).transpose(1, 0, 2)
    kv_pieces = []
    for distance in range(NTP):
        part = lax.dynamic_slice_in_dim(kv, heads * ((tp + distance) % NTP), heads, 0)
        kv_pieces.append(tp_shift(part, distance) if distance else part)

    ranked = vertical_keys.reshape(heads, KEPT // SLOTS, SLOTS, NCTX) - base
    own_keys = jnp.max(jnp.where((ranked >= 0) & (ranked < TOK), ranked, -1), axis=1)
    own_keys = own_keys.transpose(0, 2, 1).reshape(heads, NCTX * SLOTS, 1)
    devices = jnp.arange(NCTX, dtype=jnp.int32)
    started = jnp.sum(
        vertical_keys[:, None, :] < (devices * TOK)[None, :, None], axis=2, dtype=jnp.int32
    )
    kept_first = (started - ctx + NCTX - 1) // NCTX
    piece_rows = (tp + NTP - jnp.arange(NTP, dtype=jnp.int32)) % NTP

    x, y, core = ctx // 8, (ctx // 2) % 4, ctx % 2
    kept_spots = (vertical_keys - base).reshape(heads, KEPT, NX, NY, NCORE)
    for axis, place, size in ((2, x, NX), (3, y, NY), (4, core, NCORE)):
        turned = jnp.flip(kept_spots, axis)
        turned = jnp.concatenate((turned, turned), axis=axis)
        kept_spots = lax.dynamic_slice_in_dim(turned, size - 1 - place, size, axis)
    spots = kept_spots.transpose(0, 4, 2, 3, 1).reshape(heads, 1, NVERT)

    blocks = jnp.arange(-1, NBLK, dtype=jnp.int32) + ctx * NBLK - hops[:, :, None]
    blocks = blocks.reshape(heads, 3 * (NBLK + 1))
    high = (vertical_keys[:, :, None] // BLOCK == blocks[:, None, :]).astype(BF16)
    low = (vertical_keys[:, :, None] % BLOCK == jnp.arange(BLOCK)).astype(BF16)
    marked = jnp.einsum("hnb,hnl->hbl", high, low, preferred_element_type=F32)
    marks = jnp.where((marked > 0.5) | (blocks < 0)[:, :, None], NEG, 0.0)
    marks = marks.reshape(heads, 3, NBLK + 1, BLOCK)
    marks = jnp.concatenate((marks[:, :, :-1], marks[:, :, 1:]), axis=3)

    def query_parts(head):
        wide = GROUP * DH
        firsts = [wide * (heads * ((tp + step) % NTP) + head) for step in range(NTP)]
        return [lax.dynamic_slice_in_dim(queries, first, wide, 1) for first in firsts]

    def send_queries(parts):
        return parts[:1] + [tp_shift(parts[step], step) for step in (1, 2, 3)]

    first_parts, second_parts = query_parts(0), query_parts(1)
    received, first_parts, own_keys = lax.optimization_barrier(
        (kv_pieces[1:], first_parts, own_keys)
    )
    first_queries = send_queries(first_parts)
    local, sent = join_pieces(piece_rows, own_keys, kv_pieces[:1] + received)
    beside = ctx_next(local[:, TOK - BLOCK :])

    table = lax.all_to_all(sent, "ctx", split_axis=0, concat_axis=0, tiled=True)
    orders = far_hops % NBLK
    table, marks, spots, kept_first, orders = lax.optimization_barrier(
        (table, marks, spots, kept_first, orders)
    )

    kept = keep_verticals(kept_first, table)
    along_y = [kept] + [
        ctx_route(kept, lambda x, y, core, step=step: (x, y + step, core)) for step in (1, 2, 3)
    ]
    along_y, beside, first_queries, second_parts = lax.optimization_barrier(
        (along_y, beside, first_queries, second_parts)
    )
    second_queries = send_queries(second_parts)
    along_y = jnp.stack(along_y)
    along_x = [along_y] + [
        ctx_route(along_y, lambda x, y, core, step=step: (x + step, y, core)) for step in (1, 2, 3)
    ]
    across = [ctx_route(part, lambda x, y, core: (x, y, core + 1)) for part in along_x]
    shifts = (ctx % NBLK + jnp.where(ctx < NBLK, far_hops[0], far_hops[1])) // NBLK
    spread = spread_windows(shifts, table)
    near = jnp.concatenate((beside, local), axis=1)
    spread, across, near = lax.optimization_barrier((spread, across, near))
    vert = along_x + across

    windows = lax.all_to_all(
        spread, "ctx", split_axis=0, concat_axis=0, tiled=True
    ).reshape(heads, NBLK, 2, BLOCK, 2 * DH)
    prior = near_attention(0, piece_rows, first_queries, vert, near, spots, marks)
    windows, prior = lax.optimization_barrier((windows, prior))
    last = last_blocks((2 * NBLK - 1 - orders).reshape(-1) % NBLK, windows)
    halo = ctx_next(last)
    out = attend(
        1, piece_rows, orders[1], second_queries, vert, near, windows, halo, spots, marks
    )
    prior, stats, query = prior
    return far_attention(
        0, piece_rows, orders[0], query, prior, stats, windows, halo, marks, out
    )


def solution(mesh):
    in_specs = (
        P(("ctx", "tp"), None),
        P(("ctx", "tp"), None),
        P(("ctx", "tp"), None),
        P("tp", None),
        P("tp", None),
    )
    out_specs = P("ctx", "tp")
    return jax.shard_map(shards, mesh=mesh, in_specs=in_specs, out_specs=out_specs, check_vma=False)
```

time: 190 us -> 151 us (0.79); the launches traced: 187 us -> 151 us
  Pallas kernels: 79.7 us -> 60.6 us
  between operations: 10.5 us -> 0.52 us
  waiting for transfers between devices: 32.9 us -> 23 us
  starting transfers between devices: 38.1 us -> 42.8 us
  local copies, waits for them, and re-layouts: 18.6 us -> 15.2 us
  other arithmetic: 5.76 us -> 8.26 us
    pallas_call x4 -> x1, Pallas kernels: 41.6 us -> 19.1 us  [near_attention(): pl.pallas_call(near_kernel, grid_spec=pltpu.PrefetchScalarGridSpec(num_sc...]
    pallas_call x1 -> x3, Pallas kernels: 4.12 us -> 25.6 us  [the longest x1 20.6 us: attend(): pl.pallas_call(attend_kernel, grid_spec=pltpu.PrefetchScalarGridSpec(num_...]
    pallas_call x1, Pallas kernels: 27.9 us -> 9.15 us  [far_attention(): pl.pallas_call(far_kernel, grid_spec=pltpu.PrefetchScalarGridSpec(num_sca...]
    ppermute x6 -> x9, waiting for transfers between devices: 22.6 us -> 6.8 us  [tp_shift(): lax.ppermute(block, 'tp', [(i, (i + distance) % NTP) for i in range(NTP)])]
    ppermute x10, waiting for transfers between devices: 10.3 us -> 1.69 us  [ctx_route(): return lax.ppermute(block, 'ctx', pairs)]
    all_to_all x2, waiting for transfers between devices: 0.01 us -> 8.49 us  [the longest x1 6.74 us: shards(): table = lax.all_to_all(sent, 'ctx', split_axis=0, concat_axis=0, tiled=True)]
    ppermute x2, waiting for transfers between devices: 0.01 us -> 6.02 us  [ctx_next(): return lax.ppermute(block, 'ctx', [(i, i + 1) for i in range(NCTX - 1)])]
    ppermute x6 -> x9, starting transfers between devices: 10.3 us -> 16.2 us  [tp_shift(): lax.ppermute(block, 'tp', [(i, (i + distance) % NTP) for i in range(NTP)])]
  transfers between devices with their start and end apart: 20 -> 23, of which waited for: 2 -> 8; matrix products, arithmetic and copies ran while one was open for 9% -> 10% of each run, Pallas kernels for 26% -> 19%
where the time goes in v2:
time: 151 us
  Pallas kernels  60.6 us (40%)
  starting transfers between devices  42.8 us (28%)
  waiting for transfers between devices  23 us (15%)
  local copies, waits for them, and re-layouts  15.2 us (10%)
  other arithmetic  8.26 us (5%)
    pallas_call x1, Pallas kernels, attend(): pl.pallas_call(attend_kernel, grid_spec=pltpu.PrefetchScalarGridSpec(num_...  20.6 us
    pallas_call x1, Pallas kernels, near_attention(): pl.pallas_call(near_kernel, grid_spec=pltpu.PrefetchScalarGridSpec(num_sc...  19.1 us
    ppermute x9, starting transfers between devices, tp_shift(): lax.ppermute(block, 'tp', [(i, (i + distance) % NTP) for i in range(NTP)])  16.2 us
    pallas_call x1, Pallas kernels, far_attention(): pl.pallas_call(far_kernel, grid_spec=pltpu.PrefetchScalarGridSpec(num_sca...  9.15 us
    ppermute x10, starting transfers between devices, ctx_route(): return lax.ppermute(block, 'ctx', pairs)  8.56 us
    all_to_all x1, starting transfers between devices, shards(): table = lax.all_to_all(sent, 'ctx', split_axis=0, concat_axis=0, tiled=True)  7.74 us
    ppermute x9, waiting for transfers between devices, tp_shift(): lax.ppermute(block, 'tp', [(i, (i + distance) % NTP) for i in range(NTP)])  6.8 us
    all_to_all x1, waiting for transfers between devices, shards(): table = lax.all_to_all(sent, 'ctx', split_axis=0, concat_axis=0, tiled=True)  6.74 us
  transfers between devices with their start and end apart: 23, of which 8 were waited for; matrix products, arithmetic and copies ran while one was open for 10% of the time, Pallas kernels for 19%

profile of v2, /device:TPU:6, one launch (start us, length us, event | category | flops | bytes accessed | tf_op | source)
XLA Modules:
  0.0 150.6 jit_solution(12023375877922848125)
XLA Ops:
  0.0 1.3 copy.33
  2.1 0.8 fusion.4
  3.0 1.9 %collective-permute-start = (bf16[2,256,256]{2,1,0:T(8,128)(2,1)S(1)}, bf16[2,256,256]{2,1,0:T(8,128)(2,1)S(1)}, u32[]{:S(2)}, u32[]{:S(2)}) collective-permute-start(bf16[2,256,256]{2,1,0:T(8,128)(2,1)S(1)} %get-tuple-element.98), channel_id=1, source_target_pairs={{0,1},{1,2},{2,3},{3,0},{4,5},{5,6},{6,7},{7,4},{8,9},{9,10},{10,1... | collective-permute-start | bytes 786440 | tf_op jit(solution)/shard_map/ppermute | solution.py:40
  4.9 3.6 %collective-permute-start.1 = (bf16[2,256,256]{2,1,0:T(8,128)(2,1)S(1)}, bf16[2,256,256]{2,1,0:T(8,128)(2,1)S(1)}, u32[]{:S(2)}, u32[]{:S(2)}) collective-permute-start(bf16[2,256,256]{2,1,0:T(8,128)(2,1)S(1)} %get-tuple-element.99), channel_id=1, source_target_pairs={{0,2},{1,3},{2,0},{3,1},{4,6},{5,7},{6,4},{7,5},{8,10},{9,11},{10,... | collective-permute-start | bytes 786440 | tf_op jit(solution)/shard_map/ppermute | solution.py:40
  8.5 1.0 collective-permute-start.2
  9.9 4.2 %constant_dynamic-slice_fusion = (bf16[256,1024]{1,0:T(8,128)(2,1)}, bf16[256,1024]{1,0:T(8,128)(2,1)}, bf16[256,1024]{1,0:T(8,128)(2,1)}, bf16[256,1024]{1,0:T(...) fusion(bf16[256,8192]{1,0:T(8,128)(2,1)} %param.5, ...), kind=kLoop, calls=%fused_computation.44 | loop fusion | bytes 8388640 | tf_op jit(solution)/shard_map/dynamic_slice | solution.py:549
  14.7 0.7 reshape.108
  16.3 3.8 %collective-permute-done.1.p2 = bf16[2,256,256]{2,1,0:T(8,128)(2,1)S(1)} collective-permute-done((bf16[2,256,256]{2,1,0:T(8,128)(2,1)S(1)}, bf16[2,256,256]{2,1,0:T(8,128)(2,1)S(1)}, u32[]{:S(2)}, u32[]{:S(2)}) %collective-permute-start.1) | collective-permute-done | bytes 262176 | tf_op jit(solution)/shard_map/ppermute | solution.py:40
  20.1 0.9 copy.38.keys_ref
  21.0 2.9 %shard_map.55 = (bf16[2,1024,256]{2,1,0:T(8,128)(2,1)}, bf16[32,80,256]{2,1,0:T(8,128)(2,1)}) custom-call(s32[4]{0:T(128)} %and_select_fusion.7.rows_ref, s32[2,256,1]{2,1,0:T(8,128)} %copy.38.keys_ref, bf16[2,256,256]{2,1,0:T(8,128)(2,1)} %get-tuple-element.97.p0, bf16[2,256,256]{2,1,0:T(8,128)(2,1)} %copy-done.9, bf16[2,256,256]{2,1,0:T(8,128)(2,1)} %copy-done.10, ...), custom_call_target="tpu_custom_call" | custom-call | tf_op jit(solution)/shard_map/pallas_call | solution.py:78
  23.9 7.7 %all-to-all-start = ((bf16[32,80,256]{2,1,0:T(8,128)(2,1)}), bf16[32,80,256]{2,1,0:T(8,128)(2,1)S(1)}, u32[]{:S(2)}, u32[]{:S(2)}) async-start(bf16[32,80,256]{2,1,0:T(8,128)(2,1)} %get-tuple-element.50), calls=%async_computation | async-start | bytes 2621440 | tf_op jit(solution)/shard_map/all_to_all | solution.py:562
  32.1 1.1 collective-permute-start.7
  33.2 2.4 %collective-permute-start.8 = (bf16[256,1024]{1,0:T(8,128)(2,1)}, bf16[256,1024]{1,0:T(8,128)(2,1)S(1)}, u32[]{:S(2)}, u32[]{:S(2)}) collective-permute-start(bf16[256,1024]{1,0:T(8,128)(2,1)} %get-tuple-element.57), channel_id=1, source_target_pairs={{0,2},{1,3},{2,0},{3,1},{4,6},{5,7},{6,4},{7,5},{8,10},{9,11},{10,... | collective-permute-start | bytes 1572872 | tf_op jit(solution)/shard_map/ppermute | solution.py:40
  35.6 1.3 collective-permute-start.9
  37.6 0.7 reshape.109.refs_13_.refs_15_
  38.3 0.9 convert_reduce_fusion
  39.1 0.6 and_select_fusion.5.first_ref
  39.7 0.6 slice.32
  40.4 1.9 %collective-permute-start.6 = (bf16[2,64,256]{2,1,0:T(8,128)(2,1)}, bf16[2,64,256]{2,1,0:T(8,128)(2,1)}, u32[]{:S(2)}, u32[]{:S(2)}) collective-permute-start(bf16[2,64,256]{2,1,0:T(8,128)(2,1)} %slice.32), channel_id=1, source_target_pairs={{0,4},{4,8},{8,12},{12,16},{16,20},{20,24},{24,28},{28,32},{32,36}... | collective-permute-start | bytes 196616 | tf_op jit(solution)/shard_map/ppermute | solution.py:56
  42.3 0.7 pad_maximum_fusion.2.refs_14_.refs_16_.mark_ref
  43.0 6.7 %all-to-all-done.table_ref.rows_ref = bf16[32,80,256]{2,1,0:T(8,128)(2,1)S(1)} async-done(((bf16[32,80,256]{2,1,0:T(8,128)(2,1)}), bf16[32,80,256]{2,1,0:T(8,128)(2,1)S(1)}, u32[]{:S(2)}, u32[]{:S(2)}) %all-to-all-start) | async-done | bytes 1310752 | tf_op jit(solution)/shard_map/all_to_all | solution.py:562
  49.7 1.1 copy-done.1
  50.8 2.9 %shard_map.57 = bf16[2,32,256]{2,1,0:T(8,128)(2,1)} custom-call(s32[2,32]{1,0:T(2,128)} %and_select_fusion.5.first_ref, bf16[32,80,256]{2,1,0:T(8,128)(2,1)} %copy-done.1), custom_call_target="tpu_custom_call" | custom-call | tf_op jit(solution)/shard_map/pallas_call | solution.py:127
  53.7 1.2 collective-permute-start.5
  54.8 1.0 collective-permute-start.4
  55.9 0.7 collective-permute-start.3
  56.6 2.5 %collective-permute-done.8.refs_2_ = bf16[256,1024]{1,0:T(8,128)(2,1)S(1)} collective-permute-done((bf16[256,1024]{1,0:T(8,128)(2,1)}, bf16[256,1024]{1,0:T(8,128)(2,1)S(1)}, u32[]{:S(2)}, u32[]{:S(2)}) %collective-permute-start.8) | collective-permute-done | bytes 524320 | tf_op jit(solution)/shard_map/ppermute | solution.py:40
  59.5 1.2 collective-permute-done.4
  61.2 0.8 pad_maximum_fusion.1.refs_4_
  62.0 0.9 collective-permute-start.15
  62.8 2.9 %collective-permute-start.13 = (bf16[4,2,32,256]{3,2,1,0:T(8,128)(2,1)S(1)}, bf16[4,2,32,256]{3,2,1,0:T(8,128)(2,1)S(1)}, u32[]{:S(2)}, u32[]{:S(2)}) collective-permute-start(bf16[4,2,32,256]{3,2,1,0:T(8,128)(2,1)S(1)} %pad_maximum_fusion.1.refs_4_), channel_id=1, source_target_pairs={{0,64},{4,68},{8,72},{12,76},{16,80},{20,84},{24,88},{28,92},{32,9... | collective-permute-start | bytes 393224 | tf_op jit(solution)/shard_map/ppermute | solution.py:52
  65.7 0.9 collective-permute-start.11
  66.7 0.6 and_select_fusion.3.shift_ref
  67.3 3.8 %shard_map.56 = bf16[32,2,64,256]{3,2,1,0:T(8,128)(2,1)} custom-call(s32[2]{0:T(128)} %and_select_fusion.3.shift_ref, bf16[32,80,256]{2,1,0:T(8,128)(2,1)} %copy-done.1), custom_call_target="tpu_custom_call" | custom-call | tf_op jit(solution)/shard_map/pallas_call | solution.py:150
  72.1 1.9 %pad_maximum_fusion.refs_12_ = bf16[2,1088,256]{2,1,0:T(8,128)(2,1)} fusion(bf16[2,1024,256]{2,1,0:T(8,128)(2,1)S(1)} %copy-done.2, bf16[2,64,256]{2,1,0:T(8,128)(2,1)} %collective-permute-done.6), kind=kLoop, calls=%fused_computation.9 | loop fusion | flops 2228224 | bytes 2228224 | tf_op jit(solution)/shard_map/concatenate | solution.py:583
  75.4 6.3 %all-to-all-start.1 = ((bf16[32,2,64,256]{3,2,1,0:T(8,128)(2,1)}), bf16[32,2,64,256]{3,2,1,0:T(8,128)(2,1)S(1)}, u32[]{:S(2)}, u32[]{:S(2)}) async-start(bf16[32,2,64,256]{3,2,1,0:T(8,128)(2,1)} %shard_map.56), calls=%async_computation.1 | async-start | bytes 4194304 | tf_op jit(solution)/shard_map/all_to_all | solution.py:587
  81.9 1.1 collective-permute-start.18
  83.0 2.4 %collective-permute-start.19 = (bf16[256,1024]{1,0:T(8,128)(2,1)S(1)}, bf16[256,1024]{1,0:T(8,128)(2,1)}, u32[]{:S(2)}, u32[]{:S(2)}) collective-permute-start(bf16[256,1024]{1,0:T(8,128)(2,1)S(1)} %copy-done.8), channel_id=1, source_target_pairs={{0,2},{1,3},{2,0},{3,1},{4,6},{5,7},{6,4},{7,5},{8,10},{9,11},{10,... | collective-permute-start | bytes 1572872 | tf_op jit(solution)/shard_map/ppermute | solution.py:40
  85.4 1.3 collective-permute-start.20
  87.2 19.1 %shard_map.58 = (bf16[4,256,1024]{2,1,0:T(8,128)(2,1)}, bf16[4,256,128]{2,1,0:T(8,128)(2,1)}, bf16[4,256,1024]{2,1,0:T(8,128)(2,1)}) custom-call(s32[4]{0:T(128)} %and_select_fusion.7.rows_ref, bf16[256,1024]{1,0:T(8,128)(2,1)} %get-tuple-element.65.refs_0_, bf16[256,1024]{1,0:T(8,128)(2,1)} %copy-done.3, bf16[256,1024]{1,0:T(8,128)(2,1)} %copy-done.4, ...), custom_call_target="tpu_custom_call" | custom-call | flops 1000000000 | bytes 1048576 | tf_op jit(solution)/shard_map/pallas_call | solution.py:276
  106.4 1.7 %all-to-all-done.1 = bf16[32,2,64,256]{3,2,1,0:T(8,128)(2,1)S(1)} async-done(((bf16[32,2,64,256]{3,2,1,0:T(8,128)(2,1)}), bf16[32,2,64,256]{3,2,1,0:T(8,128)(2,1)S(1)}, u32[]{:S(2)}, u32[]{:S(2)}) %all-to-all-start.1) | async-done | bytes 2097184 | tf_op jit(solution)/shard_map/all_to_all | solution.py:587
  108.1 1.4 copy-done
  109.5 2.1 %shard_map.59 = bf16[2,2,64,256]{3,2,1,0:T(8,128)(2,1)} custom-call(s32[4]{0:T(128)} %and_select_fusion.2.order_ref, bf16[2,16,2,64,256]{4,3,2,1,0:T(8,128)(2,1)} %bitcast.27, bf16[2,16,2,64,256]{4,3,2,1,0:T(8,128)(2,1)} %bitcast.28, bf16[2,16,2,64,256]{4,3,2,1,0:T(8,128)(2,1)} %bitcast.29, bf16[2,16,2,64,256]{4,3,2,1,0:T(8,128)(2,1)} %bitcast.30), custom_call_target="tpu_custom_call" | custom-call | tf_op jit(solution)/shard_map/pallas_call | solution.py:99
  111.6 2.0 %collective-permute-start.17 = (bf16[2,2,64,256]{3,2,1,0:T(8,128)(2,1)}, bf16[2,2,64,256]{3,2,1,0:T(8,128)(2,1)S(1)}, u32[]{:S(2)}, u32[]{:S(2)}) collective-permute-start(bf16[2,2,64,256]{3,2,1,0:T(8,128)(2,1)} %shard_map.59), channel_id=1, source_target_pairs={{0,4},{4,8},{8,12},{12,16},{16,20},{20,24},{24,28},{28,32},{32,36}... | collective-permute-start | bytes 393224 | tf_op jit(solution)/shard_map/ppermute | solution.py:56
  114.2 6.0 %collective-permute-done.17.refs_14_.halo_ref = bf16[2,2,64,256]{3,2,1,0:T(8,128)(2,1)S(1)} collective-permute-done((bf16[2,2,64,256]{3,2,1,0:T(8,128)(2,1)}, bf16[2,2,64,256]{3,2,1,0:T(8,128)(2,1)S(1)}, u32[]{:S(2)}, u32[]{:S(2)}) %collective-permute-start.17) | collective-permute-done | bytes 131104 | tf_op jit(solution)/shard_map/ppermute | solution.py:56
  120.2 0.7 copy-done.12
  120.9 20.6 %shard_map.60.done_ref = bf16[1024,2048]{1,0:T(8,128)(2,1)} custom-call(s32[4]{0:T(128)} %and_select_fusion.7.rows_ref, s32[2]{0:T(128)} %get-tuple-element.106.order_ref, bf16[256,1024]{1,0:T(8,128)(2,1)} %get-tuple-element.83.refs_0_, bf16[256,1024]{1,0:T(8,128)(2,1)} %collective-permute-done.18.refs_1_, ...), custom_call_target="tpu_custom_call" | custom-call | flops 11811160064 | bytes 6291456 | tf_op jit(solution)/shard_map/pallas_call | solution.py:474
  141.4 9.2 %shard_map.61 = bf16[1024,2048]{1,0:T(8,128)(2,1)} custom-call(s32[4]{0:T(128)} %and_select_fusion.7.rows_ref, s32[2]{0:T(128)} %get-tuple-element.107.order_ref, bf16[4,256,1024]{2,1,0:T(8,128)(2,1)} %get-tuple-element.79.q_ref, bf16[4,256,1024]{2,1,0:T(8,128)(2,1)} %get-tuple-element.80.prior_ref, ...), custom_call_target="tpu_custom_call", output_to_operand_aliasing={{}: (8, {})} | custom-call | tf_op jit(solution)/shard_map/pallas_call | solution.py:369
  (99 shorter events, 8.0 us)
Async XLA Ops:
  0.0 1.6 %copy-start.6 = (bf16[256,1024]{1,0:T(8,128)(2,1)S(1)}, bf16[256,1024]{1,0:T(8,128)(2,1)}, u32[]{:S(2)}) copy-start(bf16[256,1024]{1,0:T(8,128)(2,1)} %param.7) | copy-start | bytes 1572868
  1.6 7.9 %copy-start.21 = (s32[2,3]{1,0:T(2,128)S(1)}, s32[2,3]{1,0:T(2,128)}, u32[]{:S(2)}) copy-start(s32[2,3]{1,0:T(2,128)} %param.9) | copy-start | bytes 76
  1.6 8.1 %copy-start.20 = (s32[2,1024]{1,0:T(2,128)S(1)}, s32[2,1024]{1,0:T(2,128)}, u32[]{:S(2)}) copy-start(s32[2,1024]{1,0:T(2,128)} %param.8) | copy-start | bytes 24580
  3.0 13.3 %collective-permute-start = (bf16[2,256,256]{2,1,0:T(8,128)(2,1)S(1)}, bf16[2,256,256]{2,1,0:T(8,128)(2,1)S(1)}, u32[]{:S(2)}, u32[]{:S(2)}) collective-permute-start(bf16[2,256,256]{2,1,0:T(8,128)(2,1)S(1)} %get-tuple-element.98), channel_id=1, source_target_pairs={{0,1},{1,2},{2,3},{3,0},{4,5},{5,6},{6,7},{7,4},{8,9},{9,10},{10,1... | collective-permute-start | bytes 786440 | tf_op jit(solution)/shard_map/ppermute | solution.py:40
  4.9 15.2 %collective-permute-start.1 = (bf16[2,256,256]{2,1,0:T(8,128)(2,1)S(1)}, bf16[2,256,256]{2,1,0:T(8,128)(2,1)S(1)}, u32[]{:S(2)}, u32[]{:S(2)}) collective-permute-start(bf16[2,256,256]{2,1,0:T(8,128)(2,1)S(1)} %get-tuple-element.99), channel_id=1, source_target_pairs={{0,2},{1,3},{2,0},{3,1},{4,6},{5,7},{6,4},{7,5},{8,10},{9,11},{10,... | collective-permute-start | bytes 786440 | tf_op jit(solution)/shard_map/ppermute | solution.py:40
  8.5 11.6 %collective-permute-start.2 = (bf16[2,256,256]{2,1,0:T(8,128)(2,1)S(1)}, bf16[2,256,256]{2,1,0:T(8,128)(2,1)S(1)}, u32[]{:S(2)}, u32[]{:S(2)}) collective-permute-start(bf16[2,256,256]{2,1,0:T(8,128)(2,1)S(1)} %get-tuple-element.100), channel_id=1, source_target_pairs={{0,3},{1,0},{2,1},{3,2},{4,7},{5,4},{6,5},{7,6},{8,11},{9,8},{10,9... | collective-permute-start | bytes 786440 | tf_op jit(solution)/shard_map/ppermute | solution.py:40
  16.3 4.8 %copy-start.9 = (bf16[2,256,256]{2,1,0:T(8,128)(2,1)}, bf16[2,256,256]{2,1,0:T(8,128)(2,1)S(1)}, u32[]{:S(2)}) copy-start(bf16[2,256,256]{2,1,0:T(8,128)(2,1)S(1)} %collective-permute-done.p1) | copy-start | bytes 786436
  20.1 0.9 copy-start.10
  20.1 0.9 copy-start.11
  23.9 15.8 %copy-start.2 = (bf16[2,1024,256]{2,1,0:T(8,128)(2,1)S(1)}, bf16[2,1024,256]{2,1,0:T(8,128)(2,1)}, u32[]{:S(2)}) copy-start(bf16[2,1024,256]{2,1,0:T(8,128)(2,1)} %get-tuple-element.54) | copy-start | bytes 3145732
  23.9 25.8 %all-to-all-start = ((bf16[32,80,256]{2,1,0:T(8,128)(2,1)}), bf16[32,80,256]{2,1,0:T(8,128)(2,1)S(1)}, u32[]{:S(2)}, u32[]{:S(2)}) async-start(bf16[32,80,256]{2,1,0:T(8,128)(2,1)} %get-tuple-element.50), calls=%async_computation | async-start | bytes 2621440 | tf_op jit(solution)/shard_map/all_to_all | solution.py:562
  32.1 23.8 %collective-permute-start.7 = (bf16[256,1024]{1,0:T(8,128)(2,1)}, bf16[256,1024]{1,0:T(8,128)(2,1)S(1)}, u32[]{:S(2)}, u32[]{:S(2)}) collective-permute-start(bf16[256,1024]{1,0:T(8,128)(2,1)} %get-tuple-element.56), channel_id=1, source_target_pairs={{0,1},{1,2},{2,3},{3,0},{4,5},{5,6},{6,7},{7,4},{8,9},{9,10},{10,1... | collective-permute-start | bytes 1572872 | tf_op jit(solution)/shard_map/ppermute | solution.py:40
  33.2 25.8 %collective-permute-start.8 = (bf16[256,1024]{1,0:T(8,128)(2,1)}, bf16[256,1024]{1,0:T(8,128)(2,1)S(1)}, u32[]{:S(2)}, u32[]{:S(2)}) collective-permute-start(bf16[256,1024]{1,0:T(8,128)(2,1)} %get-tuple-element.57), channel_id=1, source_target_pairs={{0,2},{1,3},{2,0},{3,1},{4,6},{5,7},{6,4},{7,5},{8,10},{9,11},{10,... | collective-permute-start | bytes 1572872 | tf_op jit(solution)/shard_map/ppermute | solution.py:40
  35.6 23.9 %collective-permute-start.9 = (bf16[256,1024]{1,0:T(8,128)(2,1)}, bf16[256,1024]{1,0:T(8,128)(2,1)}, u32[]{:S(2)}, u32[]{:S(2)}) collective-permute-start(bf16[256,1024]{1,0:T(8,128)(2,1)} %get-tuple-element.58), channel_id=1, source_target_pairs={{0,3},{1,0},{2,1},{3,2},{4,7},{5,4},{6,5},{7,6},{8,11},{9,8},{10,9... | collective-permute-start | bytes 1572872 | tf_op jit(solution)/shard_map/ppermute | solution.py:40
  40.4 14.5 %collective-permute-start.6 = (bf16[2,64,256]{2,1,0:T(8,128)(2,1)}, bf16[2,64,256]{2,1,0:T(8,128)(2,1)}, u32[]{:S(2)}, u32[]{:S(2)}) collective-permute-start(bf16[2,64,256]{2,1,0:T(8,128)(2,1)} %slice.32), channel_id=1, source_target_pairs={{0,4},{4,8},{8,12},{12,16},{16,20},{20,24},{24,28},{28,32},{32,36}... | collective-permute-start | bytes 196616 | tf_op jit(solution)/shard_map/ppermute | solution.py:56
  49.7 1.1 copy-start.1
  53.7 5.8 %collective-permute-start.5 = (bf16[2,32,256]{2,1,0:T(8,128)(2,1)}, bf16[2,32,256]{2,1,0:T(8,128)(2,1)S(1)}, u32[]{:S(2)}, u32[]{:S(2)}) collective-permute-start(bf16[2,32,256]{2,1,0:T(8,128)(2,1)} %shard_map.57), channel_id=1, source_target_pairs={{0,24},{4,28},{8,0},{12,4},{16,8},{20,12},{24,16},{28,20},{32,56},... | collective-permute-start | bytes 98312 | tf_op jit(solution)/shard_map/ppermute | solution.py:52
  54.8 5.9 %collective-permute-start.4 = (bf16[2,32,256]{2,1,0:T(8,128)(2,1)}, bf16[2,32,256]{2,1,0:T(8,128)(2,1)S(1)}, u32[]{:S(2)}, u32[]{:S(2)}) collective-permute-start(bf16[2,32,256]{2,1,0:T(8,128)(2,1)} %shard_map.57), channel_id=1, source_target_pairs={{0,16},{4,20},{8,24},{12,28},{16,0},{20,4},{24,8},{28,12},{32,48},... | collective-permute-start | bytes 98312 | tf_op jit(solution)/shard_map/ppermute | solution.py:52
  55.9 18.2 %copy-start.3 = (bf16[256,1024]{1,0:T(8,128)(2,1)}, bf16[256,1024]{1,0:T(8,128)(2,1)S(1)}, u32[]{:S(2)}) copy-start(bf16[256,1024]{1,0:T(8,128)(2,1)S(1)} %collective-permute-done.7.refs_1_) | copy-start | bytes 1572868
  55.9 5.3 %collective-permute-start.3 = (bf16[2,32,256]{2,1,0:T(8,128)(2,1)}, bf16[2,32,256]{2,1,0:T(8,128)(2,1)S(1)}, u32[]{:S(2)}, u32[]{:S(2)}) collective-permute-start(bf16[2,32,256]{2,1,0:T(8,128)(2,1)} %shard_map.57), channel_id=1, source_target_pairs={{0,8},{4,12},{8,16},{12,20},{16,24},{20,28},{24,0},{28,4},{32,40},... | collective-permute-start | bytes 98312 | tf_op jit(solution)/shard_map/ppermute | solution.py:52
  59.0 15.0 %copy-start.4 = (bf16[256,1024]{1,0:T(8,128)(2,1)}, bf16[256,1024]{1,0:T(8,128)(2,1)S(1)}, u32[]{:S(2)}) copy-start(bf16[256,1024]{1,0:T(8,128)(2,1)S(1)} %collective-permute-done.8.refs_2_) | copy-start | bytes 1572868
  62.0 12.1 %copy-start.5 = (bf16[4,2,32,256]{3,2,1,0:T(8,128)(2,1)}, bf16[4,2,32,256]{3,2,1,0:T(8,128)(2,1)S(1)}, u32[]{:S(2)}) copy-start(bf16[4,2,32,256]{3,2,1,0:T(8,128)(2,1)S(1)} %pad_maximum_fusion.1.refs_4_) | copy-start | bytes 393220
  62.0 9.1 %collective-permute-start.15 = (bf16[4,2,32,256]{3,2,1,0:T(8,128)(2,1)S(1)}, bf16[4,2,32,256]{3,2,1,0:T(8,128)(2,1)S(1)}, u32[]{:S(2)}, u32[]{:S(2)}) collective-permute-start(bf16[4,2,32,256]{3,2,1,0:T(8,128)(2,1)S(1)} %pad_maximum_fusion.1.refs_4_), channel_id=1, source_target_pairs={{0,96},{4,100},{8,104},{12,108},{16,112},{20,116},{24,120},{28,124... | collective-permute-start | bytes 393224 | tf_op jit(solution)/shard_map/ppermute | solution.py:52
  62.8 8.8 %collective-permute-start.13 = (bf16[4,2,32,256]{3,2,1,0:T(8,128)(2,1)S(1)}, bf16[4,2,32,256]{3,2,1,0:T(8,128)(2,1)S(1)}, u32[]{:S(2)}, u32[]{:S(2)}) collective-permute-start(bf16[4,2,32,256]{3,2,1,0:T(8,128)(2,1)S(1)} %pad_maximum_fusion.1.refs_4_), channel_id=1, source_target_pairs={{0,64},{4,68},{8,72},{12,76},{16,80},{20,84},{24,88},{28,92},{32,9... | collective-permute-start | bytes 393224 | tf_op jit(solution)/shard_map/ppermute | solution.py:52
  65.7 6.0 %collective-permute-start.11 = (bf16[4,2,32,256]{3,2,1,0:T(8,128)(2,1)S(1)}, bf16[4,2,32,256]{3,2,1,0:T(8,128)(2,1)S(1)}, u32[]{:S(2)}, u32[]{:S(2)}) collective-permute-start(bf16[4,2,32,256]{3,2,1,0:T(8,128)(2,1)S(1)} %pad_maximum_fusion.1.refs_4_), channel_id=1, source_target_pairs={{0,32},{4,36},{8,40},{12,44},{16,48},{20,52},{24,56},{28,60},{32,6... | collective-permute-start | bytes 393224 | tf_op jit(solution)/shard_map/ppermute | solution.py:52
  71.1 3.0 %collective-permute-start.10 = (bf16[4,2,32,256]{3,2,1,0:T(8,128)(2,1)S(1)}, bf16[4,2,32,256]{3,2,1,0:T(8,128)(2,1)S(1)}, u32[]{:S(2)}, u32[]{:S(2)}) collective-permute-start(bf16[4,2,32,256]{3,2,1,0:T(8,128)(2,1)S(1)} %pad_maximum_fusion.1.refs_4_), channel_id=1, source_target_pairs={{0,4},{4,0},{8,12},{12,8},{16,20},{20,16},{24,28},{28,24},{32,36},... | collective-permute-start | bytes 393224 | tf_op jit(solution)/shard_map/ppermute | solution.py:52
  71.1 4.3 %copy-start.13 = (bf16[4,2,32,256]{3,2,1,0:T(8,128)(2,1)}, bf16[4,2,32,256]{3,2,1,0:T(8,128)(2,1)S(1)}, u32[]{:S(2)}) copy-start(bf16[4,2,32,256]{3,2,1,0:T(8,128)(2,1)S(1)} %collective-permute-done.15.refs_7_) | copy-start | bytes 393220
  71.1 3.0 %collective-permute-start.16 = (bf16[4,2,32,256]{3,2,1,0:T(8,128)(2,1)S(1)}, bf16[4,2,32,256]{3,2,1,0:T(8,128)(2,1)S(1)}, u32[]{:S(2)}, u32[]{:S(2)}) collective-permute-start(bf16[4,2,32,256]{3,2,1,0:T(8,128)(2,1)S(1)} %collective-permute-done.15.refs_7_), channel_id=1, source_target_pairs={{0,4},{4,0},{8,12},{12,8},{16,20},{20,16},{24,28},{28,24},{32,36},... | collective-permute-start | bytes 393224 | tf_op jit(solution)/shard_map/ppermute | solution.py:52
  71.6 2.5 %copy-start.14 = (bf16[4,2,32,256]{3,2,1,0:T(8,128)(2,1)}, bf16[4,2,32,256]{3,2,1,0:T(8,128)(2,1)S(1)}, u32[]{:S(2)}) copy-start(bf16[4,2,32,256]{3,2,1,0:T(8,128)(2,1)S(1)} %collective-permute-done.13.refs_6_) | copy-start | bytes 393220
  71.6 2.5 %collective-permute-start.14 = (bf16[4,2,32,256]{3,2,1,0:T(8,128)(2,1)S(1)}, bf16[4,2,32,256]{3,2,1,0:T(8,128)(2,1)S(1)}, u32[]{:S(2)}, u32[]{:S(2)}) collective-permute-start(bf16[4,2,32,256]{3,2,1,0:T(8,128)(2,1)S(1)} %collective-permute-done.13.refs_6_), channel_id=1, source_target_pairs={{0,4},{4,0},{8,12},{12,8},{16,20},{20,16},{24,28},{28,24},{32,36},... | collective-permute-start | bytes 393224 | tf_op jit(solution)/shard_map/ppermute | solution.py:52
  71.7 2.4 %copy-start.15 = (bf16[4,2,32,256]{3,2,1,0:T(8,128)(2,1)}, bf16[4,2,32,256]{3,2,1,0:T(8,128)(2,1)S(1)}, u32[]{:S(2)}) copy-start(bf16[4,2,32,256]{3,2,1,0:T(8,128)(2,1)S(1)} %collective-permute-done.11.refs_5_) | copy-start | bytes 393220
  71.7 3.0 %collective-permute-start.12 = (bf16[4,2,32,256]{3,2,1,0:T(8,128)(2,1)S(1)}, bf16[4,2,32,256]{3,2,1,0:T(8,128)(2,1)S(1)}, u32[]{:S(2)}, u32[]{:S(2)}) collective-permute-start(bf16[4,2,32,256]{3,2,1,0:T(8,128)(2,1)S(1)} %collective-permute-done.11.refs_5_), channel_id=1, source_target_pairs={{0,4},{4,0},{8,12},{12,8},{16,20},{20,16},{24,28},{28,24},{32,36},... | collective-permute-start | bytes 393224 | tf_op jit(solution)/shard_map/ppermute | solution.py:52
  74.1 0.6 copy-start.16
  74.1 8.9 %copy-start.8 = (bf16[256,1024]{1,0:T(8,128)(2,1)S(1)}, bf16[256,1024]{1,0:T(8,128)(2,1)}, u32[]{:S(2)}) copy-start(bf16[256,1024]{1,0:T(8,128)(2,1)} %get-tuple-element.85) | copy-start | bytes 1572868
  74.1 11.3 %copy-start.7 = (bf16[256,1024]{1,0:T(8,128)(2,1)S(1)}, bf16[256,1024]{1,0:T(8,128)(2,1)}, u32[]{:S(2)}) copy-start(bf16[256,1024]{1,0:T(8,128)(2,1)} %get-tuple-element.86) | copy-start | bytes 1572868
  74.1 0.7 copy-start.17
  74.7 0.7 copy-start.18
  74.7 0.7 copy-start.19
  75.4 32.7 %all-to-all-start.1 = ((bf16[32,2,64,256]{3,2,1,0:T(8,128)(2,1)}), bf16[32,2,64,256]{3,2,1,0:T(8,128)(2,1)S(1)}, u32[]{:S(2)}, u32[]{:S(2)}) async-start(bf16[32,2,64,256]{3,2,1,0:T(8,128)(2,1)} %shard_map.56), calls=%async_computation.1 | async-start | bytes 4194304 | tf_op jit(solution)/shard_map/all_to_all | solution.py:587
  81.9 32.3 %collective-permute-start.18 = (bf16[256,1024]{1,0:T(8,128)(2,1)}, bf16[256,1024]{1,0:T(8,128)(2,1)}, u32[]{:S(2)}, u32[]{:S(2)}) collective-permute-start(bf16[256,1024]{1,0:T(8,128)(2,1)} %get-tuple-element.84), channel_id=1, source_target_pairs={{0,1},{1,2},{2,3},{3,0},{4,5},{5,6},{6,7},{7,4},{8,9},{9,10},{10,1... | collective-permute-start | bytes 1572872 | tf_op jit(solution)/shard_map/ppermute | solution.py:40
  83.0 31.2 %collective-permute-start.19 = (bf16[256,1024]{1,0:T(8,128)(2,1)S(1)}, bf16[256,1024]{1,0:T(8,128)(2,1)}, u32[]{:S(2)}, u32[]{:S(2)}) collective-permute-start(bf16[256,1024]{1,0:T(8,128)(2,1)S(1)} %copy-done.8), channel_id=1, source_target_pairs={{0,2},{1,3},{2,0},{3,1},{4,6},{5,7},{6,4},{7,5},{8,10},{9,11},{10,... | collective-permute-start | bytes 1572872 | tf_op jit(solution)/shard_map/ppermute | solution.py:40
  85.4 28.8 %collective-permute-start.20 = (bf16[256,1024]{1,0:T(8,128)(2,1)S(1)}, bf16[256,1024]{1,0:T(8,128)(2,1)}, u32[]{:S(2)}, u32[]{:S(2)}) collective-permute-start(bf16[256,1024]{1,0:T(8,128)(2,1)S(1)} %copy-done.7), channel_id=1, source_target_pairs={{0,3},{1,0},{2,1},{3,2},{4,7},{5,4},{6,5},{7,6},{8,11},{9,8},{10,9... | collective-permute-start | bytes 1572872 | tf_op jit(solution)/shard_map/ppermute | solution.py:40
  108.1 1.4 copy-start
  111.6 8.6 %collective-permute-start.17 = (bf16[2,2,64,256]{3,2,1,0:T(8,128)(2,1)}, bf16[2,2,64,256]{3,2,1,0:T(8,128)(2,1)S(1)}, u32[]{:S(2)}, u32[]{:S(2)}) collective-permute-start(bf16[2,2,64,256]{3,2,1,0:T(8,128)(2,1)} %shard_map.59), channel_id=1, source_target_pairs={{0,4},{4,8},{8,12},{12,16},{16,20},{20,24},{24,28},{28,32},{32,36}... | collective-permute-start | bytes 393224 | tf_op jit(solution)/shard_map/ppermute | solution.py:56
  120.2 0.7 copy-start.12

commit v3 on v2

--- a/solution.py
+++ b/solution.py
@@ -25,7 +25,7 @@
 NEG = -1e30
 BF16 = jnp.bfloat16
 F32 = jnp.float32
-VMEM_LIMIT = 60 * 2**20
+VMEM_LIMIT = 63 * 2**20 + 2**19
 
 
 def params():
@@ -205,7 +205,7 @@
 
 def near_kernel(rows_ref, *refs):
     q_refs, vert_refs = refs[:NTP], refs[NTP : NTP + 8]
-    near_ref, spot_ref, mark_ref = refs[NTP + 8 : NTP + 11]
+    beside_ref, local_ref, spot_ref, mark_ref = refs[NTP + 8 : NTP + 12]
     out_ref, stat_ref, copy_ref, vert_ref, band_ref = refs[-5:]
     piece = pl.program_id(0)
     for i in range(NTP):
@@ -221,7 +221,8 @@
                 first = (number * 4 + i) * KEPT
                 vert_ref[first : first + KEPT, : 2 * DH] = part[i, 0]
         vert_ref[:, 2 * DH :] = jnp.ones((NVERT, DH), BF16)
-        band_ref[:, : 2 * DH] = near_ref[0]
+        band_ref[:BLOCK, : 2 * DH] = beside_ref[0]
+        band_ref[BLOCK:, : 2 * DH] = local_ref[0]
         band_ref[:, 2 * DH :] = jnp.ones((TOK + BLOCK, DH), BF16)
 
     bias = band_bias()
@@ -270,7 +271,7 @@
     finish(subtiles - 1, *weighed)
 
 
-def near_attention(head, rows, queries, vert, near, spots, marks):
+def near_attention(head, rows, queries, vert, beside, local, spots, marks):
     wide = GROUP * DH
     here = lambda p, s: (p, 0, 0)
     return pl.pallas_call(
@@ -281,7 +282,8 @@
             in_specs=[pl.BlockSpec((PIECE, wide), lambda p, s: (0, 0))] * NTP
             + [pl.BlockSpec((4, 1, KEPT, 2 * DH), lambda p, s: (0, head, 0, 0))] * 8
             + [
-                pl.BlockSpec((1, TOK + BLOCK, 2 * DH), lambda p, s: (head, 0, 0)),
+                pl.BlockSpec((1, BLOCK, 2 * DH), lambda p, s: (head, 0, 0)),
+                pl.BlockSpec((1, TOK, 2 * DH), lambda p, s: (head, 0, 0)),
                 pl.BlockSpec((1, 1, NVERT), lambda p, s: (head, 0, 0)),
                 pl.BlockSpec((1, 1, NBLK, 2 * BLOCK), lambda p, s: (head, 0, 0, 0)),
             ],
@@ -302,7 +304,7 @@
         ],
         cost_estimate=pl.CostEstimate(flops=10**9, bytes_accessed=2**20, transcendentals=0),
         compiler_params=params(),
-    )(rows, *queries, *vert, near, spots, marks)
+    )(rows, *queries, *vert, beside, local, spots, marks)
 
 
 def far_kernel(
@@ -394,7 +396,7 @@
 
 def attend_kernel(rows_ref, order_ref, *refs):
     q_refs, vert_refs = refs[:NTP], refs[NTP : NTP + 8]
-    near_ref, far_ref, halo_ref, spot_ref, mark_ref = refs[NTP + 8 : NTP + 13]
+    beside_ref, local_ref, far_ref, halo_ref, spot_ref, mark_ref = refs[NTP + 8 : NTP + 14]
     out_ref, query_ref, vert_ref, band_ref = refs[-4:]
     piece = pl.program_id(0)
     for i in range(NTP):
@@ -410,6 +412,8 @@
                 first = (number * 4 + i) * KEPT
                 vert_ref[first : first + KEPT, : 2 * DH] = part[i, 0]
         vert_ref[:, 2 * DH :] = jnp.ones((NVERT, DH), BF16)
+        band_ref[2, :BLOCK, :] = beside_ref[0]
+        band_ref[2, BLOCK:, :] = local_ref[0]
         for band in range(2):
             band_ref[band, :BLOCK, :] = halo_ref[0, band]
             for block in range(NBLK):
@@ -426,7 +430,7 @@
         query = stack_heads(query_ref, sub * BLOCK)
         window = pl.ds(pl.multiple_of(block * BLOCK, BLOCK), 2 * BLOCK)
         band = jnp.concatenate(
-            [near_ref[0, window, :], band_ref[0, window, :], band_ref[1, window, :]], axis=0
+            [band_ref[2, window, :], band_ref[0, window, :], band_ref[1, window, :]], axis=0
         )
         return block, band, dot_t(query, vert_ref[:, :DH]), dot_t(query, band[:, :DH])
 
@@ -468,7 +472,7 @@
     finish(subtiles - 1, *weighed)
 
 
-def attend(head, rows, orders, queries, vert, near, far, halo, spots, marks):
+def attend(head, rows, orders, queries, vert, beside, local, far, halo, spots, marks):
     wide = GROUP * DH
     scored = TOK * GROUP * (NVERT + 6 * BLOCK)
     return pl.pallas_call(
@@ -479,7 +483,8 @@
             in_specs=[pl.BlockSpec((PIECE, wide), lambda p, s, o: (0, 0))] * NTP
             + [pl.BlockSpec((4, 1, KEPT, 2 * DH), lambda p, s, o: (0, head, 0, 0))] * 8
             + [
-                pl.BlockSpec((1, TOK + BLOCK, 2 * DH), lambda p, s, o: (head, 0, 0)),
+                pl.BlockSpec((1, BLOCK, 2 * DH), lambda p, s, o: (head, 0, 0)),
+                pl.BlockSpec((1, TOK, 2 * DH), lambda p, s, o: (head, 0, 0)),
                 pl.BlockSpec((1, NBLK, 2, BLOCK, 2 * DH), lambda p, s, o: (head, 0, 0, 0, 0)),
                 pl.BlockSpec((1, 2, BLOCK, 2 * DH), lambda p, s, o: (head, 0, 0, 0)),
                 pl.BlockSpec((1, 1, NVERT), lambda p, s, o: (head, 0, 0)),
@@ -489,7 +494,7 @@
             scratch_shapes=[
                 pltpu.VMEM((PIECE, wide), BF16),
                 pltpu.VMEM((NVERT, 3 * DH), BF16),
-                pltpu.VMEM((2, TOK + BLOCK, 2 * DH), BF16),
+                pltpu.VMEM((3, TOK + BLOCK, 2 * DH), BF16),
             ],
         ),
         out_shape=jax.ShapeDtypeStruct((TOK, 2 * wide), BF16),
@@ -497,7 +502,7 @@
             flops=scored * 4 * 2 * DH, bytes_accessed=6 * 2**20, transcendentals=scored
         ),
         compiler_params=params(),
-    )(rows, orders, *queries, *vert, near, far, halo, spots, marks)
+    )(rows, orders, *queries, *vert, beside, local, far, halo, spots, marks)
 
 
 def shards(queries, key_rows, value_rows, vertical_keys, slash_offsets):
@@ -552,9 +557,7 @@
         return parts[:1] + [tp_shift(parts[step], step) for step in (1, 2, 3)]
 
     first_parts, second_parts = query_parts(0), query_parts(1)
-    received, first_parts, own_keys = lax.optimization_barrier(
-        (kv_pieces[1:], first_parts, own_keys)
-    )
+    received, first_parts = lax.optimization_barrier((kv_pieces[1:], first_parts))
     first_queries = send_queries(first_parts)
     local, sent = join_pieces(piece_rows, own_keys, kv_pieces[:1] + received)
     beside = ctx_next(local[:, TOK - BLOCK :])
@@ -569,30 +572,39 @@
     along_y = [kept] + [
         ctx_route(kept, lambda x, y, core, step=step: (x, y + step, core)) for step in (1, 2, 3)
     ]
-    along_y, beside, first_queries, second_parts = lax.optimization_barrier(
-        (along_y, beside, first_queries, second_parts)
-    )
-    second_queries = send_queries(second_parts)
+    shifts = (ctx % NBLK + jnp.where(ctx < NBLK, far_hops[0], far_hops[1])) // NBLK
+    spread = spread_windows(shifts, table)
+    along_y, beside, spread = lax.optimization_barrier((along_y, beside, spread))
     along_y = jnp.stack(along_y)
     along_x = [along_y] + [
         ctx_route(along_y, lambda x, y, core, step=step: (x + step, y, core)) for step in (1, 2, 3)
     ]
+    spread, along_x, first_queries, second_parts = lax.optimization_barrier(
+        (spread, along_x, first_queries, second_parts)
+    )
     across = [ctx_route(part, lambda x, y, core: (x, y, core + 1)) for part in along_x]
-    shifts = (ctx % NBLK + jnp.where(ctx < NBLK, far_hops[0], far_hops[1])) // NBLK
-    spread = spread_windows(shifts, table)
-    near = jnp.concatenate((beside, local), axis=1)
-    spread, across, near = lax.optimization_barrier((spread, across, near))
+    second_queries = send_queries(second_parts)
     vert = along_x + across
 
     windows = lax.all_to_all(
         spread, "ctx", split_axis=0, concat_axis=0, tiled=True
     ).reshape(heads, NBLK, 2, BLOCK, 2 * DH)
-    prior = near_attention(0, piece_rows, first_queries, vert, near, spots, marks)
+    prior = near_attention(0, piece_rows, first_queries, vert, beside, local, spots, marks)
     windows, prior = lax.optimization_barrier((windows, prior))
     last = last_blocks((2 * NBLK - 1 - orders).reshape(-1) % NBLK, windows)
     halo = ctx_next(last)
     out = attend(
-        1, piece_rows, orders[1], second_queries, vert, near, windows, halo, spots, marks
+        1,
+        piece_rows,
+        orders[1],
+        second_queries,
+        vert,
+        beside,
+        local,
+        windows,
+        halo,
+        spots,
+        marks,
     )
     prior, stats, query = prior
     return far_attention(

time: 151 us -> 150 us (level)
  waiting for transfers between devices: 23 us -> 27.9 us
  other arithmetic: 8.26 us -> 4.97 us
  starting transfers between devices: 42.8 us -> 40.5 us
    ppermute x10, waiting for transfers between devices: 1.69 us -> 7.46 us  [ctx_route(): return lax.ppermute(block, 'ctx', pairs)]
    ppermute x9, starting transfers between devices: 16.2 us -> 12.6 us  [tp_shift(): lax.ppermute(block, 'tp', [(i, (i + distance) % NTP) for i in range(NTP)])]
    all_to_all x1, starting transfers between devices: 6.35 us -> 8.9 us  [shards(): lax.all_to_all(spread, 'ctx', split_axis=0, concat_axis=0, tiled=True)]
    ppermute x9, waiting for transfers between devices: 6.8 us -> 4.84 us  [tp_shift(): lax.ppermute(block, 'tp', [(i, (i + distance) % NTP) for i in range(NTP)])]
    concatenate x1 -> x0, other arithmetic: 1.9 us -> none  [shards(): near = jnp.concatenate((beside, local), axis=1)]
    unnamed x48 -> x42, local copies, waits for them, and re-layouts: 5.96 us -> 4.3 us
    all_to_all x1, waiting for transfers between devices: 6.74 us -> 8.35 us  [shards(): table = lax.all_to_all(sent, 'ctx', split_axis=0, concat_axis=0, tiled=True)]
  transfers between devices with their start and end apart: 23 -> 23, of which waited for: 8 -> 11; matrix products, arithmetic and copies ran while one was open for 10% -> 9% of each run, Pallas kernels for 19% -> 19%
where the time goes in v3:
time: 150 us; the launch traced here: 149 us
  Pallas kernels  60.8 us (41%)
  starting transfers between devices  40.5 us (27%)
  waiting for transfers between devices  27.9 us (19%)
  local copies, waits for them, and re-layouts  14.5 us (10%)
  other arithmetic  4.97 us (3%)
    pallas_call x1, Pallas kernels, attend(): pl.pallas_call(attend_kernel, grid_spec=pltpu.PrefetchScalarGridSpec(num_...  20.7 us
    pallas_call x1, Pallas kernels, near_attention(): pl.pallas_call(near_kernel, grid_spec=pltpu.PrefetchScalarGridSpec(num_sc...  19.2 us
    ppermute x9, starting transfers between devices, tp_shift(): lax.ppermute(block, 'tp', [(i, (i + distance) % NTP) for i in range(NTP)])  12.6 us
    pallas_call x1, Pallas kernels, far_attention(): pl.pallas_call(far_kernel, grid_spec=pltpu.PrefetchScalarGridSpec(num_sca...  9.15 us
    all_to_all x1, starting transfers between devices, shards(): lax.all_to_all(spread, 'ctx', split_axis=0, concat_axis=0, tiled=True)  8.9 us
    all_to_all x1, waiting for transfers between devices, shards(): table = lax.all_to_all(sent, 'ctx', split_axis=0, concat_axis=0, tiled=True)  8.35 us
    all_to_all x1, starting transfers between devices, shards(): table = lax.all_to_all(sent, 'ctx', split_axis=0, concat_axis=0, tiled=True)  7.78 us
    ppermute x10, waiting for transfers between devices, ctx_route(): return lax.ppermute(block, 'ctx', pairs)  7.46 us
  transfers between devices with their start and end apart: 23, of which 11 were waited for; matrix products, arithmetic and copies ran while one was open for 9% of the time, Pallas kernels for 19%

profile of v3, /device:TPU:6, one launch (start us, length us, event | category | flops | bytes accessed | tf_op | source)
XLA Modules:
  0.0 149.4 jit_solution(9488311987591062081)
XLA Ops:
  0.0 1.3 copy.34
  2.1 0.9 fusion.4
  3.0 4.0 %collective-permute-start.2 = (bf16[2,256,256]{2,1,0:T(8,128)(2,1)S(1)}, bf16[2,256,256]{2,1,0:T(8,128)(2,1)S(1)}, u32[]{:S(2)}, u32[]{:S(2)}) collective-permute-start(bf16[2,256,256]{2,1,0:T(8,128)(2,1)S(1)} %get-tuple-element.95), channel_id=1, source_target_pairs={{0,3},{1,0},{2,1},{3,2},{4,7},{5,4},{6,5},{7,6},{8,11},{9,8},{10,9... | collective-permute-start | bytes 786440 | tf_op jit(solution)/shard_map/ppermute | solution.py:40
  7.0 1.9 %collective-permute-start.1 = (bf16[2,256,256]{2,1,0:T(8,128)(2,1)S(1)}, bf16[2,256,256]{2,1,0:T(8,128)(2,1)S(1)}, u32[]{:S(2)}, u32[]{:S(2)}) collective-permute-start(bf16[2,256,256]{2,1,0:T(8,128)(2,1)S(1)} %get-tuple-element.98), channel_id=1, source_target_pairs={{0,2},{1,3},{2,0},{3,1},{4,6},{5,7},{6,4},{7,5},{8,10},{9,11},{10,... | collective-permute-start | bytes 786440 | tf_op jit(solution)/shard_map/ppermute | solution.py:40
  9.6 0.5 and_select_fusion.7.rows_ref
  10.1 1.5 reshape.108
  11.7 0.9 reshape.112.keys_ref
  12.5 4.2 %constant_dynamic-slice_fusion = (bf16[256,1024]{1,0:T(8,128)(2,1)}, bf16[256,1024]{1,0:T(8,128)(2,1)}, bf16[256,1024]{1,0:T(8,128)(2,1)}, bf16[256,1024]{1,0:T(...) fusion(bf16[256,8192]{1,0:T(8,128)(2,1)} %param.5, ...), kind=kLoop, calls=%fused_computation.43 | loop fusion | bytes 8388640 | tf_op jit(solution)/shard_map/dynamic_slice | solution.py:554
  16.8 1.4 collective-permute-done.2.p3
  18.2 3.4 %collective-permute-done.p1 = bf16[2,256,256]{2,1,0:T(8,128)(2,1)S(1)} collective-permute-done((bf16[2,256,256]{2,1,0:T(8,128)(2,1)S(1)}, bf16[2,256,256]{2,1,0:T(8,128)(2,1)S(1)}, u32[]{:S(2)}, u32[]{:S(2)}) %collective-permute-start) | collective-permute-done | bytes 262176 | tf_op jit(solution)/shard_map/ppermute | solution.py:40
  21.6 0.7 copy-done.4
  22.3 0.7 copy-done.5
  23.0 2.9 %shard_map.55 = (bf16[2,1024,256]{2,1,0:T(8,128)(2,1)}, bf16[32,80,256]{2,1,0:T(8,128)(2,1)}) custom-call(s32[4]{0:T(128)} %and_select_fusion.7.rows_ref, s32[2,256,1]{2,1,0:T(8,128)} %reshape.112.keys_ref, bf16[2,256,256]{2,1,0:T(8,128)(2,1)} %get-tuple-element.96.p0, bf16[2,256,256]{2,1,0:T(8,128)(2,1)} %copy-done.4, bf16[2,256,256]{2,1,0:T(8,128)(2,1)} %copy-done.5, ...), custom_call_target="tpu_custom_call" | custom-call | tf_op jit(solution)/shard_map/pallas_call | solution.py:78
  25.9 7.8 %all-to-all-start = ((bf16[32,80,256]{2,1,0:T(8,128)(2,1)}), bf16[32,80,256]{2,1,0:T(8,128)(2,1)}, u32[]{:S(2)}, u32[]{:S(2)}) async-start(bf16[32,80,256]{2,1,0:T(8,128)(2,1)} %get-tuple-element.48), calls=%async_computation | async-start | bytes 2621440 | tf_op jit(solution)/shard_map/all_to_all | solution.py:565
  34.3 0.7 pad_maximum_fusion.1.refs_15_.refs_17_.mark_ref
  35.2 0.7 and_select_fusion.4
  35.8 0.6 and_select_fusion.5.first_ref
  36.5 1.9 %collective-permute-start.11 = (bf16[256,1024]{1,0:T(8,128)(2,1)}, bf16[256,1024]{1,0:T(8,128)(2,1)}, u32[]{:S(2)}, u32[]{:S(2)}) collective-permute-start(bf16[256,1024]{1,0:T(8,128)(2,1)} %get-tuple-element.60), channel_id=1, source_target_pairs={{0,2},{1,3},{2,0},{3,1},{4,6},{5,7},{6,4},{7,5},{8,10},{9,11},{10,... | collective-permute-start | bytes 1572872 | tf_op jit(solution)/shard_map/ppermute | solution.py:40
  38.4 1.5 %collective-permute-start.12 = (bf16[256,1024]{1,0:T(8,128)(2,1)}, bf16[256,1024]{1,0:T(8,128)(2,1)}, u32[]{:S(2)}, u32[]{:S(2)}) collective-permute-start(bf16[256,1024]{1,0:T(8,128)(2,1)} %get-tuple-element.61), channel_id=1, source_target_pairs={{0,3},{1,0},{2,1},{3,2},{4,7},{5,4},{6,5},{7,6},{8,11},{9,8},{10,9... | collective-permute-start | bytes 1572872 | tf_op jit(solution)/shard_map/ppermute | solution.py:40
  39.9 0.8 slice.30
  40.8 1.9 %collective-permute-start.6 = (bf16[2,64,256]{2,1,0:T(8,128)(2,1)S(1)}, bf16[2,64,256]{2,1,0:T(8,128)(2,1)S(1)}, u32[]{:S(2)}, u32[]{:S(2)}) collective-permute-start(bf16[2,64,256]{2,1,0:T(8,128)(2,1)S(1)} %slice.30), channel_id=1, source_target_pairs={{0,4},{4,8},{8,12},{12,16},{16,20},{20,24},{24,28},{28,32},{32,36}... | collective-permute-start | bytes 196616 | tf_op jit(solution)/shard_map/ppermute | solution.py:56
  42.8 0.7 reshape.109.refs_14_.refs_16_
  43.5 8.3 %all-to-all-done.rows_ref.table_ref = bf16[32,80,256]{2,1,0:T(8,128)(2,1)} async-done(((bf16[32,80,256]{2,1,0:T(8,128)(2,1)}), bf16[32,80,256]{2,1,0:T(8,128)(2,1)}, u32[]{:S(2)}, u32[]{:S(2)}) %all-to-all-start) | async-done | bytes 1310752 | tf_op jit(solution)/shard_map/all_to_all | solution.py:565
  51.8 2.9 %shard_map.56 = bf16[2,32,256]{2,1,0:T(8,128)(2,1)} custom-call(s32[2,32]{1,0:T(2,128)} %and_select_fusion.5.first_ref, bf16[32,80,256]{2,1,0:T(8,128)(2,1)} %all-to-all-done.rows_ref.table_ref), custom_call_target="tpu_custom_call" | custom-call | tf_op jit(solution)/shard_map/pallas_call | solution.py:127
  54.7 1.2 collective-permute-start.5
  55.9 1.0 collective-permute-start.4
  56.9 1.9 %collective-permute-done.5 = bf16[2,32,256]{2,1,0:T(8,128)(2,1)S(1)} collective-permute-done((bf16[2,32,256]{2,1,0:T(8,128)(2,1)}, bf16[2,32,256]{2,1,0:T(8,128)(2,1)S(1)}, u32[]{:S(2)}, u32[]{:S(2)}) %collective-permute-start.5) | collective-permute-done | bytes 32800 | tf_op jit(solution)/shard_map/ppermute | solution.py:52
  58.9 0.7 and_select_fusion.3.shift_ref
  59.6 3.8 %shard_map.57 = bf16[32,2,64,256]{3,2,1,0:T(8,128)(2,1)} custom-call(s32[2]{0:T(128)} %and_select_fusion.3.shift_ref, bf16[32,80,256]{2,1,0:T(8,128)(2,1)} %all-to-all-done.rows_ref.table_ref), custom_call_target="tpu_custom_call" | custom-call | tf_op jit(solution)/shard_map/pallas_call | solution.py:150
  63.4 0.7 collective-permute-done.3
  64.2 0.7 collective-permute-start.9
  64.9 2.9 %collective-permute-start.8 = (bf16[4,2,32,256]{3,2,1,0:T(8,128)(2,1)S(1)}, bf16[4,2,32,256]{3,2,1,0:T(8,128)(2,1)S(1)}, u32[]{:S(2)}, u32[]{:S(2)}) collective-permute-start(bf16[4,2,32,256]{3,2,1,0:T(8,128)(2,1)S(1)} %pad_maximum_fusion.refs_4_), channel_id=1, source_target_pairs={{0,64},{4,68},{8,72},{12,76},{16,80},{20,84},{24,88},{28,92},{32,9... | collective-permute-start | bytes 393224 | tf_op jit(solution)/shard_map/ppermute | solution.py:52
  68.2 2.9 %collective-permute-done.9.refs_7_ = bf16[4,2,32,256]{3,2,1,0:T(8,128)(2,1)S(1)} collective-permute-done((bf16[4,2,32,256]{3,2,1,0:T(8,128)(2,1)S(1)}, bf16[4,2,32,256]{3,2,1,0:T(8,128)(2,1)S(1)}, u32[]{:S(2)}, u32[]{:S(2)}) %collective-permute-start.9) | collective-permute-done | bytes 131104 | tf_op jit(solution)/shard_map/ppermute | solution.py:52
  71.1 1.4 collective-permute-done.8.refs_6_
  72.8 8.9 %all-to-all-start.1 = ((bf16[32,2,64,256]{3,2,1,0:T(8,128)(2,1)}), bf16[32,2,64,256]{3,2,1,0:T(8,128)(2,1)}, u32[]{:S(2)}, u32[]{:S(2)}) async-start(bf16[32,2,64,256]{3,2,1,0:T(8,128)(2,1)} %shard_map.57), calls=%async_computation.1 | async-start | bytes 4194304 | tf_op jit(solution)/shard_map/all_to_all | solution.py:589
  83.1 1.6 %collective-permute-start.19 = (bf16[256,1024]{1,0:T(8,128)(2,1)}, bf16[256,1024]{1,0:T(8,128)(2,1)}, u32[]{:S(2)}, u32[]{:S(2)}) collective-permute-start(bf16[256,1024]{1,0:T(8,128)(2,1)} %get-tuple-element.83), channel_id=1, source_target_pairs={{0,2},{1,3},{2,0},{3,1},{4,6},{5,7},{6,4},{7,5},{8,10},{9,11},{10,... | collective-permute-start | bytes 1572872 | tf_op jit(solution)/shard_map/ppermute | solution.py:40
  84.7 1.7 %collective-permute-start.20 = (bf16[256,1024]{1,0:T(8,128)(2,1)}, bf16[256,1024]{1,0:T(8,128)(2,1)}, u32[]{:S(2)}, u32[]{:S(2)}) collective-permute-start(bf16[256,1024]{1,0:T(8,128)(2,1)} %get-tuple-element.84), channel_id=1, source_target_pairs={{0,3},{1,0},{2,1},{3,2},{4,7},{5,4},{6,5},{7,6},{8,11},{9,8},{10,9... | collective-permute-start | bytes 1572872 | tf_op jit(solution)/shard_map/ppermute | solution.py:40
  86.4 0.5 and_select_fusion.2.order_ref
  87.0 0.6 copy-done.12
  87.6 19.2 %shard_map.58 = (bf16[4,256,1024]{2,1,0:T(8,128)(2,1)}, bf16[4,256,128]{2,1,0:T(8,128)(2,1)}, bf16[4,256,1024]{2,1,0:T(8,128)(2,1)}) custom-call(s32[4]{0:T(128)} %and_select_fusion.7.rows_ref, bf16[256,1024]{1,0:T(8,128)(2,1)} %get-tuple-element.63.refs_0_, bf16[256,1024]{1,0:T(8,128)(2,1)} %collective-permute-done.10.refs_1_, ...), custom_call_target="tpu_custom_call" | custom-call | flops 1000000000 | bytes 1048576 | tf_op jit(solution)/shard_map/pallas_call | solution.py:277
  106.8 1.2 all-to-all-done.1
  108.1 2.3 %shard_map.59 = bf16[2,2,64,256]{3,2,1,0:T(8,128)(2,1)} custom-call(s32[4]{0:T(128)} %and_select_fusion.2.order_ref, bf16[2,16,2,64,256]{4,3,2,1,0:T(8,128)(2,1)} %bitcast.15.refs_0_.refs_1_.refs_2_.refs_3_.refs_14_.far_ref, bf16[2,16,2,64,256]{4,3,2,1,0:T(8,128)(2,1)} %bitcast.15.refs_0_.refs_1_.refs_2_.refs_3_.refs_14_.far_ref, ...), custom_call_target="tpu_custom_call" | custom-call | tf_op jit(solution)/shard_map/pallas_call | solution.py:99
  110.3 1.9 %collective-permute-start.17 = (bf16[2,2,64,256]{3,2,1,0:T(8,128)(2,1)}, bf16[2,2,64,256]{3,2,1,0:T(8,128)(2,1)S(1)}, u32[]{:S(2)}, u32[]{:S(2)}) collective-permute-start(bf16[2,2,64,256]{3,2,1,0:T(8,128)(2,1)} %shard_map.59), channel_id=1, source_target_pairs={{0,4},{4,8},{8,12},{12,16},{16,20},{20,24},{24,28},{28,32},{32,36}... | collective-permute-start | bytes 393224 | tf_op jit(solution)/shard_map/ppermute | solution.py:56
  112.3 0.6 slice_bitcast_fusion
  112.9 6.0 %collective-permute-done.17.refs_15_.halo_ref = bf16[2,2,64,256]{3,2,1,0:T(8,128)(2,1)S(1)} collective-permute-done((bf16[2,2,64,256]{3,2,1,0:T(8,128)(2,1)}, bf16[2,2,64,256]{3,2,1,0:T(8,128)(2,1)S(1)}, u32[]{:S(2)}, u32[]{:S(2)}) %collective-permute-start.17) | collective-permute-done | bytes 131104 | tf_op jit(solution)/shard_map/ppermute | solution.py:56
  118.9 0.6 copy-done.6
  119.6 20.7 %shard_map.60.done_ref = bf16[1024,2048]{1,0:T(8,128)(2,1)} custom-call(s32[4]{0:T(128)} %and_select_fusion.7.rows_ref, s32[2]{0:T(128)} %get-tuple-element.104.order_ref, bf16[256,1024]{1,0:T(8,128)(2,1)} %get-tuple-element.81.refs_0_, bf16[256,1024]{1,0:T(8,128)(2,1)} %collective-permute-done.18.refs_1_, ...), custom_call_target="tpu_custom_call" | custom-call | flops 11811160064 | bytes 6291456 | tf_op jit(solution)/shard_map/pallas_call | solution.py:478
  140.2 9.2 %shard_map.61 = bf16[1024,2048]{1,0:T(8,128)(2,1)} custom-call(s32[4]{0:T(128)} %and_select_fusion.7.rows_ref, s32[2]{0:T(128)} %get-tuple-element.105.order_ref, bf16[4,256,1024]{2,1,0:T(8,128)(2,1)} %get-tuple-element.77.q_ref, bf16[4,256,1024]{2,1,0:T(8,128)(2,1)} %get-tuple-element.78.prior_ref, ...), custom_call_target="tpu_custom_call", output_to_operand_aliasing={{}: (8, {})} | custom-call | tf_op jit(solution)/shard_map/pallas_call | solution.py:371
  (91 shorter events, 4.7 us)
Async XLA Ops:
  0.0 1.6 %copy-start.2 = (bf16[256,1024]{1,0:T(8,128)(2,1)S(1)}, bf16[256,1024]{1,0:T(8,128)(2,1)}, u32[]{:S(2)}) copy-start(bf16[256,1024]{1,0:T(8,128)(2,1)} %param.7) | copy-start | bytes 1572868
  1.6 7.3 %copy-start.18 = (s32[2,3]{1,0:T(2,128)S(1)}, s32[2,3]{1,0:T(2,128)}, u32[]{:S(2)}) copy-start(s32[2,3]{1,0:T(2,128)} %param.9) | copy-start | bytes 76
  1.6 7.5 %copy-start.15 = (s32[2,1024]{1,0:T(2,128)S(1)}, s32[2,1024]{1,0:T(2,128)}, u32[]{:S(2)}) copy-start(s32[2,1024]{1,0:T(2,128)} %param.8) | copy-start | bytes 24580
  3.0 15.2 %collective-permute-start.2 = (bf16[2,256,256]{2,1,0:T(8,128)(2,1)S(1)}, bf16[2,256,256]{2,1,0:T(8,128)(2,1)S(1)}, u32[]{:S(2)}, u32[]{:S(2)}) collective-permute-start(bf16[2,256,256]{2,1,0:T(8,128)(2,1)S(1)} %get-tuple-element.95), channel_id=1, source_target_pairs={{0,3},{1,0},{2,1},{3,2},{4,7},{5,4},{6,5},{7,6},{8,11},{9,8},{10,9... | collective-permute-start | bytes 786440 | tf_op jit(solution)/shard_map/ppermute | solution.py:40
  7.0 14.6 %collective-permute-start = (bf16[2,256,256]{2,1,0:T(8,128)(2,1)S(1)}, bf16[2,256,256]{2,1,0:T(8,128)(2,1)S(1)}, u32[]{:S(2)}, u32[]{:S(2)}) collective-permute-start(bf16[2,256,256]{2,1,0:T(8,128)(2,1)S(1)} %get-tuple-element.97), channel_id=1, source_target_pairs={{0,1},{1,2},{2,3},{3,0},{4,5},{5,6},{6,7},{7,4},{8,9},{9,10},{10,1... | collective-permute-start | bytes 786440 | tf_op jit(solution)/shard_map/ppermute | solution.py:40
  7.0 14.6 %collective-permute-start.1 = (bf16[2,256,256]{2,1,0:T(8,128)(2,1)S(1)}, bf16[2,256,256]{2,1,0:T(8,128)(2,1)S(1)}, u32[]{:S(2)}, u32[]{:S(2)}) collective-permute-start(bf16[2,256,256]{2,1,0:T(8,128)(2,1)S(1)} %get-tuple-element.98), channel_id=1, source_target_pairs={{0,2},{1,3},{2,0},{3,1},{4,6},{5,7},{6,4},{7,5},{8,10},{9,11},{10,... | collective-permute-start | bytes 786440 | tf_op jit(solution)/shard_map/ppermute | solution.py:40
  18.2 4.8 %copy-start.3 = (bf16[2,256,256]{2,1,0:T(8,128)(2,1)}, bf16[2,256,256]{2,1,0:T(8,128)(2,1)S(1)}, u32[]{:S(2)}) copy-start(bf16[2,256,256]{2,1,0:T(8,128)(2,1)S(1)} %collective-permute-done.2.p3) | copy-start | bytes 786436
  21.6 0.7 copy-start.4
  22.3 0.7 copy-start.5
  25.9 7.9 %copy-start = (s32[2,32,4,4,2]{4,3,2,1,0:T(4,128)S(1)}, s32[2,32,4,4,2]{4,3,2,1,0:T(4,128)}, u32[]{:S(2)}) copy-start(s32[2,32,4,4,2]{4,3,2,1,0:T(4,128)} %reshape.108) | copy-start | bytes 24580
  25.9 25.9 %all-to-all-start = ((bf16[32,80,256]{2,1,0:T(8,128)(2,1)}), bf16[32,80,256]{2,1,0:T(8,128)(2,1)}, u32[]{:S(2)}, u32[]{:S(2)}) async-start(bf16[32,80,256]{2,1,0:T(8,128)(2,1)} %get-tuple-element.48), calls=%async_computation | async-start | bytes 2621440 | tf_op jit(solution)/shard_map/all_to_all | solution.py:565
  36.4 31.4 %collective-permute-start.10 = (bf16[256,1024]{1,0:T(8,128)(2,1)}, bf16[256,1024]{1,0:T(8,128)(2,1)}, u32[]{:S(2)}, u32[]{:S(2)}) collective-permute-start(bf16[256,1024]{1,0:T(8,128)(2,1)} %get-tuple-element.59), channel_id=1, source_target_pairs={{0,1},{1,2},{2,3},{3,0},{4,5},{5,6},{6,7},{7,4},{8,9},{9,10},{10,1... | collective-permute-start | bytes 1572872 | tf_op jit(solution)/shard_map/ppermute | solution.py:40
  36.5 31.7 %collective-permute-start.11 = (bf16[256,1024]{1,0:T(8,128)(2,1)}, bf16[256,1024]{1,0:T(8,128)(2,1)}, u32[]{:S(2)}, u32[]{:S(2)}) collective-permute-start(bf16[256,1024]{1,0:T(8,128)(2,1)} %get-tuple-element.60), channel_id=1, source_target_pairs={{0,2},{1,3},{2,0},{3,1},{4,6},{5,7},{6,4},{7,5},{8,10},{9,11},{10,... | collective-permute-start | bytes 1572872 | tf_op jit(solution)/shard_map/ppermute | solution.py:40
  38.4 29.8 %collective-permute-start.12 = (bf16[256,1024]{1,0:T(8,128)(2,1)}, bf16[256,1024]{1,0:T(8,128)(2,1)}, u32[]{:S(2)}, u32[]{:S(2)}) collective-permute-start(bf16[256,1024]{1,0:T(8,128)(2,1)} %get-tuple-element.61), channel_id=1, source_target_pairs={{0,3},{1,0},{2,1},{3,2},{4,7},{5,4},{6,5},{7,6},{8,11},{9,8},{10,9... | collective-permute-start | bytes 1572872 | tf_op jit(solution)/shard_map/ppermute | solution.py:40
  40.8 15.1 %collective-permute-start.6 = (bf16[2,64,256]{2,1,0:T(8,128)(2,1)S(1)}, bf16[2,64,256]{2,1,0:T(8,128)(2,1)S(1)}, u32[]{:S(2)}, u32[]{:S(2)}) collective-permute-start(bf16[2,64,256]{2,1,0:T(8,128)(2,1)S(1)} %slice.30), channel_id=1, source_target_pairs={{0,4},{4,8},{8,12},{12,16},{16,20},{20,24},{24,28},{28,32},{32,36}... | collective-permute-start | bytes 196616 | tf_op jit(solution)/shard_map/ppermute | solution.py:56
  54.7 9.5 %copy-start.13 = (bf16[2,32,256]{2,1,0:T(8,128)(2,1)S(1)}, bf16[2,32,256]{2,1,0:T(8,128)(2,1)}, u32[]{:S(2)}) copy-start(bf16[2,32,256]{2,1,0:T(8,128)(2,1)} %shard_map.56) | copy-start | bytes 98308
  54.7 4.1 %collective-permute-start.5 = (bf16[2,32,256]{2,1,0:T(8,128)(2,1)}, bf16[2,32,256]{2,1,0:T(8,128)(2,1)S(1)}, u32[]{:S(2)}, u32[]{:S(2)}) collective-permute-start(bf16[2,32,256]{2,1,0:T(8,128)(2,1)} %shard_map.56), channel_id=1, source_target_pairs={{0,24},{4,28},{8,0},{12,4},{16,8},{20,12},{24,16},{28,20},{32,56},... | collective-permute-start | bytes 98312 | tf_op jit(solution)/shard_map/ppermute | solution.py:52
  55.9 16.9 %copy-start.14 = (bf16[2,64,256]{2,1,0:T(8,128)(2,1)}, bf16[2,64,256]{2,1,0:T(8,128)(2,1)S(1)}, u32[]{:S(2)}) copy-start(bf16[2,64,256]{2,1,0:T(8,128)(2,1)S(1)} %collective-permute-done.6.refs_12_) | copy-start | bytes 196612
  55.9 7.5 %collective-permute-start.4 = (bf16[2,32,256]{2,1,0:T(8,128)(2,1)}, bf16[2,32,256]{2,1,0:T(8,128)(2,1)S(1)}, u32[]{:S(2)}, u32[]{:S(2)}) collective-permute-start(bf16[2,32,256]{2,1,0:T(8,128)(2,1)} %shard_map.56), channel_id=1, source_target_pairs={{0,16},{4,20},{8,24},{12,28},{16,0},{20,4},{24,8},{28,12},{32,48},... | collective-permute-start | bytes 98312 | tf_op jit(solution)/shard_map/ppermute | solution.py:52
  58.8 5.3 %collective-permute-start.3 = (bf16[2,32,256]{2,1,0:T(8,128)(2,1)}, bf16[2,32,256]{2,1,0:T(8,128)(2,1)S(1)}, u32[]{:S(2)}, u32[]{:S(2)}) collective-permute-start(bf16[2,32,256]{2,1,0:T(8,128)(2,1)} %shard_map.56), channel_id=1, source_target_pairs={{0,8},{4,12},{8,16},{12,20},{16,24},{20,28},{24,0},{28,4},{32,40},... | collective-permute-start | bytes 98312 | tf_op jit(solution)/shard_map/ppermute | solution.py:52
  64.2 17.5 %copy-start.1 = (bf16[4,2,32,256]{3,2,1,0:T(8,128)(2,1)}, bf16[4,2,32,256]{3,2,1,0:T(8,128)(2,1)S(1)}, u32[]{:S(2)}) copy-start(bf16[4,2,32,256]{3,2,1,0:T(8,128)(2,1)S(1)} %pad_maximum_fusion.refs_4_) | copy-start | bytes 393220
  64.2 6.9 %collective-permute-start.9 = (bf16[4,2,32,256]{3,2,1,0:T(8,128)(2,1)S(1)}, bf16[4,2,32,256]{3,2,1,0:T(8,128)(2,1)S(1)}, u32[]{:S(2)}, u32[]{:S(2)}) collective-permute-start(bf16[4,2,32,256]{3,2,1,0:T(8,128)(2,1)S(1)} %pad_maximum_fusion.refs_4_), channel_id=1, source_target_pairs={{0,96},{4,100},{8,104},{12,108},{16,112},{20,116},{24,120},{28,124... | collective-permute-start | bytes 393224 | tf_op jit(solution)/shard_map/ppermute | solution.py:52
  64.9 7.6 %collective-permute-start.8 = (bf16[4,2,32,256]{3,2,1,0:T(8,128)(2,1)S(1)}, bf16[4,2,32,256]{3,2,1,0:T(8,128)(2,1)S(1)}, u32[]{:S(2)}, u32[]{:S(2)}) collective-permute-start(bf16[4,2,32,256]{3,2,1,0:T(8,128)(2,1)S(1)} %pad_maximum_fusion.refs_4_), channel_id=1, source_target_pairs={{0,64},{4,68},{8,72},{12,76},{16,80},{20,84},{24,88},{28,92},{32,9... | collective-permute-start | bytes 393224 | tf_op jit(solution)/shard_map/ppermute | solution.py:52
  67.8 5.0 %collective-permute-start.7 = (bf16[4,2,32,256]{3,2,1,0:T(8,128)(2,1)S(1)}, bf16[4,2,32,256]{3,2,1,0:T(8,128)(2,1)S(1)}, u32[]{:S(2)}, u32[]{:S(2)}) collective-permute-start(bf16[4,2,32,256]{3,2,1,0:T(8,128)(2,1)S(1)} %pad_maximum_fusion.refs_4_), channel_id=1, source_target_pairs={{0,32},{4,36},{8,40},{12,44},{16,48},{20,52},{24,56},{28,60},{32,6... | collective-permute-start | bytes 393224 | tf_op jit(solution)/shard_map/ppermute | solution.py:52
  71.1 11.4 %copy-start.7 = (bf16[4,2,32,256]{3,2,1,0:T(8,128)(2,1)}, bf16[4,2,32,256]{3,2,1,0:T(8,128)(2,1)S(1)}, u32[]{:S(2)}) copy-start(bf16[4,2,32,256]{3,2,1,0:T(8,128)(2,1)S(1)} %collective-permute-done.9.refs_7_) | copy-start | bytes 393220
  72.5 9.9 %copy-start.8 = (bf16[4,2,32,256]{3,2,1,0:T(8,128)(2,1)}, bf16[4,2,32,256]{3,2,1,0:T(8,128)(2,1)S(1)}, u32[]{:S(2)}) copy-start(bf16[4,2,32,256]{3,2,1,0:T(8,128)(2,1)S(1)} %collective-permute-done.8.refs_6_) | copy-start | bytes 393220
  72.8 9.2 %copy-start.9 = (bf16[4,2,32,256]{3,2,1,0:T(8,128)(2,1)}, bf16[4,2,32,256]{3,2,1,0:T(8,128)(2,1)S(1)}, u32[]{:S(2)}) copy-start(bf16[4,2,32,256]{3,2,1,0:T(8,128)(2,1)S(1)} %collective-permute-done.7.refs_5_) | copy-start | bytes 393220
  72.8 9.5 %copy-start.16 = (s32[2,2]{1,0:T(2,128)S(1)}, s32[2,2]{1,0:T(2,128)}, u32[]{:S(2)}) copy-start(s32[2,2]{1,0:T(2,128)} %and_select_fusion.4) | copy-start | bytes 52
  72.8 35.3 %all-to-all-start.1 = ((bf16[32,2,64,256]{3,2,1,0:T(8,128)(2,1)}), bf16[32,2,64,256]{3,2,1,0:T(8,128)(2,1)}, u32[]{:S(2)}, u32[]{:S(2)}) async-start(bf16[32,2,64,256]{3,2,1,0:T(8,128)(2,1)} %shard_map.57), calls=%async_computation.1 | async-start | bytes 4194304 | tf_op jit(solution)/shard_map/all_to_all | solution.py:589
  81.7 1.4 collective-permute-start.13
  81.9 2.8 %collective-permute-start.14 = (bf16[4,2,32,256]{3,2,1,0:T(8,128)(2,1)S(1)}, bf16[4,2,32,256]{3,2,1,0:T(8,128)(2,1)S(1)}, u32[]{:S(2)}, u32[]{:S(2)}) collective-permute-start(bf16[4,2,32,256]{3,2,1,0:T(8,128)(2,1)S(1)} %collective-permute-done.7.refs_5_), channel_id=1, source_target_pairs={{0,4},{4,0},{8,12},{12,8},{16,20},{20,16},{24,28},{28,24},{32,36},... | collective-permute-start | bytes 393224 | tf_op jit(solution)/shard_map/ppermute | solution.py:52
  82.4 4.6 %collective-permute-start.15 = (bf16[4,2,32,256]{3,2,1,0:T(8,128)(2,1)S(1)}, bf16[4,2,32,256]{3,2,1,0:T(8,128)(2,1)S(1)}, u32[]{:S(2)}, u32[]{:S(2)}) collective-permute-start(bf16[4,2,32,256]{3,2,1,0:T(8,128)(2,1)S(1)} %collective-permute-done.8.refs_6_), channel_id=1, source_target_pairs={{0,4},{4,0},{8,12},{12,8},{16,20},{20,16},{24,28},{28,24},{32,36},... | collective-permute-start | bytes 393224 | tf_op jit(solution)/shard_map/ppermute | solution.py:52
  82.5 5.1 %collective-permute-start.16 = (bf16[4,2,32,256]{3,2,1,0:T(8,128)(2,1)S(1)}, bf16[4,2,32,256]{3,2,1,0:T(8,128)(2,1)}, u32[]{:S(2)}, u32[]{:S(2)}) collective-permute-start(bf16[4,2,32,256]{3,2,1,0:T(8,128)(2,1)S(1)} %collective-permute-done.9.refs_7_), channel_id=1, source_target_pairs={{0,4},{4,0},{8,12},{12,8},{16,20},{20,16},{24,28},{28,24},{32,36},... | collective-permute-start | bytes 393224 | tf_op jit(solution)/shard_map/ppermute | solution.py:52
  82.9 30.0 %collective-permute-start.18 = (bf16[256,1024]{1,0:T(8,128)(2,1)}, bf16[256,1024]{1,0:T(8,128)(2,1)}, u32[]{:S(2)}, u32[]{:S(2)}) collective-permute-start(bf16[256,1024]{1,0:T(8,128)(2,1)} %get-tuple-element.82), channel_id=1, source_target_pairs={{0,1},{1,2},{2,3},{3,0},{4,5},{5,6},{6,7},{7,4},{8,9},{9,10},{10,1... | collective-permute-start | bytes 1572872 | tf_op jit(solution)/shard_map/ppermute | solution.py:40
  83.1 3.8 %copy-start.10 = (bf16[4,2,32,256]{3,2,1,0:T(8,128)(2,1)}, bf16[4,2,32,256]{3,2,1,0:T(8,128)(2,1)S(1)}, u32[]{:S(2)}) copy-start(bf16[4,2,32,256]{3,2,1,0:T(8,128)(2,1)S(1)} %collective-permute-done.13.refs_8_) | copy-start | bytes 393220
  83.1 29.8 %collective-permute-start.19 = (bf16[256,1024]{1,0:T(8,128)(2,1)}, bf16[256,1024]{1,0:T(8,128)(2,1)}, u32[]{:S(2)}, u32[]{:S(2)}) collective-permute-start(bf16[256,1024]{1,0:T(8,128)(2,1)} %get-tuple-element.83), channel_id=1, source_target_pairs={{0,2},{1,3},{2,0},{3,1},{4,6},{5,7},{6,4},{7,5},{8,10},{9,11},{10,... | collective-permute-start | bytes 1572872 | tf_op jit(solution)/shard_map/ppermute | solution.py:40
  84.7 2.3 %copy-start.11 = (bf16[4,2,32,256]{3,2,1,0:T(8,128)(2,1)}, bf16[4,2,32,256]{3,2,1,0:T(8,128)(2,1)S(1)}, u32[]{:S(2)}) copy-start(bf16[4,2,32,256]{3,2,1,0:T(8,128)(2,1)S(1)} %collective-permute-done.14.refs_9_) | copy-start | bytes 393220
  84.7 28.2 %collective-permute-start.20 = (bf16[256,1024]{1,0:T(8,128)(2,1)}, bf16[256,1024]{1,0:T(8,128)(2,1)}, u32[]{:S(2)}, u32[]{:S(2)}) collective-permute-start(bf16[256,1024]{1,0:T(8,128)(2,1)} %get-tuple-element.84), channel_id=1, source_target_pairs={{0,3},{1,0},{2,1},{3,2},{4,7},{5,4},{6,5},{7,6},{8,11},{9,8},{10,9... | collective-permute-start | bytes 1572872 | tf_op jit(solution)/shard_map/ppermute | solution.py:40
  87.0 0.7 copy-start.12
  108.1 4.2 %copy-start.17 = (s32[2,2]{1,0:T(2,128)S(1)}, s32[2,2]{1,0:T(2,128)}, u32[]{:S(2)}) copy-start(s32[2,2]{1,0:T(2,128)} %and_select_fusion.4) | copy-start | bytes 52
  110.3 8.6 %collective-permute-start.17 = (bf16[2,2,64,256]{3,2,1,0:T(8,128)(2,1)}, bf16[2,2,64,256]{3,2,1,0:T(8,128)(2,1)S(1)}, u32[]{:S(2)}, u32[]{:S(2)}) collective-permute-start(bf16[2,2,64,256]{3,2,1,0:T(8,128)(2,1)} %shard_map.59), channel_id=1, source_target_pairs={{0,4},{4,8},{8,12},{12,16},{16,20},{20,24},{24,28},{28,32},{32,36}... | collective-permute-start | bytes 393224 | tf_op jit(solution)/shard_map/ppermute | solution.py:56
  118.9 0.7 copy-start.6

commit v4 on v3

--- a/solution.py
+++ b/solution.py
@@ -307,7 +307,8 @@
     )(rows, *queries, *vert, beside, local, spots, marks)
 
 
-def far_kernel(
+def far_step(
+    piece,
     rows_ref,
     order_ref,
     q_ref,
@@ -316,13 +317,10 @@
     far_ref,
     halo_ref,
     mark_ref,
-    done_ref,
     out_ref,
     keys,
     picks,
 ):
-    piece = pl.program_id(0)
-
     @pl.when(piece == 0)
     def _():
         picks[...] = level_picks()
@@ -365,40 +363,23 @@
             out_ref[rows, g * DH : (g + 1) * DH] = out[g * BLOCK : (g + 1) * BLOCK]
 
 
-def far_attention(head, rows, orders, query, prior, stats, far, halo, marks, done):
-    wide = GROUP * DH
-    here = lambda p, s, o: (p, 0, 0)
-    return pl.pallas_call(
-        far_kernel,
-        grid_spec=pltpu.PrefetchScalarGridSpec(
-            num_scalar_prefetch=2,
-            grid=(NTP,),
-            in_specs=[
-                pl.BlockSpec((1, PIECE, wide), here),
-                pl.BlockSpec((1, PIECE, wide), here),
-                pl.BlockSpec((1, PIECE, DH), here),
-                pl.BlockSpec((1, NBLK, 2, BLOCK, 2 * DH), lambda p, s, o: (head, 0, 0, 0, 0)),
-                pl.BlockSpec((1, 2, BLOCK, 2 * DH), lambda p, s, o: (head, 0, 0, 0)),
-                pl.BlockSpec((1, 3, NBLK, 2 * BLOCK), lambda p, s, o: (head, 0, 0, 0)),
-                pl.BlockSpec(memory_space=pl.ANY),
-            ],
-            out_specs=pl.BlockSpec((PIECE, wide), lambda p, s, o: (s[p], head)),
-            scratch_shapes=[
-                pltpu.VMEM((2, TOK + BLOCK, 2 * DH), BF16),
-                pltpu.VMEM((DH, GROUP * DH), BF16),
-            ],
-        ),
-        out_shape=jax.ShapeDtypeStruct((TOK, 2 * wide), BF16),
-        input_output_aliases={8: 0},
-        compiler_params=params(),
-    )(rows, orders, query, prior, stats, far, halo, marks, done)
-
-
-def attend_kernel(rows_ref, order_ref, *refs):
-    q_refs, vert_refs = refs[:NTP], refs[NTP : NTP + 8]
-    beside_ref, local_ref, far_ref, halo_ref, spot_ref, mark_ref = refs[NTP + 8 : NTP + 14]
-    out_ref, query_ref, vert_ref, band_ref = refs[-4:]
-    piece = pl.program_id(0)
+def attend_step(
+    piece,
+    rows_ref,
+    order_ref,
+    q_refs,
+    vert_refs,
+    beside_ref,
+    local_ref,
+    far_ref,
+    halo_ref,
+    spot_ref,
+    mark_ref,
+    out_ref,
+    query_ref,
+    vert_ref,
+    band_ref,
+):
     for i in range(NTP):
 
         @pl.when(piece == i)
@@ -417,7 +398,7 @@
         for band in range(2):
             band_ref[band, :BLOCK, :] = halo_ref[0, band]
             for block in range(NBLK):
-                source = lax.rem(block + NBLK - order_ref[band], NBLK)
+                source = lax.rem(block + NBLK - order_ref[2 + band], NBLK)
                 band_ref[band, (block + 1) * BLOCK : (block + 2) * BLOCK, :] = far_ref[
                     0, source, band
                 ]
@@ -472,37 +453,99 @@
     finish(subtiles - 1, *weighed)
 
 
-def attend(head, rows, orders, queries, vert, beside, local, far, halo, spots, marks):
+def tail_kernel(rows_ref, order_ref, *refs):
+    q_refs, vert_refs = refs[:NTP], refs[NTP : NTP + 8]
+    beside_ref, local_ref, far_ref, halo_ref, spot_ref, mark_ref = refs[NTP + 8 : NTP + 14]
+    q_ref, prior_ref, stat_ref, out_ref = refs[NTP + 14 : NTP + 18]
+    query_ref, vert_ref, band_ref, picks = refs[-4:]
+    step = pl.program_id(0)
+
+    @pl.when(step < NTP)
+    def _():
+        attend_step(
+            step,
+            rows_ref,
+            order_ref,
+            q_refs,
+            vert_refs,
+            beside_ref,
+            local_ref,
+            far_ref,
+            halo_ref,
+            spot_ref,
+            mark_ref,
+            out_ref,
+            query_ref,
+            vert_ref,
+            band_ref,
+        )
+
+    @pl.when(step >= NTP)
+    def _():
+        far_step(
+            step - NTP,
+            rows_ref,
+            order_ref,
+            q_ref,
+            prior_ref,
+            stat_ref,
+            far_ref,
+            halo_ref,
+            mark_ref,
+            out_ref,
+            band_ref,
+            picks,
+        )
+
+
+def tail_attention(rows, orders, queries, vert, beside, local, far, halo, spots, marks, first):
+    prior, stats, query = first
     wide = GROUP * DH
-    scored = TOK * GROUP * (NVERT + 6 * BLOCK)
+    head = lambda p: 1 - p // NTP
+    later = lambda p, s, o: (jnp.maximum(p - NTP, 0), 0, 0)
     return pl.pallas_call(
-        attend_kernel,
+        tail_kernel,
         grid_spec=pltpu.PrefetchScalarGridSpec(
             num_scalar_prefetch=2,
-            grid=(NTP,),
+            grid=(2 * NTP,),
             in_specs=[pl.BlockSpec((PIECE, wide), lambda p, s, o: (0, 0))] * NTP
-            + [pl.BlockSpec((4, 1, KEPT, 2 * DH), lambda p, s, o: (0, head, 0, 0))] * 8
+            + [pl.BlockSpec((4, 1, KEPT, 2 * DH), lambda p, s, o: (0, 1, 0, 0))] * 8
             + [
-                pl.BlockSpec((1, BLOCK, 2 * DH), lambda p, s, o: (head, 0, 0)),
-                pl.BlockSpec((1, TOK, 2 * DH), lambda p, s, o: (head, 0, 0)),
-                pl.BlockSpec((1, NBLK, 2, BLOCK, 2 * DH), lambda p, s, o: (head, 0, 0, 0, 0)),
-                pl.BlockSpec((1, 2, BLOCK, 2 * DH), lambda p, s, o: (head, 0, 0, 0)),
-                pl.BlockSpec((1, 1, NVERT), lambda p, s, o: (head, 0, 0)),
-                pl.BlockSpec((1, 3, NBLK, 2 * BLOCK), lambda p, s, o: (head, 0, 0, 0)),
+                pl.BlockSpec((1, BLOCK, 2 * DH), lambda p, s, o: (1, 0, 0)),
+                pl.BlockSpec((1, TOK, 2 * DH), lambda p, s, o: (1, 0, 0)),
+                pl.BlockSpec((1, NBLK, 2, BLOCK, 2 * DH), lambda p, s, o: (head(p), 0, 0, 0, 0)),
+                pl.BlockSpec((1, 2, BLOCK, 2 * DH), lambda p, s, o: (head(p), 0, 0, 0)),
+                pl.BlockSpec((1, 1, NVERT), lambda p, s, o: (1, 0, 0)),
+                pl.BlockSpec((1, 3, NBLK, 2 * BLOCK), lambda p, s, o: (head(p), 0, 0, 0)),
+                pl.BlockSpec((1, PIECE, wide), later),
+                pl.BlockSpec((1, PIECE, wide), later),
+                pl.BlockSpec((1, PIECE, DH), later),
             ],
-            out_specs=pl.BlockSpec((PIECE, wide), lambda p, s, o: (s[p], head)),
+            out_specs=pl.BlockSpec((PIECE, wide), lambda p, s, o: (s[p % NTP], head(p))),
             scratch_shapes=[
                 pltpu.VMEM((PIECE, wide), BF16),
                 pltpu.VMEM((NVERT, 3 * DH), BF16),
                 pltpu.VMEM((3, TOK + BLOCK, 2 * DH), BF16),
+                pltpu.VMEM((DH, GROUP * DH), BF16),
             ],
         ),
         out_shape=jax.ShapeDtypeStruct((TOK, 2 * wide), BF16),
-        cost_estimate=pl.CostEstimate(
-            flops=scored * 4 * 2 * DH, bytes_accessed=6 * 2**20, transcendentals=scored
-        ),
         compiler_params=params(),
-    )(rows, orders, *queries, *vert, beside, local, far, halo, spots, marks)
+    )(
+        rows,
+        orders,
+        *queries,
+        *vert,
+        beside,
+        local,
+        far,
+        halo,
+        spots,
+        marks,
+        query,
+        prior,
+        stats,
+    )
 
 
 def shards(queries, key_rows, value_rows, vertical_keys, slash_offsets):
@@ -593,10 +636,9 @@
     windows, prior = lax.optimization_barrier((windows, prior))
     last = last_blocks((2 * NBLK - 1 - orders).reshape(-1) % NBLK, windows)
     halo = ctx_next(last)
-    out = attend(
-        1,
+    return tail_attention(
         piece_rows,
-        orders[1],
+        orders.reshape(-1),
         second_queries,
         vert,
         beside,
@@ -605,10 +647,7 @@
         halo,
         spots,
         marks,
-    )
-    prior, stats, query = prior
-    return far_attention(
-        0, piece_rows, orders[0], query, prior, stats, windows, halo, marks, out
+        prior,
     )
 
 

time: 150 us -> 148 us (0.987)
  Pallas kernels: 60.8 us -> 58.7 us
    pallas_call x2 -> x1, Pallas kernels: 29.8 us -> 27.8 us  [tail_attention(): pl.pallas_call(tail_kernel, grid_spec=pltpu.PrefetchScalarGridSpec(num_sc...]
    unnamed x42 -> x38, local copies, waits for them, and re-layouts: 4.3 us -> 3.74 us
where the time goes in v4:
time: 148 us; the launch traced here: 147 us
  Pallas kernels  58.7 us (40%)
  starting transfers between devices  40.7 us (28%)
  waiting for transfers between devices  28.7 us (19%)
  local copies, waits for them, and re-layouts  14 us (9%)
  other arithmetic  4.43 us (3%)
    pallas_call x1, Pallas kernels, tail_attention(): pl.pallas_call(tail_kernel, grid_spec=pltpu.PrefetchScalarGridSpec(num_sc...  27.8 us
    pallas_call x1, Pallas kernels, near_attention(): pl.pallas_call(near_kernel, grid_spec=pltpu.PrefetchScalarGridSpec(num_sc...  19.2 us
    ppermute x9, starting transfers between devices, tp_shift(): lax.ppermute(block, 'tp', [(i, (i + distance) % NTP) for i in range(NTP)])  12.5 us
    all_to_all x1, waiting for transfers between devices, shards(): table = lax.all_to_all(sent, 'ctx', split_axis=0, concat_axis=0, tiled=True)  8.93 us
    all_to_all x1, starting transfers between devices, shards(): lax.all_to_all(spread, 'ctx', split_axis=0, concat_axis=0, tiled=True)  8.84 us
    ppermute x10, waiting for transfers between devices, ctx_route(): return lax.ppermute(block, 'ctx', pairs)  7.83 us
    all_to_all x1, starting transfers between devices, shards(): table = lax.all_to_all(sent, 'ctx', split_axis=0, concat_axis=0, tiled=True)  7.78 us
    ppermute x10, starting transfers between devices, ctx_route(): return lax.ppermute(block, 'ctx', pairs)  7.69 us
  transfers between devices with their start and end apart: 23, of which 11 were waited for; matrix products, arithmetic and copies ran while one was open for 9% of the time, Pallas kernels for 19%

profile of v4, /device:TPU:6, one launch (start us, length us, event | category | flops | bytes accessed | tf_op | source)
XLA Modules:
  0.0 147.3 jit_solution(2494981414581006504)
XLA Ops:
  0.0 1.3 copy.33
  2.1 0.8 fusion.4
  3.0 4.0 %collective-permute-start.2 = (bf16[2,256,256]{2,1,0:T(8,128)(2,1)S(1)}, bf16[2,256,256]{2,1,0:T(8,128)(2,1)S(1)}, u32[]{:S(2)}, u32[]{:S(2)}) collective-permute-start(bf16[2,256,256]{2,1,0:T(8,128)(2,1)S(1)} %get-tuple-element.95), channel_id=1, source_target_pairs={{0,3},{1,0},{2,1},{3,2},{4,7},{5,4},{6,5},{7,6},{8,11},{9,8},{10,9... | collective-permute-start | bytes 786440 | tf_op jit(solution)/shard_map/ppermute | solution.py:40
  7.0 1.9 %collective-permute-start.1 = (bf16[2,256,256]{2,1,0:T(8,128)(2,1)S(1)}, bf16[2,256,256]{2,1,0:T(8,128)(2,1)S(1)}, u32[]{:S(2)}, u32[]{:S(2)}) collective-permute-start(bf16[2,256,256]{2,1,0:T(8,128)(2,1)S(1)} %get-tuple-element.98), channel_id=1, source_target_pairs={{0,2},{1,3},{2,0},{3,1},{4,6},{5,7},{6,4},{7,5},{8,10},{9,11},{10,... | collective-permute-start | bytes 786440 | tf_op jit(solution)/shard_map/ppermute | solution.py:40
  9.6 0.6 and_select_fusion.7.rows_ref
  10.2 1.5 reshape.111
  11.7 0.8 reshape.116.keys_ref
  12.6 4.3 %constant_dynamic-slice_fusion = (bf16[256,1024]{1,0:T(8,128)(2,1)}, bf16[256,1024]{1,0:T(8,128)(2,1)}, bf16[256,1024]{1,0:T(8,128)(2,1)}, bf16[256,1024]{1,0:T(...) fusion(bf16[256,8192]{1,0:T(8,128)(2,1)} %param.5, ...), kind=kLoop, calls=%fused_computation.43 | loop fusion | bytes 8388640 | tf_op jit(solution)/shard_map/dynamic_slice | solution.py:597
  16.9 1.3 collective-permute-done.2.p3
  18.2 3.4 %collective-permute-done.p1 = bf16[2,256,256]{2,1,0:T(8,128)(2,1)S(1)} collective-permute-done((bf16[2,256,256]{2,1,0:T(8,128)(2,1)S(1)}, bf16[2,256,256]{2,1,0:T(8,128)(2,1)S(1)}, u32[]{:S(2)}, u32[]{:S(2)}) %collective-permute-start) | collective-permute-done | bytes 262176 | tf_op jit(solution)/shard_map/ppermute | solution.py:40
  21.6 0.7 copy-done.11
  22.3 0.7 copy-done.12
  23.0 2.9 %shard_map.55 = (bf16[2,1024,256]{2,1,0:T(8,128)(2,1)}, bf16[32,80,256]{2,1,0:T(8,128)(2,1)}) custom-call(s32[4]{0:T(128)} %and_select_fusion.7.rows_ref, s32[2,256,1]{2,1,0:T(8,128)} %reshape.116.keys_ref, bf16[2,256,256]{2,1,0:T(8,128)(2,1)} %get-tuple-element.96.p0, bf16[2,256,256]{2,1,0:T(8,128)(2,1)} %copy-done.11, bf16[2,256,256]{2,1,0:T(8,128)(2,1)} %copy-done.12, ...), custom_call_target="tpu_custom_call" | custom-call | tf_op jit(solution)/shard_map/pallas_call | solution.py:78
  25.9 7.8 %all-to-all-start = ((bf16[32,80,256]{2,1,0:T(8,128)(2,1)}), bf16[32,80,256]{2,1,0:T(8,128)(2,1)}, u32[]{:S(2)}, u32[]{:S(2)}) async-start(bf16[32,80,256]{2,1,0:T(8,128)(2,1)} %get-tuple-element.48), calls=%async_computation | async-start | bytes 2621440 | tf_op jit(solution)/shard_map/all_to_all | solution.py:608
  34.2 0.7 pad_maximum_fusion.1.refs_15_.refs_17_
  35.2 0.6 and_select_fusion.5.first_ref
  35.9 1.9 %collective-permute-start.11 = (bf16[256,1024]{1,0:T(8,128)(2,1)}, bf16[256,1024]{1,0:T(8,128)(2,1)}, u32[]{:S(2)}, u32[]{:S(2)}) collective-permute-start(bf16[256,1024]{1,0:T(8,128)(2,1)} %get-tuple-element.60), channel_id=1, source_target_pairs={{0,2},{1,3},{2,0},{3,1},{4,6},{5,7},{6,4},{7,5},{8,10},{9,11},{10,... | collective-permute-start | bytes 1572872 | tf_op jit(solution)/shard_map/ppermute | solution.py:40
  37.8 1.5 %collective-permute-start.12 = (bf16[256,1024]{1,0:T(8,128)(2,1)}, bf16[256,1024]{1,0:T(8,128)(2,1)}, u32[]{:S(2)}, u32[]{:S(2)}) collective-permute-start(bf16[256,1024]{1,0:T(8,128)(2,1)} %get-tuple-element.61), channel_id=1, source_target_pairs={{0,3},{1,0},{2,1},{3,2},{4,7},{5,4},{6,5},{7,6},{8,11},{9,8},{10,9... | collective-permute-start | bytes 1572872 | tf_op jit(solution)/shard_map/ppermute | solution.py:40
  39.3 0.8 slice.23
  40.1 1.9 %collective-permute-start.6 = (bf16[2,64,256]{2,1,0:T(8,128)(2,1)S(1)}, bf16[2,64,256]{2,1,0:T(8,128)(2,1)S(1)}, u32[]{:S(2)}, u32[]{:S(2)}) collective-permute-start(bf16[2,64,256]{2,1,0:T(8,128)(2,1)S(1)} %slice.23), channel_id=1, source_target_pairs={{0,4},{4,8},{8,12},{12,16},{16,20},{20,24},{24,28},{28,32},{32,36}... | collective-permute-start | bytes 196616 | tf_op jit(solution)/shard_map/ppermute | solution.py:56
  42.2 0.7 reshape.112.refs_14_.refs_16_
  42.8 8.9 %all-to-all-done.rows_ref.table_ref = bf16[32,80,256]{2,1,0:T(8,128)(2,1)} async-done(((bf16[32,80,256]{2,1,0:T(8,128)(2,1)}), bf16[32,80,256]{2,1,0:T(8,128)(2,1)}, u32[]{:S(2)}, u32[]{:S(2)}) %all-to-all-start) | async-done | bytes 1310752 | tf_op jit(solution)/shard_map/all_to_all | solution.py:608
  51.8 2.8 %shard_map.56 = bf16[2,32,256]{2,1,0:T(8,128)(2,1)} custom-call(s32[2,32]{1,0:T(2,128)} %and_select_fusion.5.first_ref, bf16[32,80,256]{2,1,0:T(8,128)(2,1)} %all-to-all-done.rows_ref.table_ref), custom_call_target="tpu_custom_call" | custom-call | tf_op jit(solution)/shard_map/pallas_call | solution.py:127
  54.6 1.2 collective-permute-start.5
  55.8 1.0 collective-permute-start.4
  56.8 1.9 %collective-permute-done.5 = bf16[2,32,256]{2,1,0:T(8,128)(2,1)S(1)} collective-permute-done((bf16[2,32,256]{2,1,0:T(8,128)(2,1)}, bf16[2,32,256]{2,1,0:T(8,128)(2,1)S(1)}, u32[]{:S(2)}, u32[]{:S(2)}) %collective-permute-start.5) | collective-permute-done | bytes 32800 | tf_op jit(solution)/shard_map/ppermute | solution.py:52
  58.9 0.6 and_select_fusion.3.shift_ref
  59.4 3.8 %shard_map.57 = bf16[32,2,64,256]{3,2,1,0:T(8,128)(2,1)} custom-call(s32[2]{0:T(128)} %and_select_fusion.3.shift_ref, bf16[32,80,256]{2,1,0:T(8,128)(2,1)} %all-to-all-done.rows_ref.table_ref), custom_call_target="tpu_custom_call" | custom-call | tf_op jit(solution)/shard_map/pallas_call | solution.py:150
  63.3 0.8 collective-permute-done.3
  64.1 0.7 collective-permute-start.9
  64.9 2.9 %collective-permute-start.8 = (bf16[4,2,32,256]{3,2,1,0:T(8,128)(2,1)S(1)}, bf16[4,2,32,256]{3,2,1,0:T(8,128)(2,1)S(1)}, u32[]{:S(2)}, u32[]{:S(2)}) collective-permute-start(bf16[4,2,32,256]{3,2,1,0:T(8,128)(2,1)S(1)} %pad_maximum_fusion.refs_4_), channel_id=1, source_target_pairs={{0,64},{4,68},{8,72},{12,76},{16,80},{20,84},{24,88},{28,92},{32,9... | collective-permute-start | bytes 393224 | tf_op jit(solution)/shard_map/ppermute | solution.py:52
  67.7 0.4 collective-permute-start.7
  68.1 2.9 %collective-permute-done.9.refs_7_ = bf16[4,2,32,256]{3,2,1,0:T(8,128)(2,1)S(1)} collective-permute-done((bf16[4,2,32,256]{3,2,1,0:T(8,128)(2,1)S(1)}, bf16[4,2,32,256]{3,2,1,0:T(8,128)(2,1)S(1)}, u32[]{:S(2)}, u32[]{:S(2)}) %collective-permute-start.9) | collective-permute-done | bytes 131104 | tf_op jit(solution)/shard_map/ppermute | solution.py:52
  71.0 1.4 collective-permute-done.8.refs_6_
  72.7 8.8 %all-to-all-start.1 = ((bf16[32,2,64,256]{3,2,1,0:T(8,128)(2,1)}), bf16[32,2,64,256]{3,2,1,0:T(8,128)(2,1)}, u32[]{:S(2)}, u32[]{:S(2)}) async-start(bf16[32,2,64,256]{3,2,1,0:T(8,128)(2,1)} %shard_map.57), calls=%async_computation.1 | async-start | bytes 4194304 | tf_op jit(solution)/shard_map/all_to_all | solution.py:632
  82.1 1.8 %collective-permute-start.14 = (bf16[256,1024]{1,0:T(8,128)(2,1)}, bf16[256,1024]{1,0:T(8,128)(2,1)}, u32[]{:S(2)}, u32[]{:S(2)}) collective-permute-start(bf16[256,1024]{1,0:T(8,128)(2,1)} %get-tuple-element.64), channel_id=1, source_target_pairs={{0,2},{1,3},{2,0},{3,1},{4,6},{5,7},{6,4},{7,5},{8,10},{9,11},{10,... | collective-permute-start | bytes 1572872 | tf_op jit(solution)/shard_map/ppermute | solution.py:40
  83.9 1.4 collective-permute-start.15
  85.6 0.7 collective-permute-start.19
  86.3 0.6 and_select_fusion.2.order_ref
  86.9 0.5 collective-permute-done.19.refs_11_
  87.6 19.2 %shard_map.58 = (bf16[4,256,1024]{2,1,0:T(8,128)(2,1)}, bf16[4,256,128]{2,1,0:T(8,128)(2,1)}, bf16[4,256,1024]{2,1,0:T(8,128)(2,1)}) custom-call(s32[4]{0:T(128)} %and_select_fusion.7.rows_ref, bf16[256,1024]{1,0:T(8,128)(2,1)} %get-tuple-element.72.refs_0_, bf16[256,1024]{1,0:T(8,128)(2,1)} %collective-permute-done.10.refs_1_, ...), custom_call_target="tpu_custom_call" | custom-call | flops 1000000000 | bytes 1048576 | tf_op jit(solution)/shard_map/pallas_call | solution.py:277
  106.8 1.2 all-to-all-done.1
  107.9 2.1 %shard_map.59 = bf16[2,2,64,256]{3,2,1,0:T(8,128)(2,1)} custom-call(s32[4]{0:T(128)} %and_select_fusion.2.order_ref, bf16[2,16,2,64,256]{4,3,2,1,0:T(8,128)(2,1)} %bitcast.14.refs_0_.refs_1_.refs_2_.refs_3_.refs_14_, bf16[2,16,2,64,256]{4,3,2,1,0:T(8,128)(2,1)} %bitcast.14.refs_0_.refs_1_.refs_2_.refs_3_.refs_14_, ...), custom_call_target="tpu_custom_call" | custom-call | tf_op jit(solution)/shard_map/pallas_call | solution.py:99
  110.1 1.9 %collective-permute-start.20 = (bf16[2,2,64,256]{3,2,1,0:T(8,128)(2,1)}, bf16[2,2,64,256]{3,2,1,0:T(8,128)(2,1)S(1)}, u32[]{:S(2)}, u32[]{:S(2)}) collective-permute-start(bf16[2,2,64,256]{3,2,1,0:T(8,128)(2,1)} %shard_map.59), channel_id=1, source_target_pairs={{0,4},{4,8},{8,12},{12,16},{16,20},{20,24},{24,28},{28,32},{32,36}... | collective-permute-start | bytes 393224 | tf_op jit(solution)/shard_map/ppermute | solution.py:56
  112.0 0.6 reshape.113.order_ref
  112.6 6.0 %collective-permute-done.20.refs_15_ = bf16[2,2,64,256]{3,2,1,0:T(8,128)(2,1)S(1)} collective-permute-done((bf16[2,2,64,256]{3,2,1,0:T(8,128)(2,1)}, bf16[2,2,64,256]{3,2,1,0:T(8,128)(2,1)S(1)}, u32[]{:S(2)}, u32[]{:S(2)}) %collective-permute-start.20) | collective-permute-done | bytes 131104 | tf_op jit(solution)/shard_map/ppermute | solution.py:56
  118.7 0.7 copy-done.13
  119.3 27.8 %shard_map.60 = bf16[1024,2048]{1,0:T(8,128)(2,1)} custom-call(s32[4]{0:T(128)} %and_select_fusion.7.rows_ref, s32[4]{0:T(128)} %reshape.113.order_ref, bf16[256,1024]{1,0:T(8,128)(2,1)} %get-tuple-element.62.refs_0_, bf16[256,1024]{1,0:T(8,128)(2,1)} %collective-permute-done.13.refs_1_, bf16[256,1024]{1,0:T(8,128)(2,1)} %collective-permute-done.14.refs_2_, ...), custom_call_target="tpu_custom_call" | custom-call | tf_op jit(solution)/shard_map/pallas_call | solution.py:506
  (86 shorter events, 3.8 us)
Async XLA Ops:
  0.0 1.6 %copy-start.8 = (bf16[256,1024]{1,0:T(8,128)(2,1)S(1)}, bf16[256,1024]{1,0:T(8,128)(2,1)}, u32[]{:S(2)}) copy-start(bf16[256,1024]{1,0:T(8,128)(2,1)} %param.7) | copy-start | bytes 1572868
  1.6 7.3 %copy-start.16 = (s32[2,3]{1,0:T(2,128)S(1)}, s32[2,3]{1,0:T(2,128)}, u32[]{:S(2)}) copy-start(s32[2,3]{1,0:T(2,128)} %param.9) | copy-start | bytes 76
  1.6 7.5 %copy-start.15 = (s32[2,1024]{1,0:T(2,128)S(1)}, s32[2,1024]{1,0:T(2,128)}, u32[]{:S(2)}) copy-start(s32[2,1024]{1,0:T(2,128)} %param.8) | copy-start | bytes 24580
  3.0 15.2 %collective-permute-start.2 = (bf16[2,256,256]{2,1,0:T(8,128)(2,1)S(1)}, bf16[2,256,256]{2,1,0:T(8,128)(2,1)S(1)}, u32[]{:S(2)}, u32[]{:S(2)}) collective-permute-start(bf16[2,256,256]{2,1,0:T(8,128)(2,1)S(1)} %get-tuple-element.95), channel_id=1, source_target_pairs={{0,3},{1,0},{2,1},{3,2},{4,7},{5,4},{6,5},{7,6},{8,11},{9,8},{10,9... | collective-permute-start | bytes 786440 | tf_op jit(solution)/shard_map/ppermute | solution.py:40
  7.0 14.6 %collective-permute-start = (bf16[2,256,256]{2,1,0:T(8,128)(2,1)S(1)}, bf16[2,256,256]{2,1,0:T(8,128)(2,1)S(1)}, u32[]{:S(2)}, u32[]{:S(2)}) collective-permute-start(bf16[2,256,256]{2,1,0:T(8,128)(2,1)S(1)} %get-tuple-element.97), channel_id=1, source_target_pairs={{0,1},{1,2},{2,3},{3,0},{4,5},{5,6},{6,7},{7,4},{8,9},{9,10},{10,1... | collective-permute-start | bytes 786440 | tf_op jit(solution)/shard_map/ppermute | solution.py:40
  7.0 14.6 %collective-permute-start.1 = (bf16[2,256,256]{2,1,0:T(8,128)(2,1)S(1)}, bf16[2,256,256]{2,1,0:T(8,128)(2,1)S(1)}, u32[]{:S(2)}, u32[]{:S(2)}) collective-permute-start(bf16[2,256,256]{2,1,0:T(8,128)(2,1)S(1)} %get-tuple-element.98), channel_id=1, source_target_pairs={{0,2},{1,3},{2,0},{3,1},{4,6},{5,7},{6,4},{7,5},{8,10},{9,11},{10,... | collective-permute-start | bytes 786440 | tf_op jit(solution)/shard_map/ppermute | solution.py:40
  18.2 4.8 %copy-start.10 = (bf16[2,256,256]{2,1,0:T(8,128)(2,1)}, bf16[2,256,256]{2,1,0:T(8,128)(2,1)S(1)}, u32[]{:S(2)}) copy-start(bf16[2,256,256]{2,1,0:T(8,128)(2,1)S(1)} %collective-permute-done.2.p3) | copy-start | bytes 786436
  21.6 0.7 copy-start.11
  22.3 0.7 copy-start.12
  25.9 7.9 %copy-start = (s32[2,32,4,4,2]{4,3,2,1,0:T(4,128)S(1)}, s32[2,32,4,4,2]{4,3,2,1,0:T(4,128)}, u32[]{:S(2)}) copy-start(s32[2,32,4,4,2]{4,3,2,1,0:T(4,128)} %reshape.111) | copy-start | bytes 24580
  25.9 25.9 %all-to-all-start = ((bf16[32,80,256]{2,1,0:T(8,128)(2,1)}), bf16[32,80,256]{2,1,0:T(8,128)(2,1)}, u32[]{:S(2)}, u32[]{:S(2)}) async-start(bf16[32,80,256]{2,1,0:T(8,128)(2,1)} %get-tuple-element.48), calls=%async_computation | async-start | bytes 2621440 | tf_op jit(solution)/shard_map/all_to_all | solution.py:608
  35.8 31.9 %collective-permute-start.10 = (bf16[256,1024]{1,0:T(8,128)(2,1)}, bf16[256,1024]{1,0:T(8,128)(2,1)}, u32[]{:S(2)}, u32[]{:S(2)}) collective-permute-start(bf16[256,1024]{1,0:T(8,128)(2,1)} %get-tuple-element.59), channel_id=1, source_target_pairs={{0,1},{1,2},{2,3},{3,0},{4,5},{5,6},{6,7},{7,4},{8,9},{9,10},{10,1... | collective-permute-start | bytes 1572872 | tf_op jit(solution)/shard_map/ppermute | solution.py:40
  35.9 32.2 %collective-permute-start.11 = (bf16[256,1024]{1,0:T(8,128)(2,1)}, bf16[256,1024]{1,0:T(8,128)(2,1)}, u32[]{:S(2)}, u32[]{:S(2)}) collective-permute-start(bf16[256,1024]{1,0:T(8,128)(2,1)} %get-tuple-element.60), channel_id=1, source_target_pairs={{0,2},{1,3},{2,0},{3,1},{4,6},{5,7},{6,4},{7,5},{8,10},{9,11},{10,... | collective-permute-start | bytes 1572872 | tf_op jit(solution)/shard_map/ppermute | solution.py:40
  37.8 30.4 %collective-permute-start.12 = (bf16[256,1024]{1,0:T(8,128)(2,1)}, bf16[256,1024]{1,0:T(8,128)(2,1)}, u32[]{:S(2)}, u32[]{:S(2)}) collective-permute-start(bf16[256,1024]{1,0:T(8,128)(2,1)} %get-tuple-element.61), channel_id=1, source_target_pairs={{0,3},{1,0},{2,1},{3,2},{4,7},{5,4},{6,5},{7,6},{8,11},{9,8},{10,9... | collective-permute-start | bytes 1572872 | tf_op jit(solution)/shard_map/ppermute | solution.py:40
  40.1 15.6 %collective-permute-start.6 = (bf16[2,64,256]{2,1,0:T(8,128)(2,1)S(1)}, bf16[2,64,256]{2,1,0:T(8,128)(2,1)S(1)}, u32[]{:S(2)}, u32[]{:S(2)}) collective-permute-start(bf16[2,64,256]{2,1,0:T(8,128)(2,1)S(1)} %slice.23), channel_id=1, source_target_pairs={{0,4},{4,8},{8,12},{12,16},{16,20},{20,24},{24,28},{28,32},{32,36}... | collective-permute-start | bytes 196616 | tf_op jit(solution)/shard_map/ppermute | solution.py:56
  54.6 9.5 %copy-start.14 = (bf16[2,32,256]{2,1,0:T(8,128)(2,1)S(1)}, bf16[2,32,256]{2,1,0:T(8,128)(2,1)}, u32[]{:S(2)}) copy-start(bf16[2,32,256]{2,1,0:T(8,128)(2,1)} %shard_map.56) | copy-start | bytes 98308
  54.6 4.1 %collective-permute-start.5 = (bf16[2,32,256]{2,1,0:T(8,128)(2,1)}, bf16[2,32,256]{2,1,0:T(8,128)(2,1)S(1)}, u32[]{:S(2)}, u32[]{:S(2)}) collective-permute-start(bf16[2,32,256]{2,1,0:T(8,128)(2,1)} %shard_map.56), channel_id=1, source_target_pairs={{0,24},{4,28},{8,0},{12,4},{16,8},{20,12},{24,16},{28,20},{32,56},... | collective-permute-start | bytes 98312 | tf_op jit(solution)/shard_map/ppermute | solution.py:52
  55.8 16.9 %copy-start.9 = (bf16[2,64,256]{2,1,0:T(8,128)(2,1)}, bf16[2,64,256]{2,1,0:T(8,128)(2,1)S(1)}, u32[]{:S(2)}) copy-start(bf16[2,64,256]{2,1,0:T(8,128)(2,1)S(1)} %collective-permute-done.6.refs_12_) | copy-start | bytes 196612
  55.8 7.5 %collective-permute-start.4 = (bf16[2,32,256]{2,1,0:T(8,128)(2,1)}, bf16[2,32,256]{2,1,0:T(8,128)(2,1)S(1)}, u32[]{:S(2)}, u32[]{:S(2)}) collective-permute-start(bf16[2,32,256]{2,1,0:T(8,128)(2,1)} %shard_map.56), channel_id=1, source_target_pairs={{0,16},{4,20},{8,24},{12,28},{16,0},{20,4},{24,8},{28,12},{32,48},... | collective-permute-start | bytes 98312 | tf_op jit(solution)/shard_map/ppermute | solution.py:52
  58.7 5.3 %collective-permute-start.3 = (bf16[2,32,256]{2,1,0:T(8,128)(2,1)}, bf16[2,32,256]{2,1,0:T(8,128)(2,1)S(1)}, u32[]{:S(2)}, u32[]{:S(2)}) collective-permute-start(bf16[2,32,256]{2,1,0:T(8,128)(2,1)} %shard_map.56), channel_id=1, source_target_pairs={{0,8},{4,12},{8,16},{12,20},{16,24},{20,28},{24,0},{28,4},{32,40},... | collective-permute-start | bytes 98312 | tf_op jit(solution)/shard_map/ppermute | solution.py:52
  64.1 17.4 %copy-start.1 = (bf16[4,2,32,256]{3,2,1,0:T(8,128)(2,1)}, bf16[4,2,32,256]{3,2,1,0:T(8,128)(2,1)S(1)}, u32[]{:S(2)}) copy-start(bf16[4,2,32,256]{3,2,1,0:T(8,128)(2,1)S(1)} %pad_maximum_fusion.refs_4_) | copy-start | bytes 393220
  64.1 6.9 %collective-permute-start.9 = (bf16[4,2,32,256]{3,2,1,0:T(8,128)(2,1)S(1)}, bf16[4,2,32,256]{3,2,1,0:T(8,128)(2,1)S(1)}, u32[]{:S(2)}, u32[]{:S(2)}) collective-permute-start(bf16[4,2,32,256]{3,2,1,0:T(8,128)(2,1)S(1)} %pad_maximum_fusion.refs_4_), channel_id=1, source_target_pairs={{0,96},{4,100},{8,104},{12,108},{16,112},{20,116},{24,120},{28,124... | collective-permute-start | bytes 393224 | tf_op jit(solution)/shard_map/ppermute | solution.py:52
  64.9 7.6 %collective-permute-start.8 = (bf16[4,2,32,256]{3,2,1,0:T(8,128)(2,1)S(1)}, bf16[4,2,32,256]{3,2,1,0:T(8,128)(2,1)S(1)}, u32[]{:S(2)}, u32[]{:S(2)}) collective-permute-start(bf16[4,2,32,256]{3,2,1,0:T(8,128)(2,1)S(1)} %pad_maximum_fusion.refs_4_), channel_id=1, source_target_pairs={{0,64},{4,68},{8,72},{12,76},{16,80},{20,84},{24,88},{28,92},{32,9... | collective-permute-start | bytes 393224 | tf_op jit(solution)/shard_map/ppermute | solution.py:52
  67.7 5.0 %collective-permute-start.7 = (bf16[4,2,32,256]{3,2,1,0:T(8,128)(2,1)S(1)}, bf16[4,2,32,256]{3,2,1,0:T(8,128)(2,1)S(1)}, u32[]{:S(2)}, u32[]{:S(2)}) collective-permute-start(bf16[4,2,32,256]{3,2,1,0:T(8,128)(2,1)S(1)} %pad_maximum_fusion.refs_4_), channel_id=1, source_target_pairs={{0,32},{4,36},{8,40},{12,44},{16,48},{20,52},{24,56},{28,60},{32,6... | collective-permute-start | bytes 393224 | tf_op jit(solution)/shard_map/ppermute | solution.py:52
  71.0 14.6 %copy-start.2 = (bf16[4,2,32,256]{3,2,1,0:T(8,128)(2,1)}, bf16[4,2,32,256]{3,2,1,0:T(8,128)(2,1)S(1)}, u32[]{:S(2)}) copy-start(bf16[4,2,32,256]{3,2,1,0:T(8,128)(2,1)S(1)} %collective-permute-done.9.refs_7_) | copy-start | bytes 393220
  72.4 13.1 %copy-start.3 = (bf16[4,2,32,256]{3,2,1,0:T(8,128)(2,1)}, bf16[4,2,32,256]{3,2,1,0:T(8,128)(2,1)S(1)}, u32[]{:S(2)}) copy-start(bf16[4,2,32,256]{3,2,1,0:T(8,128)(2,1)S(1)} %collective-permute-done.8.refs_6_) | copy-start | bytes 393220
  72.7 9.1 %copy-start.4 = (bf16[4,2,32,256]{3,2,1,0:T(8,128)(2,1)}, bf16[4,2,32,256]{3,2,1,0:T(8,128)(2,1)S(1)}, u32[]{:S(2)}) copy-start(bf16[4,2,32,256]{3,2,1,0:T(8,128)(2,1)S(1)} %collective-permute-done.7.refs_5_) | copy-start | bytes 393220
  72.7 35.2 %all-to-all-start.1 = ((bf16[32,2,64,256]{3,2,1,0:T(8,128)(2,1)}), bf16[32,2,64,256]{3,2,1,0:T(8,128)(2,1)}, u32[]{:S(2)}, u32[]{:S(2)}) async-start(bf16[32,2,64,256]{3,2,1,0:T(8,128)(2,1)} %shard_map.57), calls=%async_computation.1 | async-start | bytes 4194304 | tf_op jit(solution)/shard_map/all_to_all | solution.py:632
  81.6 3.9 %collective-permute-start.16 = (bf16[4,2,32,256]{3,2,1,0:T(8,128)(2,1)S(1)}, bf16[4,2,32,256]{3,2,1,0:T(8,128)(2,1)S(1)}, u32[]{:S(2)}, u32[]{:S(2)}) collective-permute-start(bf16[4,2,32,256]{3,2,1,0:T(8,128)(2,1)S(1)} %pad_maximum_fusion.refs_4_), channel_id=1, source_target_pairs={{0,4},{4,0},{8,12},{12,8},{16,20},{20,16},{24,28},{28,24},{32,36},... | collective-permute-start | bytes 393224 | tf_op jit(solution)/shard_map/ppermute | solution.py:52
  81.8 3.8 %collective-permute-start.17 = (bf16[4,2,32,256]{3,2,1,0:T(8,128)(2,1)S(1)}, bf16[4,2,32,256]{3,2,1,0:T(8,128)(2,1)S(1)}, u32[]{:S(2)}, u32[]{:S(2)}) collective-permute-start(bf16[4,2,32,256]{3,2,1,0:T(8,128)(2,1)S(1)} %collective-permute-done.7.refs_5_), channel_id=1, source_target_pairs={{0,4},{4,0},{8,12},{12,8},{16,20},{20,16},{24,28},{28,24},{32,36},... | collective-permute-start | bytes 393224 | tf_op jit(solution)/shard_map/ppermute | solution.py:52
  82.1 30.5 %collective-permute-start.13 = (bf16[256,1024]{1,0:T(8,128)(2,1)}, bf16[256,1024]{1,0:T(8,128)(2,1)}, u32[]{:S(2)}, u32[]{:S(2)}) collective-permute-start(bf16[256,1024]{1,0:T(8,128)(2,1)} %get-tuple-element.63), channel_id=1, source_target_pairs={{0,1},{1,2},{2,3},{3,0},{4,5},{5,6},{6,7},{7,4},{8,9},{9,10},{10,1... | collective-permute-start | bytes 1572872 | tf_op jit(solution)/shard_map/ppermute | solution.py:40
  82.1 30.5 %collective-permute-start.14 = (bf16[256,1024]{1,0:T(8,128)(2,1)}, bf16[256,1024]{1,0:T(8,128)(2,1)}, u32[]{:S(2)}, u32[]{:S(2)}) collective-permute-start(bf16[256,1024]{1,0:T(8,128)(2,1)} %get-tuple-element.64), channel_id=1, source_target_pairs={{0,2},{1,3},{2,0},{3,1},{4,6},{5,7},{6,4},{7,5},{8,10},{9,11},{10,... | collective-permute-start | bytes 1572872 | tf_op jit(solution)/shard_map/ppermute | solution.py:40
  83.9 28.7 %collective-permute-start.15 = (bf16[256,1024]{1,0:T(8,128)(2,1)}, bf16[256,1024]{1,0:T(8,128)(2,1)}, u32[]{:S(2)}, u32[]{:S(2)}) collective-permute-start(bf16[256,1024]{1,0:T(8,128)(2,1)} %get-tuple-element.65), channel_id=1, source_target_pairs={{0,3},{1,0},{2,1},{3,2},{4,7},{5,4},{6,5},{7,6},{8,11},{9,8},{10,9... | collective-permute-start | bytes 1572872 | tf_op jit(solution)/shard_map/ppermute | solution.py:40
  85.5 1.4 copy-start.5
  85.5 1.4 collective-permute-start.18
  85.6 1.3 copy-start.6
  85.6 1.8 %collective-permute-start.19 = (bf16[4,2,32,256]{3,2,1,0:T(8,128)(2,1)S(1)}, bf16[4,2,32,256]{3,2,1,0:T(8,128)(2,1)}, u32[]{:S(2)}, u32[]{:S(2)}) collective-permute-start(bf16[4,2,32,256]{3,2,1,0:T(8,128)(2,1)S(1)} %collective-permute-done.9.refs_7_), channel_id=1, source_target_pairs={{0,4},{4,0},{8,12},{12,8},{16,20},{20,16},{24,28},{28,24},{32,36},... | collective-permute-start | bytes 393224 | tf_op jit(solution)/shard_map/ppermute | solution.py:52
  86.9 0.7 copy-start.7
  110.1 8.6 %collective-permute-start.20 = (bf16[2,2,64,256]{3,2,1,0:T(8,128)(2,1)}, bf16[2,2,64,256]{3,2,1,0:T(8,128)(2,1)S(1)}, u32[]{:S(2)}, u32[]{:S(2)}) collective-permute-start(bf16[2,2,64,256]{3,2,1,0:T(8,128)(2,1)} %shard_map.59), channel_id=1, source_target_pairs={{0,4},{4,8},{8,12},{12,16},{16,20},{20,24},{24,28},{28,32},{32,36}... | collective-permute-start | bytes 393224 | tf_op jit(solution)/shard_map/ppermute | solution.py:56
  118.7 0.7 copy-start.13

commit v5 on v4

--- a/solution.py
+++ b/solution.py
@@ -280,7 +280,10 @@
             num_scalar_prefetch=1,
             grid=(NTP,),
             in_specs=[pl.BlockSpec((PIECE, wide), lambda p, s: (0, 0))] * NTP
-            + [pl.BlockSpec((4, 1, KEPT, 2 * DH), lambda p, s: (0, head, 0, 0))] * 8
+            + [
+                pl.BlockSpec((4, 1, KEPT, 2 * DH), lambda p, s, i=i: (i, head, 0, 0))
+                for i in (0, 0, 0, 0, 0, 1, 2, 3)
+            ]
             + [
                 pl.BlockSpec((1, BLOCK, 2 * DH), lambda p, s: (head, 0, 0)),
                 pl.BlockSpec((1, TOK, 2 * DH), lambda p, s: (head, 0, 0)),
@@ -509,7 +512,10 @@
             num_scalar_prefetch=2,
             grid=(2 * NTP,),
             in_specs=[pl.BlockSpec((PIECE, wide), lambda p, s, o: (0, 0))] * NTP
-            + [pl.BlockSpec((4, 1, KEPT, 2 * DH), lambda p, s, o: (0, 1, 0, 0))] * 8
+            + [
+                pl.BlockSpec((4, 1, KEPT, 2 * DH), lambda p, s, o, i=i: (i, 1, 0, 0))
+                for i in (0, 0, 0, 0, 0, 1, 2, 3)
+            ]
             + [
                 pl.BlockSpec((1, BLOCK, 2 * DH), lambda p, s, o: (1, 0, 0)),
                 pl.BlockSpec((1, TOK, 2 * DH), lambda p, s, o: (1, 0, 0)),
@@ -625,9 +631,9 @@
     spread, along_x, first_queries, second_parts = lax.optimization_barrier(
         (spread, along_x, first_queries, second_parts)
     )
-    across = [ctx_route(part, lambda x, y, core: (x, y, core + 1)) for part in along_x]
+    across = ctx_route(jnp.concatenate(along_x), lambda x, y, core: (x, y, core + 1))
     second_queries = send_queries(second_parts)
-    vert = along_x + across
+    vert = along_x + [across] * 4
 
     windows = lax.all_to_all(
         spread, "ctx", split_axis=0, concat_axis=0, tiled=True

time: 148 us -> 148 us (level)
    all_to_all x1, waiting for transfers between devices: 1.15 us -> 2.98 us  [shards(): lax.all_to_all(spread, 'ctx', split_axis=0, concat_axis=0, tiled=True)]
    ppermute x10 -> x7, starting transfers between devices: 7.69 us -> 6.51 us  [ctx_route(): return lax.ppermute(block, 'ctx', pairs)]
    ppermute x10 -> x7, waiting for transfers between devices: 7.83 us -> 7.28 us  [ctx_route(): return lax.ppermute(block, 'ctx', pairs)]
    unnamed x38 -> x32, local copies, waits for them, and re-layouts: 3.74 us -> 3.59 us
  transfers between devices with their start and end apart: 23 -> 20, of which waited for: 11 -> 10; matrix products, arithmetic and copies ran while one was open for 9% -> 9% of each run, Pallas kernels for 19% -> 19%
where the time goes in v5:
time: 148 us; the launch traced here: 147 us
  Pallas kernels  58.6 us (40%)
  starting transfers between devices  39.6 us (27%)
  waiting for transfers between devices  30 us (20%)
  local copies, waits for them, and re-layouts  13.8 us (9%)
  other arithmetic  4.5 us (3%)
    pallas_call x1, Pallas kernels, tail_attention(): pl.pallas_call(tail_kernel, grid_spec=pltpu.PrefetchScalarGridSpec(num_sc...  27.8 us
    pallas_call x1, Pallas kernels, near_attention(): pl.pallas_call(near_kernel, grid_spec=pltpu.PrefetchScalarGridSpec(num_sc...  19.2 us
    ppermute x9, starting transfers between devices, tp_shift(): lax.ppermute(block, 'tp', [(i, (i + distance) % NTP) for i in range(NTP)])  12.6 us
    all_to_all x1, waiting for transfers between devices, shards(): table = lax.all_to_all(sent, 'ctx', split_axis=0, concat_axis=0, tiled=True)  8.94 us
    all_to_all x1, starting transfers between devices, shards(): lax.all_to_all(spread, 'ctx', split_axis=0, concat_axis=0, tiled=True)  8.86 us
    all_to_all x1, starting transfers between devices, shards(): table = lax.all_to_all(sent, 'ctx', split_axis=0, concat_axis=0, tiled=True)  7.78 us
    ppermute x7, waiting for transfers between devices, ctx_route(): return lax.ppermute(block, 'ctx', pairs)  7.28 us
    ppermute x7, starting transfers between devices, ctx_route(): return lax.ppermute(block, 'ctx', pairs)  6.51 us
  transfers between devices with their start and end apart: 20, of which 10 were waited for; matrix products, arithmetic and copies ran while one was open for 9% of the time, Pallas kernels for 19%

profile of v5, /device:TPU:6, one launch (start us, length us, event | category | flops | bytes accessed | tf_op | source)
XLA Modules:
  0.0 147.3 jit_solution(7228097005360207773)
XLA Ops:
  0.0 1.3 copy.33
  2.1 0.8 fusion.4
  3.0 4.0 %collective-permute-start.2 = (bf16[2,256,256]{2,1,0:T(8,128)(2,1)S(1)}, bf16[2,256,256]{2,1,0:T(8,128)(2,1)S(1)}, u32[]{:S(2)}, u32[]{:S(2)}) collective-permute-start(bf16[2,256,256]{2,1,0:T(8,128)(2,1)S(1)} %get-tuple-element.95), channel_id=1, source_target_pairs={{0,3},{1,0},{2,1},{3,2},{4,7},{5,4},{6,5},{7,6},{8,11},{9,8},{10,9... | collective-permute-start | bytes 786440 | tf_op jit(solution)/shard_map/ppermute | solution.py:40
  7.0 1.9 %collective-permute-start.1 = (bf16[2,256,256]{2,1,0:T(8,128)(2,1)S(1)}, bf16[2,256,256]{2,1,0:T(8,128)(2,1)S(1)}, u32[]{:S(2)}, u32[]{:S(2)}) collective-permute-start(bf16[2,256,256]{2,1,0:T(8,128)(2,1)S(1)} %get-tuple-element.98), channel_id=1, source_target_pairs={{0,2},{1,3},{2,0},{3,1},{4,6},{5,7},{6,4},{7,5},{8,10},{9,11},{10,... | collective-permute-start | bytes 786440 | tf_op jit(solution)/shard_map/ppermute | solution.py:40
  9.3 0.3 fusion.1
  9.6 0.6 and_select_fusion.7.rows_ref
  10.2 1.4 reshape.111
  11.7 0.8 reshape.116.keys_ref
  12.6 4.3 %constant_dynamic-slice_fusion = (bf16[256,1024]{1,0:T(8,128)(2,1)}, bf16[256,1024]{1,0:T(8,128)(2,1)}, bf16[256,1024]{1,0:T(8,128)(2,1)}, bf16[256,1024]{1,0:T(...) fusion(bf16[256,8192]{1,0:T(8,128)(2,1)} %param.5, ...), kind=kLoop, calls=%fused_computation.44 | loop fusion | bytes 8388640 | tf_op jit(solution)/shard_map/dynamic_slice | solution.py:603
  16.9 1.3 collective-permute-done.2.p3
  18.2 3.4 %collective-permute-done.p1 = bf16[2,256,256]{2,1,0:T(8,128)(2,1)S(1)} collective-permute-done((bf16[2,256,256]{2,1,0:T(8,128)(2,1)S(1)}, bf16[2,256,256]{2,1,0:T(8,128)(2,1)S(1)}, u32[]{:S(2)}, u32[]{:S(2)}) %collective-permute-start) | collective-permute-done | bytes 262176 | tf_op jit(solution)/shard_map/ppermute | solution.py:40
  21.6 0.7 copy-done.8
  22.3 0.7 copy-done.9
  23.0 2.9 %shard_map.55 = (bf16[2,1024,256]{2,1,0:T(8,128)(2,1)}, bf16[32,80,256]{2,1,0:T(8,128)(2,1)}) custom-call(s32[4]{0:T(128)} %and_select_fusion.7.rows_ref, s32[2,256,1]{2,1,0:T(8,128)} %reshape.116.keys_ref, bf16[2,256,256]{2,1,0:T(8,128)(2,1)} %get-tuple-element.96.p0, bf16[2,256,256]{2,1,0:T(8,128)(2,1)} %copy-done.8, bf16[2,256,256]{2,1,0:T(8,128)(2,1)} %copy-done.9, ...), custom_call_target="tpu_custom_call" | custom-call | tf_op jit(solution)/shard_map/pallas_call | solution.py:78
  25.8 7.8 %all-to-all-start = ((bf16[32,80,256]{2,1,0:T(8,128)(2,1)}), bf16[32,80,256]{2,1,0:T(8,128)(2,1)}, u32[]{:S(2)}, u32[]{:S(2)}) async-start(bf16[32,80,256]{2,1,0:T(8,128)(2,1)} %get-tuple-element.48), calls=%async_computation | async-start | bytes 2621440 | tf_op jit(solution)/shard_map/all_to_all | solution.py:614
  33.8 0.3 copy.41
  34.2 0.7 pad_maximum_fusion.2.refs_15_.refs_17_
  35.2 0.6 and_select_fusion.5.first_ref
  35.9 1.9 %collective-permute-start.11 = (bf16[256,1024]{1,0:T(8,128)(2,1)}, bf16[256,1024]{1,0:T(8,128)(2,1)}, u32[]{:S(2)}, u32[]{:S(2)}) collective-permute-start(bf16[256,1024]{1,0:T(8,128)(2,1)} %get-tuple-element.60), channel_id=1, source_target_pairs={{0,2},{1,3},{2,0},{3,1},{4,6},{5,7},{6,4},{7,5},{8,10},{9,11},{10,... | collective-permute-start | bytes 1572872 | tf_op jit(solution)/shard_map/ppermute | solution.py:40
  37.7 1.5 %collective-permute-start.12 = (bf16[256,1024]{1,0:T(8,128)(2,1)}, bf16[256,1024]{1,0:T(8,128)(2,1)}, u32[]{:S(2)}, u32[]{:S(2)}) collective-permute-start(bf16[256,1024]{1,0:T(8,128)(2,1)} %get-tuple-element.61), channel_id=1, source_target_pairs={{0,3},{1,0},{2,1},{3,2},{4,7},{5,4},{6,5},{7,6},{8,11},{9,8},{10,9... | collective-permute-start | bytes 1572872 | tf_op jit(solution)/shard_map/ppermute | solution.py:40
  39.3 0.8 slice.23
  40.1 1.9 %collective-permute-start.6 = (bf16[2,64,256]{2,1,0:T(8,128)(2,1)S(1)}, bf16[2,64,256]{2,1,0:T(8,128)(2,1)S(1)}, u32[]{:S(2)}, u32[]{:S(2)}) collective-permute-start(bf16[2,64,256]{2,1,0:T(8,128)(2,1)S(1)} %slice.23), channel_id=1, source_target_pairs={{0,4},{4,8},{8,12},{12,16},{16,20},{20,24},{24,28},{28,32},{32,36}... | collective-permute-start | bytes 196616 | tf_op jit(solution)/shard_map/ppermute | solution.py:56
  42.1 0.7 reshape.112.refs_14_.refs_16_
  42.8 8.9 %all-to-all-done.rows_ref.table_ref = bf16[32,80,256]{2,1,0:T(8,128)(2,1)} async-done(((bf16[32,80,256]{2,1,0:T(8,128)(2,1)}), bf16[32,80,256]{2,1,0:T(8,128)(2,1)}, u32[]{:S(2)}, u32[]{:S(2)}) %all-to-all-start) | async-done | bytes 1310752 | tf_op jit(solution)/shard_map/all_to_all | solution.py:614
  51.8 2.8 %shard_map.56 = bf16[2,32,256]{2,1,0:T(8,128)(2,1)} custom-call(s32[2,32]{1,0:T(2,128)} %and_select_fusion.5.first_ref, bf16[32,80,256]{2,1,0:T(8,128)(2,1)} %all-to-all-done.rows_ref.table_ref), custom_call_target="tpu_custom_call" | custom-call | tf_op jit(solution)/shard_map/pallas_call | solution.py:127
  54.6 1.2 collective-permute-start.5
  55.8 1.0 collective-permute-start.4
  56.8 1.9 %collective-permute-done.5 = bf16[2,32,256]{2,1,0:T(8,128)(2,1)S(1)} collective-permute-done((bf16[2,32,256]{2,1,0:T(8,128)(2,1)}, bf16[2,32,256]{2,1,0:T(8,128)(2,1)S(1)}, u32[]{:S(2)}, u32[]{:S(2)}) %collective-permute-start.5) | collective-permute-done | bytes 32800 | tf_op jit(solution)/shard_map/ppermute | solution.py:52
  58.8 0.6 and_select_fusion.3.shift_ref
  59.5 3.8 %shard_map.57 = bf16[32,2,64,256]{3,2,1,0:T(8,128)(2,1)} custom-call(s32[2]{0:T(128)} %and_select_fusion.3.shift_ref, bf16[32,80,256]{2,1,0:T(8,128)(2,1)} %all-to-all-done.rows_ref.table_ref), custom_call_target="tpu_custom_call" | custom-call | tf_op jit(solution)/shard_map/pallas_call | solution.py:150
  63.3 0.8 collective-permute-done.3
  64.1 0.7 collective-permute-start.9
  64.8 2.9 %collective-permute-start.8 = (bf16[4,2,32,256]{3,2,1,0:T(8,128)(2,1)S(1)}, bf16[4,2,32,256]{3,2,1,0:T(8,128)(2,1)S(1)}, u32[]{:S(2)}, u32[]{:S(2)}) collective-permute-start(bf16[4,2,32,256]{3,2,1,0:T(8,128)(2,1)S(1)} %pad_maximum_fusion.1.refs_4_), channel_id=1, source_target_pairs={{0,64},{4,68},{8,72},{12,76},{16,80},{20,84},{24,88},{28,92},{32,9... | collective-permute-start | bytes 393224 | tf_op jit(solution)/shard_map/ppermute | solution.py:52
  67.7 0.4 collective-permute-start.7
  68.1 2.9 %collective-permute-done.9.refs_7_ = bf16[4,2,32,256]{3,2,1,0:T(8,128)(2,1)S(1)} collective-permute-done((bf16[4,2,32,256]{3,2,1,0:T(8,128)(2,1)S(1)}, bf16[4,2,32,256]{3,2,1,0:T(8,128)(2,1)S(1)}, u32[]{:S(2)}, u32[]{:S(2)}) %collective-permute-start.9) | collective-permute-done | bytes 131104 | tf_op jit(solution)/shard_map/ppermute | solution.py:52
  71.0 1.4 collective-permute-done.8.refs_6_
  72.7 8.9 %all-to-all-start.1 = ((bf16[32,2,64,256]{3,2,1,0:T(8,128)(2,1)}), bf16[32,2,64,256]{3,2,1,0:T(8,128)(2,1)}, u32[]{:S(2)}, u32[]{:S(2)}) async-start(bf16[32,2,64,256]{3,2,1,0:T(8,128)(2,1)} %shard_map.57), calls=%async_computation.1 | async-start | bytes 4194304 | tf_op jit(solution)/shard_map/all_to_all | solution.py:638
  81.9 1.8 %collective-permute-start.14 = (bf16[256,1024]{1,0:T(8,128)(2,1)}, bf16[256,1024]{1,0:T(8,128)(2,1)}, u32[]{:S(2)}, u32[]{:S(2)}) collective-permute-start(bf16[256,1024]{1,0:T(8,128)(2,1)} %get-tuple-element.64), channel_id=1, source_target_pairs={{0,2},{1,3},{2,0},{3,1},{4,6},{5,7},{6,4},{7,5},{8,10},{9,11},{10,... | collective-permute-start | bytes 1572872 | tf_op jit(solution)/shard_map/ppermute | solution.py:40
  83.7 1.5 collective-permute-start.15
  85.2 0.6 and_select_fusion.2.order_ref
  85.8 19.2 %shard_map.58 = (bf16[4,256,1024]{2,1,0:T(8,128)(2,1)}, bf16[4,256,128]{2,1,0:T(8,128)(2,1)}, bf16[4,256,1024]{2,1,0:T(8,128)(2,1)}) custom-call(s32[4]{0:T(128)} %and_select_fusion.7.rows_ref, bf16[256,1024]{1,0:T(8,128)(2,1)} %get-tuple-element.72.refs_0_, bf16[256,1024]{1,0:T(8,128)(2,1)} %collective-permute-done.10.refs_1_, ...), custom_call_target="tpu_custom_call" | custom-call | flops 1000000000 | bytes 1048576 | tf_op jit(solution)/shard_map/pallas_call | solution.py:277
  105.0 3.0 %all-to-all-done.1 = bf16[32,2,64,256]{3,2,1,0:T(8,128)(2,1)} async-done(((bf16[32,2,64,256]{3,2,1,0:T(8,128)(2,1)}), bf16[32,2,64,256]{3,2,1,0:T(8,128)(2,1)}, u32[]{:S(2)}, u32[]{:S(2)}) %all-to-all-start.1) | async-done | bytes 2097184 | tf_op jit(solution)/shard_map/all_to_all | solution.py:638
  107.9 2.1 %shard_map.59 = bf16[2,2,64,256]{3,2,1,0:T(8,128)(2,1)} custom-call(s32[4]{0:T(128)} %and_select_fusion.2.order_ref, bf16[2,16,2,64,256]{4,3,2,1,0:T(8,128)(2,1)} %bitcast.14.refs_0_.refs_1_.refs_2_.refs_3_.refs_14_, bf16[2,16,2,64,256]{4,3,2,1,0:T(8,128)(2,1)} %bitcast.14.refs_0_.refs_1_.refs_2_.refs_3_.refs_14_, ...), custom_call_target="tpu_custom_call" | custom-call | tf_op jit(solution)/shard_map/pallas_call | solution.py:99
  110.1 1.9 %collective-permute-start.17 = (bf16[2,2,64,256]{3,2,1,0:T(8,128)(2,1)}, bf16[2,2,64,256]{3,2,1,0:T(8,128)(2,1)S(1)}, u32[]{:S(2)}, u32[]{:S(2)}) collective-permute-start(bf16[2,2,64,256]{3,2,1,0:T(8,128)(2,1)} %shard_map.59), channel_id=1, source_target_pairs={{0,4},{4,8},{8,12},{12,16},{16,20},{20,24},{24,28},{28,32},{32,36}... | collective-permute-start | bytes 393224 | tf_op jit(solution)/shard_map/ppermute | solution.py:56
  112.0 0.6 reshape.113.order_ref
  112.6 6.0 %collective-permute-done.17.refs_15_ = bf16[2,2,64,256]{3,2,1,0:T(8,128)(2,1)S(1)} collective-permute-done((bf16[2,2,64,256]{3,2,1,0:T(8,128)(2,1)}, bf16[2,2,64,256]{3,2,1,0:T(8,128)(2,1)S(1)}, u32[]{:S(2)}, u32[]{:S(2)}) %collective-permute-start.17) | collective-permute-done | bytes 131104 | tf_op jit(solution)/shard_map/ppermute | solution.py:56
  118.7 0.6 copy-done.10
  119.3 27.8 %shard_map.60 = bf16[1024,2048]{1,0:T(8,128)(2,1)} custom-call(s32[4]{0:T(128)} %and_select_fusion.7.rows_ref, s32[4]{0:T(128)} %reshape.113.order_ref, bf16[256,1024]{1,0:T(8,128)(2,1)} %get-tuple-element.62.refs_0_, bf16[256,1024]{1,0:T(8,128)(2,1)} %collective-permute-done.13.refs_1_, bf16[256,1024]{1,0:T(8,128)(2,1)} %collective-permute-done.14.refs_2_, ...), custom_call_target="tpu_custom_call" | custom-call | tf_op jit(solution)/shard_map/pallas_call | solution.py:509
  (75 shorter events, 2.7 us)
Async XLA Ops:
  0.0 1.6 %copy-start.5 = (bf16[256,1024]{1,0:T(8,128)(2,1)S(1)}, bf16[256,1024]{1,0:T(8,128)(2,1)}, u32[]{:S(2)}) copy-start(bf16[256,1024]{1,0:T(8,128)(2,1)} %param.7) | copy-start | bytes 1572868
  1.6 7.3 %copy-start.13 = (s32[2,3]{1,0:T(2,128)S(1)}, s32[2,3]{1,0:T(2,128)}, u32[]{:S(2)}) copy-start(s32[2,3]{1,0:T(2,128)} %param.9) | copy-start | bytes 76
  1.6 7.5 %copy-start.12 = (s32[2,1024]{1,0:T(2,128)S(1)}, s32[2,1024]{1,0:T(2,128)}, u32[]{:S(2)}) copy-start(s32[2,1024]{1,0:T(2,128)} %param.8) | copy-start | bytes 24580
  3.0 15.2 %collective-permute-start.2 = (bf16[2,256,256]{2,1,0:T(8,128)(2,1)S(1)}, bf16[2,256,256]{2,1,0:T(8,128)(2,1)S(1)}, u32[]{:S(2)}, u32[]{:S(2)}) collective-permute-start(bf16[2,256,256]{2,1,0:T(8,128)(2,1)S(1)} %get-tuple-element.95), channel_id=1, source_target_pairs={{0,3},{1,0},{2,1},{3,2},{4,7},{5,4},{6,5},{7,6},{8,11},{9,8},{10,9... | collective-permute-start | bytes 786440 | tf_op jit(solution)/shard_map/ppermute | solution.py:40
  7.0 14.6 %collective-permute-start = (bf16[2,256,256]{2,1,0:T(8,128)(2,1)S(1)}, bf16[2,256,256]{2,1,0:T(8,128)(2,1)S(1)}, u32[]{:S(2)}, u32[]{:S(2)}) collective-permute-start(bf16[2,256,256]{2,1,0:T(8,128)(2,1)S(1)} %get-tuple-element.97), channel_id=1, source_target_pairs={{0,1},{1,2},{2,3},{3,0},{4,5},{5,6},{6,7},{7,4},{8,9},{9,10},{10,1... | collective-permute-start | bytes 786440 | tf_op jit(solution)/shard_map/ppermute | solution.py:40
  7.0 14.6 %collective-permute-start.1 = (bf16[2,256,256]{2,1,0:T(8,128)(2,1)S(1)}, bf16[2,256,256]{2,1,0:T(8,128)(2,1)S(1)}, u32[]{:S(2)}, u32[]{:S(2)}) collective-permute-start(bf16[2,256,256]{2,1,0:T(8,128)(2,1)S(1)} %get-tuple-element.98), channel_id=1, source_target_pairs={{0,2},{1,3},{2,0},{3,1},{4,6},{5,7},{6,4},{7,5},{8,10},{9,11},{10,... | collective-permute-start | bytes 786440 | tf_op jit(solution)/shard_map/ppermute | solution.py:40
  18.2 4.8 %copy-start.7 = (bf16[2,256,256]{2,1,0:T(8,128)(2,1)}, bf16[2,256,256]{2,1,0:T(8,128)(2,1)S(1)}, u32[]{:S(2)}) copy-start(bf16[2,256,256]{2,1,0:T(8,128)(2,1)S(1)} %collective-permute-done.2.p3) | copy-start | bytes 786436
  21.6 0.7 copy-start.8
  22.3 0.7 copy-start.9
  25.8 7.9 %copy-start.1 = (s32[2,32,4,4,2]{4,3,2,1,0:T(4,128)S(1)}, s32[2,32,4,4,2]{4,3,2,1,0:T(4,128)}, u32[]{:S(2)}) copy-start(s32[2,32,4,4,2]{4,3,2,1,0:T(4,128)} %reshape.111) | copy-start | bytes 24580
  25.8 25.9 %all-to-all-start = ((bf16[32,80,256]{2,1,0:T(8,128)(2,1)}), bf16[32,80,256]{2,1,0:T(8,128)(2,1)}, u32[]{:S(2)}, u32[]{:S(2)}) async-start(bf16[32,80,256]{2,1,0:T(8,128)(2,1)} %get-tuple-element.48), calls=%async_computation | async-start | bytes 2621440 | tf_op jit(solution)/shard_map/all_to_all | solution.py:614
  35.8 31.9 %collective-permute-start.10 = (bf16[256,1024]{1,0:T(8,128)(2,1)}, bf16[256,1024]{1,0:T(8,128)(2,1)}, u32[]{:S(2)}, u32[]{:S(2)}) collective-permute-start(bf16[256,1024]{1,0:T(8,128)(2,1)} %get-tuple-element.59), channel_id=1, source_target_pairs={{0,1},{1,2},{2,3},{3,0},{4,5},{5,6},{6,7},{7,4},{8,9},{9,10},{10,1... | collective-permute-start | bytes 1572872 | tf_op jit(solution)/shard_map/ppermute | solution.py:40
  35.9 32.3 %collective-permute-start.11 = (bf16[256,1024]{1,0:T(8,128)(2,1)}, bf16[256,1024]{1,0:T(8,128)(2,1)}, u32[]{:S(2)}, u32[]{:S(2)}) collective-permute-start(bf16[256,1024]{1,0:T(8,128)(2,1)} %get-tuple-element.60), channel_id=1, source_target_pairs={{0,2},{1,3},{2,0},{3,1},{4,6},{5,7},{6,4},{7,5},{8,10},{9,11},{10,... | collective-permute-start | bytes 1572872 | tf_op jit(solution)/shard_map/ppermute | solution.py:40
  37.7 30.4 %collective-permute-start.12 = (bf16[256,1024]{1,0:T(8,128)(2,1)}, bf16[256,1024]{1,0:T(8,128)(2,1)}, u32[]{:S(2)}, u32[]{:S(2)}) collective-permute-start(bf16[256,1024]{1,0:T(8,128)(2,1)} %get-tuple-element.61), channel_id=1, source_target_pairs={{0,3},{1,0},{2,1},{3,2},{4,7},{5,4},{6,5},{7,6},{8,11},{9,8},{10,9... | collective-permute-start | bytes 1572872 | tf_op jit(solution)/shard_map/ppermute | solution.py:40
  40.1 15.7 %collective-permute-start.6 = (bf16[2,64,256]{2,1,0:T(8,128)(2,1)S(1)}, bf16[2,64,256]{2,1,0:T(8,128)(2,1)S(1)}, u32[]{:S(2)}, u32[]{:S(2)}) collective-permute-start(bf16[2,64,256]{2,1,0:T(8,128)(2,1)S(1)} %slice.23), channel_id=1, source_target_pairs={{0,4},{4,8},{8,12},{12,16},{16,20},{20,24},{24,28},{28,32},{32,36}... | collective-permute-start | bytes 196616 | tf_op jit(solution)/shard_map/ppermute | solution.py:56
  54.6 9.5 %copy-start.11 = (bf16[2,32,256]{2,1,0:T(8,128)(2,1)S(1)}, bf16[2,32,256]{2,1,0:T(8,128)(2,1)}, u32[]{:S(2)}) copy-start(bf16[2,32,256]{2,1,0:T(8,128)(2,1)} %shard_map.56) | copy-start | bytes 98308
  54.6 4.1 %collective-permute-start.5 = (bf16[2,32,256]{2,1,0:T(8,128)(2,1)}, bf16[2,32,256]{2,1,0:T(8,128)(2,1)S(1)}, u32[]{:S(2)}, u32[]{:S(2)}) collective-permute-start(bf16[2,32,256]{2,1,0:T(8,128)(2,1)} %shard_map.56), channel_id=1, source_target_pairs={{0,24},{4,28},{8,0},{12,4},{16,8},{20,12},{24,16},{28,20},{32,56},... | collective-permute-start | bytes 98312 | tf_op jit(solution)/shard_map/ppermute | solution.py:52
  55.8 16.9 %copy-start.6 = (bf16[2,64,256]{2,1,0:T(8,128)(2,1)}, bf16[2,64,256]{2,1,0:T(8,128)(2,1)S(1)}, u32[]{:S(2)}) copy-start(bf16[2,64,256]{2,1,0:T(8,128)(2,1)S(1)} %collective-permute-done.6.refs_12_) | copy-start | bytes 196612
  55.8 7.5 %collective-permute-start.4 = (bf16[2,32,256]{2,1,0:T(8,128)(2,1)}, bf16[2,32,256]{2,1,0:T(8,128)(2,1)S(1)}, u32[]{:S(2)}, u32[]{:S(2)}) collective-permute-start(bf16[2,32,256]{2,1,0:T(8,128)(2,1)} %shard_map.56), channel_id=1, source_target_pairs={{0,16},{4,20},{8,24},{12,28},{16,0},{20,4},{24,8},{28,12},{32,48},... | collective-permute-start | bytes 98312 | tf_op jit(solution)/shard_map/ppermute | solution.py:52
  58.7 5.3 %collective-permute-start.3 = (bf16[2,32,256]{2,1,0:T(8,128)(2,1)}, bf16[2,32,256]{2,1,0:T(8,128)(2,1)S(1)}, u32[]{:S(2)}, u32[]{:S(2)}) collective-permute-start(bf16[2,32,256]{2,1,0:T(8,128)(2,1)} %shard_map.56), channel_id=1, source_target_pairs={{0,8},{4,12},{8,16},{12,20},{16,24},{20,28},{24,0},{28,4},{32,40},... | collective-permute-start | bytes 98312 | tf_op jit(solution)/shard_map/ppermute | solution.py:52
  64.1 17.5 %copy-start = (bf16[4,2,32,256]{3,2,1,0:T(8,128)(2,1)}, bf16[4,2,32,256]{3,2,1,0:T(8,128)(2,1)S(1)}, u32[]{:S(2)}) copy-start(bf16[4,2,32,256]{3,2,1,0:T(8,128)(2,1)S(1)} %pad_maximum_fusion.1.refs_4_) | copy-start | bytes 393220
  64.1 6.9 %collective-permute-start.9 = (bf16[4,2,32,256]{3,2,1,0:T(8,128)(2,1)S(1)}, bf16[4,2,32,256]{3,2,1,0:T(8,128)(2,1)S(1)}, u32[]{:S(2)}, u32[]{:S(2)}) collective-permute-start(bf16[4,2,32,256]{3,2,1,0:T(8,128)(2,1)S(1)} %pad_maximum_fusion.1.refs_4_), channel_id=1, source_target_pairs={{0,96},{4,100},{8,104},{12,108},{16,112},{20,116},{24,120},{28,124... | collective-permute-start | bytes 393224 | tf_op jit(solution)/shard_map/ppermute | solution.py:52
  64.8 7.6 %collective-permute-start.8 = (bf16[4,2,32,256]{3,2,1,0:T(8,128)(2,1)S(1)}, bf16[4,2,32,256]{3,2,1,0:T(8,128)(2,1)S(1)}, u32[]{:S(2)}, u32[]{:S(2)}) collective-permute-start(bf16[4,2,32,256]{3,2,1,0:T(8,128)(2,1)S(1)} %pad_maximum_fusion.1.refs_4_), channel_id=1, source_target_pairs={{0,64},{4,68},{8,72},{12,76},{16,80},{20,84},{24,88},{28,92},{32,9... | collective-permute-start | bytes 393224 | tf_op jit(solution)/shard_map/ppermute | solution.py:52
  67.7 5.0 %collective-permute-start.7 = (bf16[4,2,32,256]{3,2,1,0:T(8,128)(2,1)S(1)}, bf16[4,2,32,256]{3,2,1,0:T(8,128)(2,1)S(1)}, u32[]{:S(2)}, u32[]{:S(2)}) collective-permute-start(bf16[4,2,32,256]{3,2,1,0:T(8,128)(2,1)S(1)} %pad_maximum_fusion.1.refs_4_), channel_id=1, source_target_pairs={{0,32},{4,36},{8,40},{12,44},{16,48},{20,52},{24,56},{28,60},{32,6... | collective-permute-start | bytes 393224 | tf_op jit(solution)/shard_map/ppermute | solution.py:52
  71.0 10.6 %copy-start.2 = (bf16[4,2,32,256]{3,2,1,0:T(8,128)(2,1)}, bf16[4,2,32,256]{3,2,1,0:T(8,128)(2,1)S(1)}, u32[]{:S(2)}) copy-start(bf16[4,2,32,256]{3,2,1,0:T(8,128)(2,1)S(1)} %collective-permute-done.9.refs_7_) | copy-start | bytes 393220
  72.4 9.2 %copy-start.3 = (bf16[4,2,32,256]{3,2,1,0:T(8,128)(2,1)}, bf16[4,2,32,256]{3,2,1,0:T(8,128)(2,1)S(1)}, u32[]{:S(2)}) copy-start(bf16[4,2,32,256]{3,2,1,0:T(8,128)(2,1)S(1)} %collective-permute-done.8.refs_6_) | copy-start | bytes 393220
  72.7 8.9 %copy-start.4 = (bf16[4,2,32,256]{3,2,1,0:T(8,128)(2,1)}, bf16[4,2,32,256]{3,2,1,0:T(8,128)(2,1)S(1)}, u32[]{:S(2)}) copy-start(bf16[4,2,32,256]{3,2,1,0:T(8,128)(2,1)S(1)} %collective-permute-done.7.refs_5_) | copy-start | bytes 393220
  72.7 35.2 %all-to-all-start.1 = ((bf16[32,2,64,256]{3,2,1,0:T(8,128)(2,1)}), bf16[32,2,64,256]{3,2,1,0:T(8,128)(2,1)}, u32[]{:S(2)}, u32[]{:S(2)}) async-start(bf16[32,2,64,256]{3,2,1,0:T(8,128)(2,1)} %shard_map.57), calls=%async_computation.1 | async-start | bytes 4194304 | tf_op jit(solution)/shard_map/all_to_all | solution.py:638
  81.7 4.1 %collective-permute-start.16 = (bf16[16,2,32,256]{3,2,1,0:T(8,128)(2,1)S(1)}, bf16[16,2,32,256]{3,2,1,0:T(8,128)(2,1)}, u32[]{:S(2)}, u32[]{:S(2)}) collective-permute-start(bf16[16,2,32,256]{3,2,1,0:T(8,128)(2,1)S(1)} %pad_maximum_fusion), channel_id=1, source_target_pairs={{0,4},{4,0},{8,12},{12,8},{16,20},{20,16},{24,28},{28,24},{32,36},... | collective-permute-start | bytes 1572872 | tf_op jit(solution)/shard_map/ppermute | solution.py:52
  81.9 30.7 %collective-permute-start.13 = (bf16[256,1024]{1,0:T(8,128)(2,1)}, bf16[256,1024]{1,0:T(8,128)(2,1)}, u32[]{:S(2)}, u32[]{:S(2)}) collective-permute-start(bf16[256,1024]{1,0:T(8,128)(2,1)} %get-tuple-element.63), channel_id=1, source_target_pairs={{0,1},{1,2},{2,3},{3,0},{4,5},{5,6},{6,7},{7,4},{8,9},{9,10},{10,1... | collective-permute-start | bytes 1572872 | tf_op jit(solution)/shard_map/ppermute | solution.py:40
  81.9 30.7 %collective-permute-start.14 = (bf16[256,1024]{1,0:T(8,128)(2,1)}, bf16[256,1024]{1,0:T(8,128)(2,1)}, u32[]{:S(2)}, u32[]{:S(2)}) collective-permute-start(bf16[256,1024]{1,0:T(8,128)(2,1)} %get-tuple-element.64), channel_id=1, source_target_pairs={{0,2},{1,3},{2,0},{3,1},{4,6},{5,7},{6,4},{7,5},{8,10},{9,11},{10,... | collective-permute-start | bytes 1572872 | tf_op jit(solution)/shard_map/ppermute | solution.py:40
  83.7 28.9 %collective-permute-start.15 = (bf16[256,1024]{1,0:T(8,128)(2,1)}, bf16[256,1024]{1,0:T(8,128)(2,1)}, u32[]{:S(2)}, u32[]{:S(2)}) collective-permute-start(bf16[256,1024]{1,0:T(8,128)(2,1)} %get-tuple-element.65), channel_id=1, source_target_pairs={{0,3},{1,0},{2,1},{3,2},{4,7},{5,4},{6,5},{7,6},{8,11},{9,8},{10,9... | collective-permute-start | bytes 1572872 | tf_op jit(solution)/shard_map/ppermute | solution.py:40
  110.1 8.6 %collective-permute-start.17 = (bf16[2,2,64,256]{3,2,1,0:T(8,128)(2,1)}, bf16[2,2,64,256]{3,2,1,0:T(8,128)(2,1)S(1)}, u32[]{:S(2)}, u32[]{:S(2)}) collective-permute-start(bf16[2,2,64,256]{3,2,1,0:T(8,128)(2,1)} %shard_map.59), channel_id=1, source_target_pairs={{0,4},{4,8},{8,12},{12,16},{16,20},{20,24},{24,28},{28,32},{32,36}... | collective-permute-start | bytes 393224 | tf_op jit(solution)/shard_map/ppermute | solution.py:56
  118.7 0.6 copy-start.10
